TPU v7x, 32 devices: a whole 2x2x4 slice. The times are simulated.
32 devices in a mesh: shard: 8 (over y, x, core), rep: 4 (over z).
Axes of the slice: x: 2, y: 2, z: 4, core: 2. Of those that a mesh axis runs over, the one named last changes fastest.
Arguments:
- inputs: bfloat16 [32768, 768], P(('shard', 'rep')), may hold values from -6 to 6
- w_query: bfloat16 [768, 768], P('shard'), may hold values from -0.21875 to 0.21875
- w_key: bfloat16 [768, 768], P('shard'), may hold values from -0.21875 to 0.21875
- w_value: bfloat16 [768, 768], P('shard'), may hold values from -0.21875 to 0.21875
- w_output: bfloat16 [768, 768], P('shard'), may hold values from -0.875 to 0.875
- w_router: bfloat16 [768, 8], P('shard'), may hold values from -0.15625 to 0.15625
- gain_attn: bfloat16 [768], P('shard'), may hold values from 0.5 to 1.5
- gain_expert: bfloat16 [768], P('shard'), may hold values from 0.5 to 1.5
- rel_bias: bfloat16 [32, 12], P('shard'), may hold values from -4 to 4
- w_in: bfloat16 [8, 768, 3072], P('shard'), may hold values from -0.21875 to 0.21875
- w_out: bfloat16 [8, 3072, 768], P('shard'), may hold values from -0.21875 to 0.21875
- segment_ids: int32 [32, 1024], P(('shard', 'rep')), may hold values from 0 to 3, never falling along the last dimension, each value on 1 to 512 neighbouring positions
- expert_ids: int32 [32768, 2], P(('shard', 'rep')), may hold values from 0 to 7, all different within a row; in each aligned block of 1024 rows (0 to 1023, 1024 to 2047, ...) at most 384 rows name the same one
- out_grad: bfloat16 [32768, 768], P(('shard', 'rep')), may hold values from -6 to 6
Outputs:
- output: bfloat16 [32768, 768], P(('shard', 'rep'))
- input_grad: bfloat16 [32768, 768], P(('shard', 'rep'))
- grad_w_query: float32 [768, 768], P('shard')
- grad_w_key: float32 [768, 768], P('shard')
- grad_w_value: float32 [768, 768], P('shard')
- grad_w_output: float32 [768, 768], P('shard')
- grad_w_router: float32 [768, 8], P('shard')
- grad_gain_attn: float32 [768], P('shard')
- grad_gain_expert: float32 [768], P('shard')
- grad_rel_bias: float32 [32, 12], P('shard')
- grad_w_in: float32 [8, 768, 3072], P('shard', None, 'rep')
- grad_w_out: float32 [8, 3072, 768], P('shard', 'rep')
Inputs may be any that keep to these rules, and one draw needn't show every extreme that they name: `segment_ids`: document numbers never fall along a sequence. `expert_ids`: a token's two experts differ; among the tokens of one device no expert is named more than 384 times, a bound that some block reaches.
All inputs are finite; a program needn't handle non-finite values.
Results may differ from a plain program's by a relative error of at most 0.02.
Values may be sent and summed in bfloat16 or wider, within the bound.
No kernel may reach another device: no remote copies, remote signals or barrier semaphores. Data moves between devices by JAX's collectives and lax.ppermute only.
A program may use at most 320 MiB of HBM per device.

v0:
```python
import math

import jax
import jax.numpy as jnp
from jax import lax
from jax.sharding import PartitionSpec as P

HEADS = 12
BUCKETS = 32
MAX_DISTANCE = 128


eps_norm = 1e-06
neg_fill = -1000000000.0


def rms_scale(values, gain_vec):
    mean_square = jnp.mean(values * values, axis=-1, keepdims=True)
    return values * lax.rsqrt(mean_square + eps_norm) * gain_vec


def bucket_table(distance):
    half_count = BUCKETS // 2
    clipped = jnp.maximum(distance, 0)
    counted = jnp.zeros(distance.shape, jnp.int32)
    for section_number in range(1, half_count):
        threshold = math.ceil(
            half_count * (MAX_DISTANCE / half_count) ** (section_number / half_count)
        )
        counted = counted + (clipped >= threshold).astype(jnp.int32)
    return jnp.where(clipped < half_count, clipped, half_count + counted)


def pair_softmax(chosen):
    return jax.nn.softmax(chosen, axis=-1)


def gelu_tanh(values):
    return jax.nn.gelu(values, approximate=True)


def block_scores(query_block, key_seq, segment_seq, first_row, relative_bias_matrix):
    block_rows = query_block.shape[0]
    length = key_seq.shape[0]
    scale_factor = query_block.shape[2] ** (-0.5)
    raw_scores = (
        jnp.einsum("qhe,khe->hqk", query_block, key_seq, preferred_element_type=jnp.float32)
        * scale_factor
    )
    query_place = first_row + jnp.arange(block_rows, dtype=jnp.int32)
    key_place = jnp.arange(length, dtype=jnp.int32)
    distance = query_place[:, None] - key_place[None, :]
    one_hot_matrix = (
        bucket_table(distance)[None] == jnp.arange(BUCKETS, dtype=jnp.int32)[:, None, None]
    ).astype(jnp.bfloat16)
    bias_entries = jnp.einsum(
        "vye,vo->oye", one_hot_matrix, relative_bias_matrix, preferred_element_type=jnp.float32
    )
    segment_block = segment_seq[first_row : first_row + block_rows]
    allowed = (distance >= 0) & (segment_block[:, None] == segment_seq[None, :])
    scores = jnp.where(allowed[None], raw_scores + bias_entries, neg_fill)
    return (scores, one_hot_matrix)


def sequence_forward(query_seq, key_seq, value_seq, segment_seq, relative_bias_matrix):
    length = query_seq.shape[0]
    block_rows = min(512, length)
    mixed_parts = []
    log_parts = []
    for first_row in range(0, length, block_rows):
        scores, one_hot_matrix = block_scores(
            query_seq[first_row : first_row + block_rows],
            key_seq,
            segment_seq,
            first_row,
            relative_bias_matrix,
        )
        row_peak = jnp.max(scores, axis=-1, keepdims=True)
        row_total = jnp.sum(jnp.exp(scores - row_peak), axis=-1, keepdims=True)
        log_total = row_peak + jnp.log(row_total)
        attn_probs = jnp.exp(scores - log_total).astype(jnp.bfloat16)
        mixed_parts.append(
            jnp.einsum("hqk,khe->qhe", attn_probs, value_seq, preferred_element_type=jnp.float32)
        )
        log_parts.append(log_total)
    return (jnp.concatenate(mixed_parts, axis=0), jnp.concatenate(log_parts, axis=1))


def sequence_backward(
    query_seq, key_seq, value_seq, segment_seq, relative_bias_matrix, log_sums, grad_mixed
):
    length = query_seq.shape[0]
    block_rows = min(512, length)
    scale_factor = query_seq.shape[2] ** (-0.5)
    grad_key = jnp.zeros(key_seq.shape, jnp.float32)
    grad_value = jnp.zeros(value_seq.shape, jnp.float32)
    grad_table = jnp.zeros(relative_bias_matrix.shape, jnp.float32)
    query_parts = []
    for first_row in range(0, length, block_rows):
        query_block = query_seq[first_row : first_row + block_rows]
        grad_block = grad_mixed[first_row : first_row + block_rows]
        scores, one_hot_matrix = block_scores(
            query_block, key_seq, segment_seq, first_row, relative_bias_matrix
        )
        attn_probs = jnp.exp(scores - log_sums[:, first_row : first_row + block_rows])
        grad_probs = jnp.einsum(
            "qhe,khe->hqk", grad_block, value_seq, preferred_element_type=jnp.float32
        )
        row_dot = jnp.sum(grad_probs * attn_probs, axis=-1, keepdims=True)
        score_gradient = (attn_probs * (grad_probs - row_dot)).astype(jnp.bfloat16)
        query_parts.append(
            (
                jnp.einsum(
                    "hqk,khe->qhe", score_gradient, key_seq, preferred_element_type=jnp.float32
                )
                * scale_factor
            ).astype(jnp.bfloat16)
        )
        grad_key = (
            grad_key
            + jnp.einsum(
                "hqk,qhe->khe", score_gradient, query_block, preferred_element_type=jnp.float32
            )
            * scale_factor
        )
        grad_value = grad_value + jnp.einsum(
            "hqk,qhe->khe",
            attn_probs.astype(jnp.bfloat16),
            grad_block,
            preferred_element_type=jnp.float32,
        )
        grad_table = grad_table + jnp.einsum(
            "ygc,mgc->ym", one_hot_matrix, score_gradient, preferred_element_type=jnp.float32
        )
    return (
        jnp.concatenate(query_parts, axis=0),
        grad_key.astype(jnp.bfloat16),
        grad_value.astype(jnp.bfloat16),
        grad_table,
    )


def body(
    inputs,
    w_query,
    w_key,
    w_value,
    w_output,
    w_router,
    gain_attn,
    gain_expert,
    rel_bias,
    w_in,
    w_out,
    segment_ids,
    expert_ids,
    out_grad,
):
    tokens_here, model_width = inputs.shape
    seq_here, seq_length = segment_ids.shape
    head_width = model_width // HEADS
    experts = lax.axis_size("shard")
    capacity = 3 * tokens_here // experts
    hidden_width = w_in.shape[2]
    shared = (w_query, w_key, w_value, w_output, w_router, gain_attn, gain_expert, rel_bias)
    gathered = (
        lax.all_gather(shared[0], "shard", axis=0, tiled=True),
        lax.all_gather(shared[1], "shard", axis=0, tiled=True),
        lax.all_gather(shared[2], "shard", axis=0, tiled=True),
        lax.all_gather(shared[3], "shard", axis=0, tiled=True),
        lax.all_gather(shared[4], "shard", axis=0, tiled=True),
        lax.all_gather(shared[5], "shard", axis=0, tiled=True),
        lax.all_gather(shared[6], "shard", axis=0, tiled=True),
        lax.all_gather(shared[7], "shard", axis=0, tiled=True),
    )
    query_full, key_full, value_full, output_full, router_full, gain_one, gain_two, table_full = (
        gathered
    )
    inputs_f = inputs.astype(jnp.float32)
    normed = rms_scale(inputs_f, gain_one.astype(jnp.float32)).astype(jnp.bfloat16)
    query_low = jnp.dot(normed, query_full, preferred_element_type=jnp.float32).astype(jnp.bfloat16)
    key_low = jnp.dot(normed, key_full, preferred_element_type=jnp.float32).astype(jnp.bfloat16)
    value_low = jnp.dot(normed, value_full, preferred_element_type=jnp.float32).astype(jnp.bfloat16)
    heads_shape = (seq_here, seq_length, HEADS, head_width)
    query_seqs = query_low.reshape(heads_shape)
    key_seqs = key_low.reshape(heads_shape)
    value_seqs = value_low.reshape(heads_shape)
    seq_number = 0
    mixed_one, sums_one = sequence_forward(
        query_seqs[seq_number],
        key_seqs[seq_number],
        value_seqs[seq_number],
        segment_ids[seq_number],
        table_full,
    )
    mixed_list = [mixed_one]
    log_list = [sums_one]
    attended = jnp.stack(mixed_list).reshape(tokens_here, model_width).astype(jnp.bfloat16)
    branch = jnp.dot(attended, output_full, preferred_element_type=jnp.float32)
    hidden = inputs_f + branch
    normed_two = rms_scale(hidden, gain_two.astype(jnp.float32)).astype(jnp.bfloat16)
    logits = jnp.dot(normed_two, router_full, preferred_element_type=jnp.float32)
    expert_onehot = (
        expert_ids[:, :, None] == jnp.arange(experts, dtype=jnp.int32)[None, None, :]
    ).astype(jnp.float32)
    chosen = jnp.sum(expert_onehot * logits[:, None, :], axis=2)
    gate_probs, gate_pull = jax.vjp(pair_softmax, chosen)
    flat_ids = expert_ids.reshape(-1)
    onehot_count = (flat_ids[:, None] == jnp.arange(experts, dtype=jnp.int32)[None, :]).astype(
        jnp.int32
    )
    before = jnp.cumsum(onehot_count, axis=0, dtype=jnp.int32) - onehot_count
    slot_ids = jnp.sum(before * onehot_count, axis=1, dtype=jnp.int32)
    flat_rows = flat_ids * capacity + slot_ids
    send_rows = (
        jnp.zeros((experts * capacity, model_width), jnp.bfloat16)
        .at[flat_rows]
        .set(jnp.repeat(normed_two, 2, axis=0))
        .reshape(experts, capacity, model_width)
    )
    weight_in = w_in[0]
    weight_out = w_out[0]
    received = lax.all_to_all(send_rows, "shard", split_axis=0, concat_axis=0, tiled=True)
    slot_count = received.shape[1]
    rows_in = received.reshape(-1, model_width)
    pre_act = jnp.dot(rows_in, weight_in, preferred_element_type=jnp.float32)
    active = gelu_tanh(pre_act).astype(jnp.bfloat16)
    result = (
        jnp.dot(active, weight_out, preferred_element_type=jnp.float32)
        .astype(jnp.bfloat16)
        .reshape(experts, slot_count, model_width)
    )
    back_rows = lax.all_to_all(result, "shard", split_axis=0, concat_axis=0, tiled=True)
    kept_pre = pre_act.reshape(experts, slot_count, hidden_width)
    routed = (
        back_rows.reshape(experts * capacity, model_width)[flat_rows]
        .reshape(tokens_here, 2, model_width)
        .astype(jnp.float32)
    )
    combined = jnp.sum(gate_probs[:, :, None] * routed, axis=1)
    output = (hidden + combined).astype(jnp.bfloat16)
    grad_out = out_grad.astype(jnp.float32)
    grad_gates = jnp.sum(grad_out[:, None, :] * routed, axis=2)
    grad_routed = (
        (gate_probs[:, :, None] * grad_out[:, None, :])
        .astype(jnp.bfloat16)
        .reshape(tokens_here * 2, model_width)
    )
    grad_send = (
        jnp.zeros((experts * capacity, model_width), jnp.bfloat16)
        .at[flat_rows]
        .set(grad_routed)
        .reshape(experts, capacity, model_width)
    )
    grad_received = lax.all_to_all(grad_send, "shard", split_axis=0, concat_axis=0, tiled=True)
    grad_rows = grad_received.reshape(-1, model_width)
    pre_flat = kept_pre.reshape(-1, hidden_width)
    active_f, gelu_pull = jax.vjp(gelu_tanh, pre_flat)
    active_low = active_f.astype(jnp.bfloat16)
    grad_out_part = jnp.einsum(
        "rf,rd->fd", active_low, grad_rows, preferred_element_type=jnp.float32
    )
    grad_active = jnp.einsum("rd,fd->rf", grad_rows, weight_out, preferred_element_type=jnp.float32)
    grad_pre = gelu_pull(grad_active)[0].astype(jnp.bfloat16)
    rows_kept = received.reshape(-1, model_width)
    grad_in_part = jnp.einsum("rd,rf->df", rows_kept, grad_pre, preferred_element_type=jnp.float32)
    grad_rows_in = (
        jnp.einsum("rf,df->rd", grad_pre, weight_in, preferred_element_type=jnp.float32)
        .astype(jnp.bfloat16)
        .reshape(experts, capacity, model_width)
    )
    in_summed, out_summed = (
        lax.psum_scatter(grad_in_part, "rep", scatter_dimension=1, tiled=True),
        lax.psum_scatter(grad_out_part, "rep", scatter_dimension=0, tiled=True),
    )
    grad_back = lax.all_to_all(grad_rows_in, "shard", split_axis=0, concat_axis=0, tiled=True)
    regathered = (
        lax.all_gather(shared[0], "shard", axis=0, tiled=True),
        lax.all_gather(shared[1], "shard", axis=0, tiled=True),
        lax.all_gather(shared[2], "shard", axis=0, tiled=True),
        lax.all_gather(shared[3], "shard", axis=0, tiled=True),
        lax.all_gather(shared[4], "shard", axis=0, tiled=True),
        lax.all_gather(shared[5], "shard", axis=0, tiled=True),
        lax.all_gather(shared[6], "shard", axis=0, tiled=True),
        lax.all_gather(shared[7], "shard", axis=0, tiled=True),
    )
    (
        query_back,
        key_back,
        value_back,
        output_back,
        router_back,
        gain_one_back,
        gain_two_back,
        table_back,
    ) = regathered
    grad_copies = (
        grad_back.reshape(experts * capacity, model_width)[flat_rows]
        .reshape(tokens_here, 2, model_width)
        .astype(jnp.float32)
    )
    grad_chosen = gate_pull(grad_gates)[0]
    grad_logits = jnp.sum(expert_onehot * grad_chosen[:, :, None], axis=1)
    grad_router = jnp.einsum(
        "td,te->de",
        normed_two,
        grad_logits,
        precision=lax.Precision.HIGHEST,
        preferred_element_type=jnp.float32,
    )
    grad_normed_two = jnp.sum(grad_copies, axis=1) + jnp.dot(
        grad_logits, router_back.astype(jnp.float32).T, precision=lax.Precision.HIGHEST
    )
    unused_two, norm_two_pull = jax.vjp(rms_scale, hidden, gain_two_back.astype(jnp.float32))
    grad_hidden_norm, grad_gain_two = norm_two_pull(grad_normed_two)
    grad_hidden = grad_out + grad_hidden_norm
    grad_branch = grad_hidden.astype(jnp.bfloat16)
    grad_wo = jnp.einsum("td,te->de", attended, grad_branch, preferred_element_type=jnp.float32)
    grad_attended = (
        jnp.einsum("te,de->td", grad_branch, output_back, preferred_element_type=jnp.float32)
        .astype(jnp.bfloat16)
        .reshape(heads_shape)
    )
    seq_number = 0
    grad_q_one, grad_k_one, grad_v_one, table_one = sequence_backward(
        query_seqs[seq_number],
        key_seqs[seq_number],
        value_seqs[seq_number],
        segment_ids[seq_number],
        table_back,
        log_list[seq_number],
        grad_attended[seq_number],
    )
    query_grads = [grad_q_one]
    key_grads = [grad_k_one]
    value_grads = [grad_v_one]
    grad_query_low = jnp.stack(query_grads).reshape(tokens_here, model_width)
    grad_key_low = jnp.stack(key_grads).reshape(tokens_here, model_width)
    grad_value_low = jnp.stack(value_grads).reshape(tokens_here, model_width)
    grad_wq = jnp.einsum("td,te->de", normed, grad_query_low, preferred_element_type=jnp.float32)
    grad_wk = jnp.einsum("td,te->de", normed, grad_key_low, preferred_element_type=jnp.float32)
    grad_wv = jnp.einsum("td,te->de", normed, grad_value_low, preferred_element_type=jnp.float32)
    grad_normed = jnp.einsum(
        "te,de->td", grad_query_low, query_back, preferred_element_type=jnp.float32
    )
    grad_normed = grad_normed + jnp.einsum(
        "te,de->td", grad_key_low, key_back, preferred_element_type=jnp.float32
    )
    grad_normed = grad_normed + jnp.einsum(
        "te,de->td", grad_value_low, value_back, preferred_element_type=jnp.float32
    )
    unused_one, norm_one_pull = jax.vjp(rms_scale, inputs_f, gain_one_back.astype(jnp.float32))
    grad_inputs_norm, grad_gain_one = norm_one_pull(grad_normed)
    input_grad = (grad_hidden + grad_inputs_norm).astype(jnp.bfloat16)
    partial_grads = (
        grad_wq,
        grad_wk,
        grad_wv,
        grad_wo,
        grad_router,
        grad_gain_one,
        grad_gain_two,
        table_one,
    )
    owned = (
        lax.psum_scatter(partial_grads[0], "shard", scatter_dimension=0, tiled=True),
        lax.psum_scatter(partial_grads[1], "shard", scatter_dimension=0, tiled=True),
        lax.psum_scatter(partial_grads[2], "shard", scatter_dimension=0, tiled=True),
        lax.psum_scatter(partial_grads[3], "shard", scatter_dimension=0, tiled=True),
        lax.psum_scatter(partial_grads[4], "shard", scatter_dimension=0, tiled=True),
        lax.psum_scatter(partial_grads[5], "shard", scatter_dimension=0, tiled=True),
        lax.psum_scatter(partial_grads[6], "shard", scatter_dimension=0, tiled=True),
        lax.psum_scatter(partial_grads[7], "shard", scatter_dimension=0, tiled=True),
    )
    summed = lax.psum(
        (owned[0], owned[1], owned[2], owned[3], owned[4], owned[5], owned[6], owned[7]), "rep"
    )
    return (
        output,
        input_grad,
        summed[0],
        summed[1],
        summed[2],
        summed[3],
        summed[4],
        summed[5],
        summed[6],
        summed[7],
        in_summed[None],
        out_summed[None],
    )


def solution(mesh):
    in_specs = (
        P(("shard", "rep"), None),
        P("shard", None),
        P("shard", None),
        P("shard", None),
        P("shard", None),
        P("shard", None),
        P("shard"),
        P("shard"),
        P("shard", None),
        P("shard", None, None),
        P("shard", None, None),
        P(("shard", "rep"), None),
        P(("shard", "rep"), None),
        P(("shard", "rep"), None),
    )
    out_specs = (
        P(("shard", "rep"), None),
        P(("shard", "rep"), None),
        P("shard", None),
        P("shard", None),
        P("shard", None),
        P("shard", None),
        P("shard", None),
        P("shard"),
        P("shard"),
        P("shard", None),
        P("shard", None, "rep"),
        P("shard", "rep", None),
    )
    return jax.shard_map(body, mesh=mesh, in_specs=in_specs, out_specs=out_specs, check_vma=False)
```

profile of v0, /device:TPU:0, one launch (start us, length us, event | category | flops | bytes accessed | tf_op | source)
XLA Modules:
  0.0 1356.5 jit_solution(9301852920095120976)
XLA Ops:
  17.9 15.2 %all-reduce.8 = (bf16[768]{0:T(1024)(128)(2,1)S(1)}, bf16[768]{0:T(1024)(128)(2,1)S(1)}) all-reduce(bf16[768]{0:T(1024)(128)(2,1)S(1)} %dynamic-update-slice, bf16[768]{0:T(1024)(128)(2,1)S(1)} %dynamic-update-slice.1), channel_id=1, replica_groups=mesh['shard'=8,'rep'=4] {'shard'}, use_global_device_ids=true, to_apply=%add | all-reduce | flops 1536 | bytes 6144
  49.0 16.5 %fusion.1 = f32[512,1024,12]{0,2,1:T(8,128)} fusion(bf16[32,12,1]{1,0,2:T(8,128)(2,1)S(1)} %bitcast.175, s32[512,1024]{0,1:T(8,128)} %copy.129), kind=kOutput, calls=%fused_computation.6 | convolution fusion | flops 419430400 | bytes 27263744 | tf_op jit(solution)/shard_map/vye,vo->oye/dot_general | solution.py:56
  65.5 30.5 %copy.131 = f32[512,1024,12]{1,0,2:T(8,128)} copy(f32[512,1024,12]{0,2,1:T(8,128)} %fusion.1) | data formatting | bytes 50331648 | tf_op jit(solution)/shard_map/vye,vo->oye/dot_general | solution.py:56
  98.9 16.5 %fusion.3 = f32[512,1024,12]{0,2,1:T(8,128)} fusion(bf16[32,12,1]{1,0,2:T(8,128)(2,1)S(1)} %bitcast.176, s32[512,1024]{0,1:T(8,128)} %copy.126), kind=kOutput, calls=%fused_computation.9 | convolution fusion | flops 419430400 | bytes 27263744 | tf_op jit(solution)/shard_map/vye,vo->oye/dot_general | solution.py:56
  115.4 30.3 %copy.128 = f32[512,1024,12]{1,0,2:T(8,128)} copy(f32[512,1024,12]{0,2,1:T(8,128)} %fusion.3) | data formatting | bytes 50331648 | tf_op jit(solution)/shard_map/vye,vo->oye/dot_general | solution.py:56
  158.5 16.7 %fusion.124 = (f32[12,512]{1,0:T(8,128)S(1)}, f32[12,512,1024]{2,1,0:T(8,128)}) fusion(f32[512,1024,12]{1,0,2:T(8,128)} %copy.131, bf16[512,12,64]{0,2,1:T(8,128)(2,1)} %bitcast.157, bf16[1024,12,64]{0,2,1:T(8,128)(2,1)S(1)} %bitcast.147, pred[512,1024]{1,0:T(8,128)(4,1)} %get-tuple-element.98), kind=kOutput, calls=%fused_computation.180 | convolution fusion | flops 830466048 | bytes 53239808 | tf_op jit(solution)/shard_map/qhe,khe->hqk/dot_general | solution.py:47
  201.1 16.5 %fusion.125 = (f32[12,512]{1,0:T(8,128)S(1)}, f32[12,512,1024]{2,1,0:T(8,128)}) fusion(f32[512,1024,12]{1,0,2:T(8,128)} %copy.128, bf16[512,12,64]{0,2,1:T(8,128)(2,1)} %bitcast.159, bf16[1024,12,64]{0,2,1:T(8,128)(2,1)S(1)} %bitcast.148, pred[512,1024]{1,0:T(8,128)(4,1)} %get-tuple-element.97), kind=kOutput, calls=%fused_computation.181 | convolution fusion | flops 830466048 | bytes 53239808 | tf_op jit(solution)/shard_map/qhe,khe->hqk/dot_general | solution.py:47
  292.3 40.9 %all-gather.1 = bf16[8,96,8]{1,2,0:T(8,128)(2,1)S(1)} all-gather(bf16[1,96,8]{1,2,0:T(8,128)(2,1)S(1)} %bitcast.185), channel_id=1, replica_groups=mesh['shard'=8,'rep'=4] {'shard'}, dimensions={0}, use_global_device_ids=true | all-gather | bytes 13824 | tf_op jit(solution)/shard_map/all_gather | solution.py:171
  336.7 14.3 %scatter_custom_fusion.1 = bf16[3072,768]{1,0:T(8,128)(2,1)} fusion(s32[2048]{0:T(1024)S(1)} %bitcast.179, f32[2048,768]{1,0:T(8,128)} %mul.317, f32[2048]{0:T(1024)S(1)} %div.64, bf16[]{:T(256)} %constant.28.clone.1), kind=kCustom, calls=%fused_computation.70 | custom fusion | flops 3145728 | bytes 11018242 | tf_op jit(solution)/shard_map/scatter | solution.py:252
  355.7 32.2 %multiply_convert_fusion = (bf16[3072,3072]{1,0:T(8,128)(2,1)}, f32[3072,3072]{1,0:T(8,128)}) fusion(bf16[3072,768]{1,0:T(8,128)(2,1)} %bitcast.22, bf16[1,768,3072]{2,1,0:T(8,128)(2,1)} %param.23), kind=kOutput, calls=%fused_computation.19 | convolution fusion | flops 14580449280 | bytes 66060288 | tf_op jit(solution)/shard_map/dot_general | solution.py:226
  387.8 22.6 %all-to-all-done.2 = bf16[8,384,768]{2,1,0:T(8,128)(2,1)} async-done(((bf16[8,384,768]{2,1,0:T(8,128)(2,1)}), bf16[8,384,768]{2,1,0:T(8,128)(2,1)}, u32[]{:S(2)}, u32[]{:S(2)}) %all-to-all-start.2) | async-done | bytes 4718624 | tf_op jit(solution)/shard_map/all_to_all | solution.py:255
  410.4 43.3 %fusion.10 = bf16[3072,3072]{1,0:T(8,128)(2,1)} fusion(f32[3072,3072]{1,0:T(8,128)} %get-tuple-element.110, bf16[3072,768]{1,0:T(8,128)(2,1)} %bitcast.28, bf16[1,3072,768]{2,1,0:T(8,128)(2,1)} %param.24), kind=kOutput, calls=%fused_computation.18 | convolution fusion | flops 14684258304 | bytes 66060288 | tf_op jit(solution)/shard_map/rd,fd->rf/dot_general | solution.py:263
  453.7 19.3 %convolution_convert_fusion = bf16[3072,768]{1,0:T(8,128)(2,1)} fusion(bf16[3072,3072]{1,0:T(8,128)(2,1)} %fusion.10, bf16[1,768,3072]{2,1,0:T(8,128)(2,1)S(1)} %bitcast.188), kind=kOutput, calls=%fused_computation.48 | convolution fusion | flops 14497873920 | bytes 28311552 | tf_op jit(solution)/shard_map/rf,df->rd/dot_general | solution.py:268
  477.7 20.4 %convolution_convert_fusion.1 = bf16[3072,768]{1,0:T(8,128)(2,1)} fusion(bf16[3072,3072]{1,0:T(8,128)(2,1)} %get-tuple-element.109, bf16[1,3072,768]{2,1,0:T(8,128)(2,1)} %param.24), kind=kOutput, calls=%fused_computation.49 | convolution fusion | flops 14497873920 | bytes 28311552 | tf_op jit(solution)/shard_map/dot_general | solution.py:229
  498.1 34.3 %all-to-all-done.3 = bf16[8,384,768]{2,1,0:T(8,128)(2,1)} async-done(((bf16[8,384,768]{2,1,0:T(8,128)(2,1)}), bf16[8,384,768]{2,1,0:T(8,128)(2,1)}, u32[]{:S(2)}, u32[]{:S(2)}) %all-to-all-start.3) | async-done | bytes 4718624 | tf_op jit(solution)/shard_map/all_to_all | solution.py:276
  566.3 25.6 %all-to-all-done.1 = bf16[8,384,768]{2,1,0:T(8,128)(2,1)} async-done(((bf16[8,384,768]{2,1,0:T(8,128)(2,1)}), bf16[8,384,768]{2,1,0:T(8,128)(2,1)}, u32[]{:S(2)}, u32[]{:S(2)}) %all-to-all-start.1) | async-done | bytes 4718624 | tf_op jit(solution)/shard_map/all_to_all | solution.py:233
  608.1 17.9 %multiply_reduce_fusion.2 = (f32[1024,2]{1,0:T(8,128)}, f32[1024,768]{1,0:T(8,128)}) fusion(f32[1024,2,768]{2,1,0:T(2,128)} %reshape.522, f32[1024,768]{1,0:T(8,128)} %copy-done.4, f32[1024,2]{1,0:T(8,128)} %copy-done.26), kind=kLoop, calls=%fused_computation.38 | loop fusion | flops 5502976 | bytes 12599296 | tf_op jit(solution)/shard_map/reduce_sum | solution.py:243
  646.0 19.7 %multiply_reduce_fusion = (f32[12,512]{1,0:T(8,128)S(1)}, f32[12,512,1024]{2,1,0:T(8,128)}) fusion(f32[12,512,1024]{2,1,0:T(8,128)} %get-tuple-element.104, f32[12,512]{1,0:T(8,128)S(1)} %copy-done.37, bf16[512,12,64]{0,2,1:T(8,128)(2,1)S(1)} %bitcast.163, bf16[1024,12,64]{0,2,1:T(8,128)(2,1)S(1)} %bitcast.154), kind=kOutput, calls=%fused_computation.29 | convolution fusion | flops 824174592 | bytes 52740096 | tf_op jit(solution)/shard_map/qhe,khe->hqk/dot_general | solution.py:106
  665.7 16.7 %multiply_convert_fusion.1 = bf16[12,512,1024]{2,1,0:T(8,128)(2,1)S(1)} fusion(f32[12,512,1024]{2,1,0:T(8,128)} %get-tuple-element.113, f32[12,512,1024]{2,1,0:T(8,128)} %get-tuple-element.104, f32[12,512]{1,0:T(8,128)S(1)} %get-tuple-element.112, f32[12,512]{1,0:T(8,128)S(1)} %copy-done.37), kind=kLoop, calls=%fused_computation.28 | loop fusion | flops 25165824 | bytes 62963712 | tf_op jit(solution)/shard_map/convert_element_type | solution.py:110
  690.0 16.5 %multiply_reduce_fusion.1 = (f32[12,512]{1,0:T(8,128)S(1)}, f32[12,512,1024]{2,1,0:T(8,128)}) fusion(f32[12,512,1024]{2,1,0:T(8,128)} %get-tuple-element.106, f32[12,512]{1,0:T(8,128)S(1)} %copy-done.35, bf16[512,12,64]{0,2,1:T(8,128)(2,1)} %bitcast.161, bf16[1024,12,64]{0,2,1:T(8,128)(2,1)} %bitcast.153), kind=kOutput, calls=%fused_computation.31 | convolution fusion | flops 824174592 | bytes 52740096 | tf_op jit(solution)/shard_map/qhe,khe->hqk/dot_general | solution.py:106
  706.5 16.5 %multiply_convert_fusion.2 = bf16[12,512,1024]{2,1,0:T(8,128)(2,1)S(1)} fusion(f32[12,512,1024]{2,1,0:T(8,128)} %get-tuple-element.115, f32[12,512,1024]{2,1,0:T(8,128)} %get-tuple-element.106, f32[12,512]{1,0:T(8,128)S(1)} %get-tuple-element.114, f32[12,512]{1,0:T(8,128)S(1)} %copy-done.35), kind=kLoop, calls=%fused_computation.30 | loop fusion | flops 25165824 | bytes 62963712 | tf_op jit(solution)/shard_map/convert_element_type | solution.py:110
  789.0 35.9 %reduce-scatter.12.cloned.1.call-done = f32[96,768]{1,0:T(8,128)} async-done(((f32[768,768]{1,0:T(8,128)}), f32[96,768]{1,0:T(8,128)}) %reduce-scatter.12.cloned.1.call-update) | async-done | bytes 294928 | tf_op jit(solution)/shard_map/reduce_scatter | solution.py:367
  825.0 45.9 %reduce-scatter.14.cloned.1.call-done = f32[96,768]{1,0:T(8,128)} async-done(((f32[768,768]{1,0:T(8,128)}), f32[96,768]{1,0:T(8,128)}) %reduce-scatter.14.cloned.1.call-update) | async-done | bytes 294928 | tf_op jit(solution)/shard_map/reduce_scatter | solution.py:368
  870.8 46.2 %reduce-scatter.16.cloned.1.call-done = f32[96,768]{1,0:T(8,128)} async-done(((f32[768,768]{1,0:T(8,128)}), f32[96,768]{1,0:T(8,128)}) %reduce-scatter.16.cloned.1.call-update) | async-done | bytes 294928 | tf_op jit(solution)/shard_map/reduce_scatter | solution.py:369
  917.2 21.3 %fusion.129 = f32[768,3072]{1,0:T(8,128)} fusion(bf16[3072,768]{1,0:T(8,128)(2,1)} %bitcast.22, bf16[3072,3072]{1,0:T(8,128)(2,1)} %fusion.10), kind=kOutput, calls=%fused_computation.185 | convolution fusion | flops 14495514624 | bytes 33030144 | tf_op jit(solution)/shard_map/rd,rf->df/dot_general | solution.py:266
  938.5 21.7 %fusion.130 = f32[3072,768]{1,0:T(8,128)} fusion(bf16[3072,3072]{1,0:T(8,128)(2,1)} %get-tuple-element.109, bf16[3072,768]{1,0:T(8,128)(2,1)} %bitcast.28), kind=kOutput, calls=%fused_computation.186 | convolution fusion | flops 14495514624 | bytes 33030144 | tf_op jit(solution)/shard_map/rf,rd->fd/dot_general | solution.py:260
  961.6 23.1 %copy.149 = bf16[12,512,1024]{1,0,2:T(8,128)(2,1)} copy(bf16[12,512,1024]{2,1,0:T(8,128)(2,1)} %copy-done.1) | data formatting | bytes 25165824 | tf_op jit(solution)/shard_map/convert_element_type | solution.py:110
  984.6 23.2 %copy.150 = bf16[12,512,1024]{1,0,2:T(8,128)(2,1)} copy(bf16[12,512,1024]{2,1,0:T(8,128)(2,1)} %copy-done) | data formatting | bytes 25165824 | tf_op jit(solution)/shard_map/convert_element_type | solution.py:110
  1047.7 22.8 %all-reduce.5 = (f32[768]{0:T(1024)S(1)}, f32[768]{0:T(1024)S(1)}, f32[32,12]{1,0:T(8,128)S(1)}) all-reduce(f32[768]{0:T(1024)S(1)} %get-tuple-element.76, f32[768]{0:T(1024)S(1)} %copy-done.60, f32[32,12]{1,0:T(8,128)S(1)} %fusion.100), channel_id=7, replica_groups=mesh['shard'=8,'rep'=4] {'shard'}, use_global_device_ids=true, to_apply=%region_34.35.clone | all-reduce | flops 1920 | bytes 15360
  1071.5 13.6 %all-reduce.6 = (f32[96,8]{0,1:T(8,128)}, f32[96]{0:T(128)}, f32[96]{0:T(128)}, f32[4,12]{1,0:T(4,128)}) all-reduce(f32[96,8]{0,1:T(8,128)S(1)} %copy.162, f32[96]{0:T(128)S(1)} %dynamic-slice.3, f32[96]{0:T(128)S(1)} %dynamic-slice.5, f32[4,12]{1,0:T(4,128)S(1)} %constant_dynamic-slice_fusion), channel_id=1, replica_groups=mesh['shard'=8,'rep'=4] {'rep'}, use_global_device_ids=true, to_apply=%region_32.33 | all-reduce | flops 1008 | bytes 8064 | tf_op jit(solution)/shard_map/psum | solution.py:375
  1085.2 92.6 %reduce-scatter.18.cloned.1.call-done = f32[768,768]{1,0:T(8,128)} async-done(((f32[768,3072]{1,0:T(8,128)}), f32[768,768]{1,0:T(8,128)}) %reduce-scatter.18.cloned.1.call-update) | async-done | bytes 2359312 | tf_op jit(solution)/shard_map/reduce_scatter | solution.py:273
  1177.8 164.9 %reduce-scatter.20.cloned.1.call-done = f32[768,768]{1,0:T(8,128)} async-done(((f32[3072,768]{1,0:T(8,128)}), f32[768,768]{1,0:T(8,128)}) %reduce-scatter.20.cloned.1.call-update) | async-done | bytes 2359312 | tf_op jit(solution)/shard_map/reduce_scatter | solution.py:274
  (293 shorter events, 345.2 us)
Async XLA Ops:
  7.2 144.4 %all-gather.9.cloned.1.call-start = ((), (), s32[]{:S(2)}) async-start(), calls=%async_computation.12 | async-start | bytes 1327104 | tf_op jit(solution)/shard_map/all_gather | solution.py:167
  7.9 147.7 %all-gather.11.cloned.1.call-start = ((), (), s32[]{:S(2)}) async-start(), calls=%async_computation.13 | async-start | bytes 1327104 | tf_op jit(solution)/shard_map/all_gather | solution.py:168
  8.7 177.4 %all-gather.7.cloned.1.call-start = ((), (), s32[]{:S(2)}) async-start(), calls=%async_computation.11 | async-start | bytes 1327104 | tf_op jit(solution)/shard_map/all_gather | solution.py:169
  9.4 229.8 %all-gather.13.cloned.1.call-start = ((), (), s32[]{:S(2)}) async-start(), calls=%async_computation.14 | async-start | bytes 1327104 | tf_op jit(solution)/shard_map/all_gather | solution.py:170
  12.8 20.7 %copy-start.66 = (bf16[4,12]{1,0:T(4,128)(2,1)S(1)}, bf16[4,12]{1,0:T(4,128)(2,1)}, u32[]{:S(2)}) copy-start(bf16[4,12]{1,0:T(4,128)(2,1)} %param.22) | copy-start | bytes 292
  16.0 139.7 %copy-start.8 = (bf16[1024,768]{0,1:T(8,128)(2,1)}, bf16[1024,768]{0,1:T(8,128)(2,1)S(1)}, u32[]{:S(2)}) copy-start(bf16[1024,768]{0,1:T(8,128)(2,1)S(1)} %copy.125) | copy-start | bytes 4718596
  33.1 153.0 %copy-start.52 = (f32[768]{0:T(1024)}, f32[768]{0:T(1024)S(1)}, u32[]{:S(2)}) copy-start(f32[768]{0:T(1024)S(1)} %convert_element_type.430) | copy-start | bytes 9220
  33.5 152.6 %copy-start.54 = (f32[1024]{0:T(1024)}, f32[1024]{0:T(1024)S(1)}, u32[]{:S(2)}) copy-start(f32[1024]{0:T(1024)S(1)} %fusion.108) | copy-start | bytes 12292
  65.5 30.5 %copy-start.61 = (s32[1,1024]{1,0:T(1,128)S(1)}, s32[1,1024]{1,0:T(1,128)}, u32[]{:S(2)}) copy-start(s32[1,1024]{1,0:T(1,128)} %param.25) | copy-start | bytes 12292
  145.7 98.3 %copy-start.48 = (f32[768]{0:T(1024)}, f32[768]{0:T(1024)S(1)}, u32[]{:S(2)}) copy-start(f32[768]{0:T(1024)S(1)} %convert_element_type.468) | copy-start | bytes 9220
  149.1 187.6 %copy-start.58 = (s32[2048,1]{0,1:T(1,128)}, s32[2048,1]{0,1:T(1,128)S(1)}, u32[]{:S(2)}) copy-start(s32[2048,1]{0,1:T(1,128)S(1)} %compare_select_fusion.2) | copy-start | bytes 24580
  158.4 42.7 %copy-start.5 = (bf16[1024,768]{0,1:T(8,128)(2,1)}, bf16[1024,768]{0,1:T(8,128)(2,1)S(1)}, u32[]{:S(2)}) copy-start(bf16[1024,768]{0,1:T(8,128)(2,1)S(1)} %convolution_convert_fusion.3) | copy-start | bytes 4718596
  189.4 39.2 %copy-start.6 = (bf16[1024,768]{0,1:T(8,128)(2,1)}, bf16[1024,768]{0,1:T(8,128)(2,1)S(1)}, u32[]{:S(2)}) copy-start(bf16[1024,768]{0,1:T(8,128)(2,1)S(1)} %convolution_convert_fusion.5) | copy-start | bytes 4718596
  270.7 80.4 %all-to-all-start = ((bf16[8,384,768]{2,1,0:T(8,128)(2,1)}), bf16[8,384,768]{2,1,0:T(8,128)(2,1)}, u32[]{:S(2)}, u32[]{:S(2)}) async-start(bf16[8,384,768]{2,1,0:T(8,128)(2,1)} %bitcast.155), calls=%async_computation | async-start | bytes 9437184 | tf_op jit(solution)/shard_map/all_to_all | solution.py:223
  283.7 51.2 %copy-start.40 = (s32[1024,2]{0,1:T(2,128)S(1)}, s32[1024,2]{0,1:T(2,128)}, u32[]{:S(2)}) copy-start(s32[1024,2]{0,1:T(2,128)} %param.26) | copy-start | bytes 24580
  351.0 59.4 %all-to-all-start.2 = ((bf16[8,384,768]{2,1,0:T(8,128)(2,1)}), bf16[8,384,768]{2,1,0:T(8,128)(2,1)}, u32[]{:S(2)}, u32[]{:S(2)}) async-start(bf16[8,384,768]{2,1,0:T(8,128)(2,1)} %bitcast.156), calls=%async_computation.2 | async-start | bytes 9437184 | tf_op jit(solution)/shard_map/all_to_all | solution.py:255
  355.6 98.1 %slice-start = ((s8[4718592]{0:T(1024)(128)(4,1)}), s8[524288]{0:T(1024)(128)(4,1)S(1)}, s32[]{:S(2)}) async-start(s8[4718592]{0:T(1024)(128)(4,1)} %bitcast.187), calls=%async_computation.23 | async-start | bytes 1048576
  410.4 43.3 %slice-start.1 = ((s8[4718592]{0:T(1024)(128)(4,1)}), s8[4194304]{0:T(1024)(128)(4,1)S(1)}, s32[]{:S(2)}) async-start(s8[4718592]{0:T(1024)(128)(4,1)} %bitcast.187), calls=%async_computation.24 | async-start | bytes 8388608
  473.1 59.4 %all-to-all-start.3 = ((bf16[8,384,768]{2,1,0:T(8,128)(2,1)}), bf16[8,384,768]{2,1,0:T(8,128)(2,1)}, u32[]{:S(2)}, u32[]{:S(2)}) async-start(bf16[8,384,768]{2,1,0:T(8,128)(2,1)} %bitcast.168), calls=%async_computation.3 | async-start | bytes 9437184 | tf_op jit(solution)/shard_map/all_to_all | solution.py:276
  532.4 59.5 %all-to-all-start.1 = ((bf16[8,384,768]{2,1,0:T(8,128)(2,1)}), bf16[8,384,768]{2,1,0:T(8,128)(2,1)}, u32[]{:S(2)}, u32[]{:S(2)}) async-start(bf16[8,384,768]{2,1,0:T(8,128)(2,1)} %bitcast.167), calls=%async_computation.1 | async-start | bytes 9437184 | tf_op jit(solution)/shard_map/all_to_all | solution.py:233
  537.2 251.9 %reduce-scatter.10.cloned.1.call-start = ((), (), s32[]{:S(2)}) async-start(), calls=%async_computation.15 | async-start | bytes 2654208 | tf_op jit(solution)/shard_map/reduce_scatter | solution.py:366
  608.0 19.3 %copy-start.43 = (bf16[768,8]{0,1:T(8,128)(2,1)S(1)}, bf16[768,8]{0,1:T(8,128)(2,1)}, u32[]{:S(2)}) copy-start(bf16[768,8]{0,1:T(8,128)(2,1)} %copy-done.42) | copy-start | bytes 36868
  608.1 19.3 %copy-start.49 = (f32[768]{0:T(1024)S(1)}, f32[768]{0:T(1024)}, u32[]{:S(2)}) copy-start(f32[768]{0:T(1024)} %copy-done.48) | copy-start | bytes 9220
  645.4 20.4 %copy-start.21 = (bf16[512,768]{0,1:T(8,128)(2,1)}, bf16[512,768]{0,1:T(8,128)(2,1)S(1)}, u32[]{:S(2)}) copy-start(bf16[512,768]{0,1:T(8,128)(2,1)S(1)} %get-tuple-element.94) | copy-start | bytes 2359300
  736.2 88.8 %reduce-scatter.12.cloned.1.call-start = ((), (), s32[]{:S(2)}) async-start(), calls=%async_computation.16 | async-start | bytes 2654208 | tf_op jit(solution)/shard_map/reduce_scatter | solution.py:367
  755.4 115.5 %reduce-scatter.14.cloned.1.call-start = ((), (), s32[]{:S(2)}) async-start(), calls=%async_computation.17 | async-start | bytes 2654208 | tf_op jit(solution)/shard_map/reduce_scatter | solution.py:368
  781.2 135.9 %reduce-scatter.16.cloned.1.call-start = ((), (), s32[]{:S(2)}) async-start(), calls=%async_computation.18 | async-start | bytes 2654208 | tf_op jit(solution)/shard_map/reduce_scatter | solution.py:369
  786.6 284.1 %reduce-scatter.22.cloned.1.call-start = ((), (), s32[]{:S(2)}) async-start(), calls=%async_computation.21 | async-start | bytes 442368
  788.8 296.4 %all-reduce.11.cloned.1.call-start = ((), (), s32[]{:S(2)}) async-start(), calls=%async_computation.22 | async-start | bytes 2359296 | tf_op jit(solution)/shard_map/psum | solution.py:375
  917.1 260.7 %reduce-scatter.18.cloned.1.call-start = ((), (), s32[]{:S(2)}) async-start(), calls=%async_computation.19 | async-start | bytes 11796480 | tf_op jit(solution)/shard_map/reduce_scatter | solution.py:273
  938.5 404.2 %reduce-scatter.20.cloned.1.call-start = ((), (), s32[]{:S(2)}) async-start(), calls=%async_computation.20 | async-start | bytes 11796480 | tf_op jit(solution)/shard_map/reduce_scatter | solution.py:274
  984.6 23.2 %copy-start.25 = (bf16[1024,768]{0,1:T(8,128)(2,1)S(1)}, bf16[1024,768]{0,1:T(8,128)(2,1)}, u32[]{:S(2)}) copy-start(bf16[1024,768]{0,1:T(8,128)(2,1)} %get-tuple-element.92) | copy-start | bytes 4718596
  (57 other events, 353.2 us)
Sparse Core Ops, SparseCore 0:
  9.9 26.8 all-gather.8
  38.6 24.0 all-gather.10
  64.6 24.0 all-gather.6
  90.4 24.0 all-gather.12
  736.3 41.9 reduce-scatter.9
  782.4 42.4 reduce-scatter.11
  828.3 42.4 reduce-scatter.13
  874.6 42.4 reduce-scatter.15
  920.1 33.8 reduce-scatter.21
  956.5 56.9 all-reduce.10
  1016.4 161.3 reduce-scatter.17
  1180.6 162.0 reduce-scatter.19
where the time goes:
time: 1360 us
  waiting for transfers between devices  471 us (35%)
  matrix products  404 us (30%)
  local copies, waits for them, and re-layouts  224 us (16%)
  other arithmetic  120 us (9%)
  blocking collectives  101 us (7%)
  starting transfers between devices  19.7 us (1%)
  between operations  17.6 us (1%)
    reduce_scatter x1, waiting for transfers between devices, body(): lax.psum_scatter(grad_out_part, 'rep', scatter_dimension=0, tiled=True)  165 us
    reduce_scatter x1, waiting for transfers between devices, body(): lax.psum_scatter(grad_in_part, 'rep', scatter_dimension=1, tiled=True)  92.6 us
    dot_general x2, local copies, waits for them, and re-layouts, block_scores(): jnp.einsum('vye,vo->oye', one_hot_matrix, relative_bias_matrix, preferred...  60.8 us
    convert_element_type x2, local copies, waits for them, and re-layouts, sequence_backward(): score_gradient = (attn_probs * (grad_probs - row_dot)).astype(jnp.bfloat16)  46.3 us
    reduce_scatter x1, waiting for transfers between devices, body(): lax.psum_scatter(partial_grads[3], 'shard', scatter_dimension=0, tiled=True)  46.2 us
    reduce_scatter x1, waiting for transfers between devices, body(): lax.psum_scatter(partial_grads[2], 'shard', scatter_dimension=0, tiled=True)  45.9 us
    dot_general x1, matrix products, body(): jnp.einsum('rd,fd->rf', grad_rows, weight_out, preferred_element_type=jnp...  43.3 us
    all_gather x1, blocking collectives, body(): lax.all_gather(shared[4], 'shard', axis=0, tiled=True)  40.9 us
  transfers between devices with their start and end apart: 16, of which 8 were waited for; matrix products, arithmetic and copies ran while one was open for 37% of the time, Pallas kernels for 0%

commit v1 on v0

v1 whole, which is shorter than its diff:
```python
import functools
import math
import jax
import jax.numpy as jnp
from jax import lax
from jax.experimental import pallas as pl
from jax.experimental.pallas import tpu as pltpu
from jax.sharding import PartitionSpec as P

HEADS = 12
BUCKETS = 32
MAX_DISTANCE = 128
LONGEST = 512
QB = 256
BIG = 1e9
LANES = 128
FF_TILE = 512
ROW_BLOCK = 384
TILE = 256
CHUNKS = 2
GELU_A = math.sqrt(2 / math.pi)
GELU_B = 0.044715
eps_norm = 1e-06


def bucket_table(distance):
    half_count = BUCKETS // 2
    clipped = jnp.maximum(distance, 0)
    counted = jnp.zeros(distance.shape, jnp.int32)
    for section_number in range(1, half_count):
        threshold = math.ceil(
            half_count * (MAX_DISTANCE / half_count) ** (section_number / half_count)
        )
        counted = counted + (clipped >= threshold).astype(jnp.int32)
    return jnp.where(clipped < half_count, clipped, half_count + counted)


def window_distance():
    span = LONGEST + 2 * QB
    place = jnp.arange(span, dtype=jnp.int32)
    place = jnp.where(place >= LONGEST + QB, place - span, place)
    return LONGEST - place


def bias_rows(table):
    distance = window_distance()
    onehot = bucket_table(distance)[None, :] == jnp.arange(BUCKETS, dtype=jnp.int32)[:, None]
    rows = jnp.sum(
        jnp.where(onehot[None], table.astype(jnp.float32).T[:, :, None], 0.0), axis=1
    )
    return jnp.where(distance[None, :] >= 0, rows, -BIG)


def segment_lanes(segment, width):
    lane = jnp.arange(width, dtype=jnp.int32)[None, :] % (width // 2)
    same = segment[:, None] == lane
    first = lane < 4
    query_lanes = jnp.where(first & same, 1.0, 0.0)
    key_lanes = jnp.where(first, jnp.where(same, 0.0, -BIG), jnp.where(lane < 7, 1.0, 0.0))
    return query_lanes.astype(jnp.bfloat16), key_lanes.astype(jnp.bfloat16)


def toeplitz(row):
    span = row.shape[-1]
    full = jnp.broadcast_to(row, (QB, span))
    return pltpu.roll(full, 0, 1, stride=1, stride_axis=0)[:, : LONGEST + QB]


def nt(a, b):
    return lax.dot_general(a, b, (((1,), (1,)), ((), ())), preferred_element_type=jnp.float32)


def nn(a, b):
    return jnp.dot(a, b, preferred_element_type=jnp.float32)


def tn(a, b):
    return lax.dot_general(a, b, (((0,), (0,)), ((), ())), preferred_element_type=jnp.float32)


def forward_kernel(q_ref, k_ref, v_ref, ql_ref, kl_ref, row_ref, out_ref, lse_ref):
    pair = pl.program_id(0)
    length, width = q_ref.shape
    half = width // 2
    lane = lax.broadcasted_iota(jnp.int32, (QB, width), 1)
    lane_k = lax.broadcasted_iota(jnp.int32, (length, width), 1)

    @pl.when(pair == 0)
    def _():
        lse_ref[...] = jnp.zeros_like(lse_ref)

    biases = [toeplitz(row_ref[0, h : h + 1, :]) for h in range(2)]
    keys = [
        jnp.where((lane_k < half) == (h == 0), k_ref[...], kl_ref[...]) for h in range(2)
    ]
    for start in range(0, length, QB):
        low = max(0, start - LONGEST)
        wide = start + QB - low
        q = (q_ref[start : start + QB, :].astype(jnp.float32) * (half**-0.5)).astype(jnp.bfloat16)
        outs = []
        lse = lse_ref[start : start + QB, :]
        for h in range(2):
            mine = (lane < half) == (h == 0)
            q_own = jnp.where(mine, q, ql_ref[start : start + QB, :])
            s = nt(q_own, keys[h][low : start + QB, :]) + biases[h][:, LONGEST + QB - wide :]
            peak = jnp.max(s, axis=1, keepdims=True)
            p = jnp.exp(s - peak)
            total = jnp.sum(p, axis=1, keepdims=True)
            o = nn(p.astype(jnp.bfloat16), v_ref[low : start + QB, :])
            outs.append(o * (1.0 / total))
            lse = jnp.where(lane == 2 * pair + h, peak + jnp.log(total), lse)
        lse_ref[start : start + QB, :] = lse
        out_ref[start : start + QB, :] = jnp.where(lane < half, outs[0], outs[1]).astype(
            jnp.bfloat16
        )


def attention_forward(qk, v, query_lanes, key_lanes, rows):
    length, model = v.shape
    pairs = HEADS // 2
    width = model // pairs
    span = rows.shape[-1]
    return pl.pallas_call(
        forward_kernel,
        grid=(pairs,),
        in_specs=[
            pl.BlockSpec((length, width), lambda p: (0, p)),
            pl.BlockSpec((length, width), lambda p: (0, p + pairs)),
            pl.BlockSpec((length, width), lambda p: (0, p)),
            pl.BlockSpec((length, width), lambda p: (0, 0)),
            pl.BlockSpec((length, width), lambda p: (0, 0)),
            pl.BlockSpec((1, 2, span), lambda p: (p, 0, 0)),
        ],
        out_specs=[
            pl.BlockSpec((length, width), lambda p: (0, p)),
            pl.BlockSpec((length, width), lambda p: (0, 0)),
        ],
        out_shape=[
            jax.ShapeDtypeStruct((length, model), jnp.bfloat16),
            jax.ShapeDtypeStruct((length, width), jnp.float32),
        ],
        compiler_params=pltpu.CompilerParams(
            dimension_semantics=("arbitrary",), vmem_limit_bytes=40 * 1024 * 1024
        ),
        cost_estimate=pl.CostEstimate(
            flops=1024, bytes_accessed=1024, transcendentals=0
        ),
        name="attention_forward",
    )(qk, qk, v, query_lanes, key_lanes, rows.reshape(pairs, 2, span))


def three_parts(column):
    first = column.astype(jnp.bfloat16).astype(jnp.float32)
    rest = column - first
    second = rest.astype(jnp.bfloat16).astype(jnp.float32)
    return first, second, rest - second


def with_column(lane, half, base, column):
    a, b, c = three_parts(column)
    spare = lane % half
    packed = jnp.where(spare == 4, a, jnp.where(spare == 5, b, jnp.where(spare == 6, c, base)))
    return packed.astype(jnp.bfloat16)


def backward_kernel(
    q_ref, k_ref, v_ref, o_ref, g_ref, ql_ref, kl_ref, row_ref, lse_ref,
    grad_ref, table_ref, dk_acc, dv_acc, diag_acc,
):
    pair = pl.program_id(0)
    length, width = q_ref.shape
    half = width // 2
    window = LONGEST + QB
    lane = lax.broadcasted_iota(jnp.int32, (QB, width), 1)
    lane_k = lax.broadcasted_iota(jnp.int32, (length, width), 1)
    dk_acc[...] = jnp.zeros_like(dk_acc)
    dv_acc[...] = jnp.zeros_like(dv_acc)
    diag_acc[...] = jnp.zeros_like(diag_acc)
    zero = jnp.zeros((), jnp.bfloat16)
    biases = [toeplitz(row_ref[0, h : h + 1, :]).T for h in range(2)]
    owned_k = [(lane_k < half) == (h == 0) for h in range(2)]
    keys = [jnp.where(owned_k[h], k_ref[...], kl_ref[...]) for h in range(2)]
    bare_keys = [jnp.where(owned_k[h], k_ref[...], zero) for h in range(2)]
    values = [jnp.where(owned_k[h], v_ref[...], kl_ref[...]) for h in range(2)]
    for start in range(0, length, QB):
        low = max(0, start - LONGEST)
        wide = start + QB - low
        stop = start + QB
        q = (q_ref[start:stop, :].astype(jnp.float32) * (half**-0.5)).astype(jnp.bfloat16)
        g = g_ref[start:stop, :]
        dot_all = g.astype(jnp.float32) * o_ref[start:stop, :].astype(jnp.float32)
        lse_all = lse_ref[start:stop, :]
        q_lanes = ql_ref[start:stop, :].astype(jnp.float32)
        turned = None
        for h in range(2):
            mine = (lane < half) == (h == 0)
            lse = jnp.sum(jnp.where(lane == 2 * pair + h, lse_all, 0.0), axis=1, keepdims=True)
            dot = jnp.sum(jnp.where(mine, dot_all, 0.0), axis=1, keepdims=True)
            q_own = jnp.where(mine, q, with_column(lane, half, q_lanes, -lse))
            g_own = jnp.where(mine, g, with_column(lane, half, jnp.zeros_like(q_lanes), -dot))
            s = nt(keys[h][low:stop, :], q_own) + biases[h][window - wide :, :]
            p = jnp.exp(s)
            dp = nt(values[h][low:stop, :], g_own)
            ds = p * dp
            diag_acc[h, window - wide :, :] += ds
            ds_low = ds.astype(jnp.bfloat16)
            dv_acc[low:stop, :] += nn(p.astype(jnp.bfloat16), jnp.where(mine, g, zero))
            dk_acc[low:stop, :] += nn(ds_low, jnp.where(mine, q, zero))
            part = tn(bare_keys[h][low:stop, :], ds_low)
            turned = part if turned is None else turned + part
        grad_ref[0, start:stop, :] = (turned * (half**-0.5)).T.astype(jnp.bfloat16)
    grad_ref[1] = dk_acc[...].astype(jnp.bfloat16)
    grad_ref[2] = dv_acc[...].astype(jnp.bfloat16)
    span = window + QB
    for h in range(2):
        flat = jnp.concatenate([diag_acc[h].T, jnp.zeros((QB, QB), jnp.float32)], axis=1)
        eight = flat[0:8, :]
        for row in range(8, QB, 8):
            eight = eight + pltpu.roll(flat[row : row + 8, :], span - row, 1)
        total = eight[0:1, :]
        for row in range(1, 8):
            total = total + pltpu.roll(eight[row : row + 1, :], span - row, 1)
        table_ref[0, h : h + 1, :] = total


def attention_backward(qk, v, attended, grad_attended, query_lanes, key_lanes, rows, lse):
    length, model = v.shape
    pairs = HEADS // 2
    width = model // pairs
    span = rows.shape[-1]
    block = pl.BlockSpec((length, width), lambda p: (0, p))
    same = pl.BlockSpec((length, width), lambda p: (0, 0))
    low = jax.ShapeDtypeStruct((3, length, model), jnp.bfloat16)
    return pl.pallas_call(
        backward_kernel,
        grid=(pairs,),
        in_specs=[
            block,
            pl.BlockSpec((length, width), lambda p: (0, p + pairs)),
            pl.BlockSpec((length, width), lambda p: (0, p)),
            block,
            block,
            same,
            same,
            pl.BlockSpec((1, 2, span), lambda p: (p, 0, 0)),
            same,
        ],
        out_specs=[
            pl.BlockSpec((3, length, width), lambda p: (0, 0, p)),
            pl.BlockSpec((1, 2, span), lambda p: (p, 0, 0)),
        ],
        out_shape=[low, jax.ShapeDtypeStruct((pairs, 2, span), jnp.float32)],
        scratch_shapes=[
            pltpu.VMEM((length, width), jnp.float32),
            pltpu.VMEM((length, width), jnp.float32),
            pltpu.VMEM((2, LONGEST + QB, QB), jnp.float32),
        ],
        compiler_params=pltpu.CompilerParams(
            dimension_semantics=("arbitrary",), vmem_limit_bytes=48 * 1024 * 1024
        ),
        cost_estimate=pl.CostEstimate(
            flops=1024, bytes_accessed=1024, transcendentals=0
        ),
        name="attention_backward",
    )(
        qk, qk, v, attended, grad_attended, query_lanes, key_lanes,
        rows.reshape(pairs, 2, span), lse,
    )


def table_gradient(diagonals):
    distance = window_distance()
    onehot = (bucket_table(distance)[:, None] == jnp.arange(BUCKETS, dtype=jnp.int32)[None, :]) & (
        distance >= 0
    )[:, None]
    flat = diagonals.reshape(HEADS, -1)
    return jnp.sum(jnp.where(onehot[:, :, None], flat.T[:, None, :], 0.0), axis=0)


def expert_forward_kernel(
    me_ref, x_ref, g_ref, sum_ref, in_ref, out_ref, router_ref, *refs
):
    y_ref, active_ref, gated_ref, slope_ref, logit_ref, router_grad_ref = refs[-6:]
    step = pl.program_id(0)
    model, hidden = in_ref.shape
    rows = x_ref.shape[0] * x_ref.shape[1]
    x = x_ref[...].reshape(rows, model)
    grad = g_ref[...].reshape(rows, model).astype(jnp.float32)
    id_sum = sum_ref[...].reshape(rows, LANES).astype(jnp.float32)
    me = me_ref[0].astype(jnp.float32)
    lane = lax.broadcasted_iota(jnp.int32, (rows, LANES), 1)
    expert = (lane % (LANES // 2)).astype(jnp.float32)
    own = expert == me
    other = expert == id_sum - me
    first = lane < LANES // 2
    logits = nn(x, router_ref[...])
    own_logit = jnp.sum(jnp.where(first & own, logits, 0.0), axis=1, keepdims=True)
    other_logit = jnp.sum(jnp.where(first & other, logits, 0.0), axis=1, keepdims=True)
    gate = 1.0 / (1.0 + jnp.exp(other_logit - own_logit))
    other_gate = 1.0 / (1.0 + jnp.exp(own_logit - other_logit))
    gated_ref[...] = (gate * grad).astype(jnp.bfloat16)
    for low in range(0, hidden, FF_TILE):
        cut = slice(low, low + FF_TILE)
        v = nn(x, in_ref[:, cut])
        square = v * v
        t = jnp.tanh(v * (GELU_A + GELU_A * GELU_B * square))
        h = 0.5 + 0.5 * t
        a = v * h
        slope = h + (a * (1.0 - h)) * (2.0 * GELU_A + 6.0 * GELU_A * GELU_B * square)
        active_ref[:, cut] = a.astype(jnp.bfloat16)
        slope_ref[:, cut] = slope.astype(jnp.bfloat16)
    result = nn(active_ref[...], out_ref[...])
    y_ref[...] = (gate * result).astype(jnp.bfloat16).reshape(y_ref.shape)
    gate_grad = jnp.sum(grad * result, axis=1, keepdims=True)
    weight = gate * other_gate * gate_grad
    logit_grad = jnp.where(own, weight, 0.0) - jnp.where(other, weight, 0.0)
    high = logit_grad.astype(jnp.bfloat16)
    rest = (logit_grad - high.astype(jnp.float32)).astype(jnp.bfloat16)
    logit_low = jnp.where(first, high, rest)
    logit_ref[...] = logit_low
    part = tn(x, logit_low)

    @pl.when(step == 0)
    def _():
        router_grad_ref[...] = part

    @pl.when(step > 0)
    def _():
        router_grad_ref[...] += part


def expert_backward_kernel(
    gated_ref, slope_ref, logit_ref, in_ref, out_ref, router_ref, *refs
):
    pre_ref, back_ref = refs[-2:]
    hidden = in_ref.shape[1]
    gated = gated_ref[...]
    for low in range(0, hidden, FF_TILE):
        cut = slice(low, low + FF_TILE)
        d = nt(gated, out_ref[cut, :])
        pre_ref[:, cut] = (d * slope_ref[:, cut].astype(jnp.float32)).astype(jnp.bfloat16)
    back = nt(pre_ref[...], in_ref[...]) + nt(logit_ref[...], router_ref[...])
    back_ref[...] = back.astype(jnp.bfloat16).reshape(back_ref.shape)


def low_shape(*dims):
    return jax.ShapeDtypeStruct(dims, jnp.bfloat16)


def expert_forward(me, x, grads, sums, chunk, weight_in, weight_out, router_two, kept):
    experts, half, model = x.shape
    hidden = weight_in.shape[1]
    group = max(1, min(experts, ROW_BLOCK // half))
    rows = group * half
    total = experts * half
    fixed = lambda *dims: pl.BlockSpec(dims, lambda i, m: (0, 0), pipeline_mode=pl.Buffered(1))
    flat = lambda width: pl.BlockSpec((rows, width), lambda i, m: (i, 0))
    steps = experts // group
    joint = lambda width: pl.BlockSpec((rows, width), lambda i, m: (i + chunk * steps, 0))
    return pl.pallas_call(
        expert_forward_kernel,
        grid_spec=pltpu.PrefetchScalarGridSpec(
            num_scalar_prefetch=1,
            grid=(experts // group,),
            in_specs=[
                pl.BlockSpec((group, half, model), lambda i, m: (i, 0, 0)),
                pl.BlockSpec((group, half, model), lambda i, m: (i, chunk, 0)),
                pl.BlockSpec((group, half, LANES), lambda i, m: (i, chunk, 0)),
                fixed(model, hidden),
                fixed(hidden, model),
                fixed(model, LANES),
            ]
            + [pl.BlockSpec(memory_space=pl.ANY)] * len(kept),
            out_specs=[
                pl.BlockSpec((group, half, model), lambda i, m: (i, chunk, 0)),
                joint(hidden),
                joint(model),
                flat(hidden),
                flat(LANES),
                pl.BlockSpec((model, LANES), lambda i, m: (0, 0)),
            ],
        ),
        out_shape=[
            low_shape(experts, CHUNKS * half, model),
            low_shape(CHUNKS * total, hidden),
            low_shape(CHUNKS * total, model),
            low_shape(total, hidden),
            low_shape(total, LANES),
            jax.ShapeDtypeStruct((model, LANES), jnp.float32),
        ],
        compiler_params=pltpu.CompilerParams(
            dimension_semantics=("arbitrary",), vmem_limit_bytes=56 * 1024 * 1024
        ),
        cost_estimate=pl.CostEstimate(
            flops=4 * total * model * hidden,
            bytes_accessed=4 * total * hidden + 4 * model * hidden + 8 * total * model,
            transcendentals=total * hidden,
        ),
        input_output_aliases={7 + place: place for place in range(len(kept))},
        name="expert_forward",
    )(me, x, grads, sums, weight_in, weight_out, router_two, *kept)


def expert_backward(
    experts, gated, slope, logit_low, chunk, weight_in, weight_out, router_two, kept
):
    total, hidden = slope.shape
    model = gated.shape[1]
    half = total // experts
    group = max(1, min(experts, ROW_BLOCK // half))
    rows = group * half
    fixed = lambda *dims: pl.BlockSpec(dims, lambda i: (0, 0), pipeline_mode=pl.Buffered(1))
    flat = lambda width: pl.BlockSpec((rows, width), lambda i: (i, 0))
    steps = experts // group
    joint = lambda width: pl.BlockSpec((rows, width), lambda i: (i + chunk * steps, 0))
    return pl.pallas_call(
        expert_backward_kernel,
        grid=(experts // group,),
        in_specs=[
            joint(model),
            flat(hidden),
            flat(LANES),
            fixed(model, hidden),
            fixed(hidden, model),
            fixed(model, LANES),
        ]
        + [pl.BlockSpec(memory_space=pl.ANY)] * len(kept),
        out_specs=[joint(hidden), pl.BlockSpec((group, half, model), lambda i: (i, 0, 0))],
        out_shape=[low_shape(CHUNKS * total, hidden), low_shape(experts, half, model)],
        compiler_params=pltpu.CompilerParams(
            dimension_semantics=("arbitrary",), vmem_limit_bytes=56 * 1024 * 1024
        ),
        cost_estimate=pl.CostEstimate(flops=1024, bytes_accessed=1024, transcendentals=0),
        input_output_aliases={6 + place: place for place in range(len(kept))},
        name="expert_backward",
    )(gated, slope, logit_low, weight_in, weight_out, router_two, *kept)


def swap(values, axis, bit):
    count = lax.axis_size(axis)
    return lax.ppermute(values, axis, [(place, place ^ bit) for place in range(count)])


def bits_of(axis):
    count = lax.axis_size(axis)
    return [1 << place for place in range(count.bit_length() - 1)]


def spread_rows(part, axis, bits):
    held, offsets = part[None], [0]
    for bit in bits:
        held = jnp.concatenate([held, swap(held, axis, bit)], axis=0)
        offsets = offsets + [offset ^ bit for offset in offsets]
    place = [0] * len(offsets)
    for index, offset in enumerate(offsets):
        place[offset // 2] = index
    return held, swap(held, axis, 1), place


def order_kernel(order_ref, *refs):
    count = len(refs) // 3
    chips = refs[0].shape[0]
    core = order_ref[0]
    for part in range(count):
        near, far, out = refs[2 * part], refs[2 * part + 1], refs[2 * count + part]
        for chip in range(chips):
            source = order_ref[1 + part * chips + chip]
            out[chip, core] = near[source]
            out[chip, 1 - core] = far[source]


def gather_rows(parts, axis, orders):
    spread = [spread_rows(part, axis, bits) for part, bits in zip(parts, orders)]
    me = lax.axis_index(axis).astype(jnp.int32)
    chips = spread[0][0].shape[0]
    order = [(me % 2)[None]]
    for _, _, place in spread:
        order.append(
            jnp.asarray(place, jnp.int32)[jnp.arange(chips, dtype=jnp.int32) ^ (me // 2)]
        )
    whole = pl.BlockSpec(memory_space=pltpu.VMEM)
    full = pl.pallas_call(
        order_kernel,
        in_specs=[pl.BlockSpec(memory_space=pltpu.SMEM)] + [whole] * (2 * len(parts)),
        out_specs=[whole] * len(parts),
        out_shape=[
            jax.ShapeDtypeStruct((chips, 2) + part.shape, part.dtype) for part in parts
        ],
        compiler_params=pltpu.CompilerParams(vmem_limit_bytes=24 * 1024 * 1024),
        name="rows_in_order",
    )(jnp.concatenate(order), *(array for near, far, _ in spread for array in (near, far)))
    return [
        array.reshape(2 * chips * part.shape[0], part.shape[1])
        for array, part in zip(full, parts)
    ], [near for near, _, _ in spread]


def scatter_sum(blocks, axis):
    count, rows, width = blocks.shape
    bits = bits_of(axis)
    me = lax.axis_index(axis)

    def step(values, left, bit):
        at = left.index(bit)
        mine = (me // bit) % 2
        keep = lax.dynamic_index_in_dim(values, mine, at, keepdims=False)
        away = lax.dynamic_index_in_dim(values, 1 - mine, at, keepdims=False)
        came = swap(away, axis, bit)
        total = keep.astype(jnp.float32) + came.astype(jnp.float32)
        return total.astype(jnp.bfloat16), [other for other in left if other != bit]

    left = bits[::-1]
    values = blocks.reshape((2,) * len(bits) + (rows, width))
    values, left = step(values, left, 1)
    cut = width // 2
    parts = []
    for half, order in ((values[..., :cut], bits[1:]), (values[..., cut:], bits[:0:-1])):
        remaining = left
        for bit in order:
            half, remaining = step(half, remaining, bit)
        parts.append(half)
    return jnp.concatenate(parts, axis=-1)


def sum_all(values, axis):
    rows = values.shape[0]
    bits = bits_of(axis)
    mine = lax.axis_index(axis) % 2
    low, high = values[: rows // 2], values[rows // 2 :]
    keep = jnp.where(mine == 0, low, high)
    came = swap(jnp.where(mine == 0, high, low), axis, 1)
    half = (keep.astype(jnp.float32) + came.astype(jnp.float32)).astype(jnp.bfloat16)
    for bit in bits[1:]:
        came = swap(half, axis, bit)
        half = (half.astype(jnp.float32) + came.astype(jnp.float32)).astype(jnp.bfloat16)
    came = swap(half, axis, 1)
    return jnp.concatenate(
        [jnp.where(mine == 0, half, came), jnp.where(mine == 0, came, half)], axis=0
    )


def weight_grad_kernel(steps, left_ref, right_ref, *refs):
    out_ref, turned = refs[-2:]
    step = pl.program_id(0)

    @pl.when(step == 0)
    def _():
        turned[...] = left_ref[...].T

    def product():
        out_ref[...] = nn(turned[...], right_ref[0]).astype(jnp.bfloat16)

    if len(refs) == 2:
        product()
    else:
        pl.when(step < steps)(product)

        @pl.when(step >= steps)
        def _():
            out_ref[...] = refs[0][...]


def weight_grad(left, right, extra=None):
    tokens, model = left.shape
    parts, _, width = right.shape
    cuts = width // TILE
    steps = parts * cuts
    last = steps - 1
    in_specs = [
        pl.BlockSpec((tokens, model), lambda i: (0, 0)),
        pl.BlockSpec(
            (1, tokens, TILE), lambda i: (jnp.minimum(i, last) // cuts, 0, jnp.minimum(i, last) % cuts)
        ),
    ]
    operands = [left, right]
    if extra is not None:
        in_specs.append(pl.BlockSpec((model, TILE), lambda i: (0, jnp.maximum(i - last - 1, 0))))
        operands.append(extra)
        steps = steps + extra.shape[1] // TILE
    return pl.pallas_call(
        functools.partial(weight_grad_kernel, last + 1),
        grid=(steps,),
        in_specs=in_specs,
        out_specs=pl.BlockSpec((model, TILE), lambda i: (0, i)),
        out_shape=jax.ShapeDtypeStruct((model, steps * TILE), jnp.bfloat16),
        scratch_shapes=[pltpu.VMEM((model, tokens), jnp.bfloat16)],
        compiler_params=pltpu.CompilerParams(
            dimension_semantics=("arbitrary",), vmem_limit_bytes=32 * 1024 * 1024
        ),
        cost_estimate=pl.CostEstimate(flops=1024, bytes_accessed=1024, transcendentals=0),
        name="weight_grad",
    )(*operands)


def rms_scale(values, gain_vec):
    mean_square = jnp.mean(values * values, axis=-1, keepdims=True)
    return values * lax.rsqrt(mean_square + eps_norm) * gain_vec


def pick_rows(places, source):
    return jnp.dot(places, source, preferred_element_type=jnp.float32).astype(jnp.bfloat16)


def back_rows(places, slots):
    return jnp.einsum("st,sd->td", places, slots, preferred_element_type=jnp.float32)


def body(
    inputs,
    w_query,
    w_key,
    w_value,
    w_output,
    w_router,
    gain_attn,
    gain_expert,
    rel_bias,
    w_in,
    w_out,
    segment_ids,
    expert_ids,
    out_grad,
):
    tokens_here, model_width = inputs.shape
    experts = lax.axis_size("shard")
    me = lax.axis_index("shard").astype(jnp.int32)
    capacity = 3 * tokens_here // experts
    half = capacity // CHUNKS
    rows_here = w_query.shape[0]
    table_here = rel_bias.shape[0]
    table_at = experts + 2

    small = jnp.concatenate(
        [
            w_router,
            gain_attn[:, None],
            gain_expert[:, None],
            jnp.pad(rel_bias, ((0, rows_here - table_here), (0, 0))),
            jnp.zeros((rows_here, LANES - table_at - HEADS), jnp.bfloat16),
        ],
        axis=1,
    )
    bits = bits_of("shard")
    (first_full, second_full), (first_held, second_held) = gather_rows(
        (
            jnp.concatenate([w_query, w_key, small], axis=1),
            jnp.concatenate([w_value, w_output], axis=1),
        ),
        "shard",
        (bits[1:], bits[:0:-1]),
    )
    qk_full = first_full[:, : 2 * model_width]
    small_full = first_full[:, 2 * model_width :]
    value_full = second_full[:, :model_width]
    output_full = second_full[:, model_width:]
    router_full = small_full[:, :experts]
    gain_one = small_full[:, experts].astype(jnp.float32)
    gain_two = small_full[:, experts + 1].astype(jnp.float32)
    table_full = small_full.reshape(experts, rows_here, LANES)[
        :, :table_here, table_at : table_at + HEADS
    ].reshape(BUCKETS, HEADS)
    router_two = jnp.pad(router_full, ((0, 0), (0, LANES // 2 - experts)))
    router_two = jnp.concatenate([router_two, router_two], axis=1)

    flat_ids = expert_ids.reshape(-1)
    onehot_count = (flat_ids[:, None] == jnp.arange(experts, dtype=jnp.int32)[None, :]).astype(
        jnp.int32
    )
    before = jnp.cumsum(onehot_count, axis=0, dtype=jnp.int32) - onehot_count
    slot_ids = jnp.sum(before * onehot_count, axis=1, dtype=jnp.int32)
    flat_rows = (flat_ids * capacity + slot_ids).reshape(tokens_here, 2)
    def places_of(low, count):
        slots = (
            jnp.arange(experts, dtype=jnp.int32)[:, None] * capacity
            + low
            + jnp.arange(count, dtype=jnp.int32)[None, :]
        ).reshape(-1)
        hit = (slots[:, None] == flat_rows[None, :, 0]) | (slots[:, None] == flat_rows[None, :, 1])
        return hit.astype(jnp.bfloat16)

    places = [places_of(chunk * half, half) for chunk in range(CHUNKS)]
    all_places = places_of(0, capacity)

    id_sum = jnp.sum(expert_ids, axis=1).astype(jnp.float32)
    slot_sums = jnp.dot(all_places.astype(jnp.float32), id_sum).reshape(experts, capacity)
    slot_sums = lax.all_to_all(slot_sums, "shard", split_axis=0, concat_axis=0, tiled=True)
    slot_sums = jnp.broadcast_to(
        slot_sums[:, :, None], (experts, capacity, LANES)
    ).astype(jnp.bfloat16)
    grad_send = pick_rows(all_places, out_grad).reshape(experts, capacity, model_width)
    grad_send, first_held, second_held = lax.optimization_barrier(
        (grad_send, first_held, second_held)
    )
    grad_received = lax.all_to_all(grad_send, "shard", split_axis=0, concat_axis=0, tiled=True)

    inputs_f = inputs.astype(jnp.float32)
    normed = rms_scale(inputs_f, gain_one).astype(jnp.bfloat16)
    qk = jnp.dot(normed, qk_full, preferred_element_type=jnp.float32).astype(jnp.bfloat16)
    value = jnp.dot(normed, value_full, preferred_element_type=jnp.float32).astype(jnp.bfloat16)
    query_lanes, key_lanes = segment_lanes(segment_ids[0], model_width // (HEADS // 2))
    rows = bias_rows(table_full)
    attended, lse = attention_forward(qk, value, query_lanes, key_lanes, rows)
    hidden = inputs_f + jnp.dot(attended, output_full, preferred_element_type=jnp.float32)
    normed_two = rms_scale(hidden, gain_two).astype(jnp.bfloat16)

    normed_two, grad_received = lax.optimization_barrier((normed_two, grad_received))
    weight_in = w_in[0]
    weight_out = w_out[0]
    sent = [
        lax.all_to_all(
            pick_rows(places[k], normed_two).reshape(experts, half, model_width),
            "shard",
            split_axis=0,
            concat_axis=0,
            tiled=True,
        )
        for k in range(CHUNKS)
    ]
    kept = ()
    slopes, logit_lows = [], []
    router_part = jnp.zeros((model_width, LANES), jnp.float32)
    for k in range(CHUNKS):
        *kept, slope, logit_low, part = expert_forward(
            me[None],
            sent[k],
            grad_received,
            slot_sums,
            k,
            weight_in,
            weight_out,
            router_two,
            kept,
        )
        slopes.append(slope)
        logit_lows.append(logit_low)
        router_part = router_part + part
    results, active, gated = kept
    grad_out_part = jnp.einsum(
        "rf,rd->fd", active, gated, preferred_element_type=jnp.float32
    ).astype(jnp.bfloat16)
    out_summed = lax.psum_scatter(grad_out_part, "rep", scatter_dimension=0, tiled=True)
    gated, grad_out_part = lax.optimization_barrier((gated, grad_out_part))
    kept = ()
    returned = []
    for k in range(CHUNKS):
        *kept, back = expert_backward(
            experts,
            gated,
            slopes[k],
            logit_lows[k],
            k,
            weight_in,
            weight_out,
            router_two,
            kept,
        )
        returned.append(
            lax.all_to_all(back, "shard", split_axis=0, concat_axis=0, tiled=True)
        )
    returned[0], grad_pre = lax.optimization_barrier((returned[0], kept[0]))
    rows_in = jnp.concatenate([part.reshape(-1, model_width) for part in sent], axis=0)
    grad_in_part = jnp.einsum(
        "rd,rf->df", rows_in, grad_pre, preferred_element_type=jnp.float32
    ).astype(jnp.bfloat16)
    in_summed = lax.psum_scatter(grad_in_part, "rep", scatter_dimension=1, tiled=True)
    *returned, grad_in_part, results = lax.optimization_barrier(
        (*returned, grad_in_part, results)
    )
    results = lax.all_to_all(results, "shard", split_axis=0, concat_axis=0, tiled=True)

    grad_out = out_grad.astype(jnp.float32)
    grad_normed_two = sum(
        back_rows(places[k], returned[k].reshape(-1, model_width)) for k in range(CHUNKS)
    )
    unused_two, norm_two_pull = jax.vjp(rms_scale, hidden, gain_two)
    grad_hidden_norm, grad_gain_two = norm_two_pull(grad_normed_two)
    grad_hidden = grad_out + grad_hidden_norm
    grad_branch = grad_hidden.astype(jnp.bfloat16)
    grad_wo = weight_grad(attended, grad_branch[None])
    grad_attended = jnp.einsum(
        "te,de->td", grad_branch, output_full, preferred_element_type=jnp.float32
    ).astype(jnp.bfloat16)

    out_summed, grad_attended = lax.optimization_barrier((out_summed, grad_attended))
    grad_qkv, diagonals = attention_backward(
        qk, value, attended, grad_attended, query_lanes, key_lanes, rows, lse
    )
    grad_qkv, results = lax.optimization_barrier((grad_qkv, results))
    grad_table = table_gradient(diagonals)
    grad_normed = jnp.zeros((tokens_here, model_width), jnp.float32)
    for place, weight in enumerate(
        (qk_full[:, :model_width], qk_full[:, model_width:], value_full)
    ):
        grad_normed = grad_normed + jnp.einsum(
            "te,de->td", grad_qkv[place], weight, preferred_element_type=jnp.float32
        )
    unused_one, norm_one_pull = jax.vjp(rms_scale, inputs_f, gain_one)
    grad_inputs_norm, grad_gain_one = norm_one_pull(grad_normed)
    input_grad = (grad_hidden + grad_inputs_norm).astype(jnp.bfloat16)

    grad_router = router_part[:, :experts] + router_part[
        :, LANES // 2 : LANES // 2 + experts
    ]
    table_rows = jnp.pad(
        grad_table.reshape(experts, table_here, HEADS),
        ((0, 0), (0, rows_here - table_here), (0, 0)),
    ).reshape(model_width, HEADS)
    small_grads = jnp.concatenate(
        [
            grad_router,
            grad_gain_one[:, None],
            grad_gain_two[:, None],
            table_rows,
            jnp.zeros((model_width, TILE - table_at - HEADS), jnp.float32),
        ],
        axis=1,
    )
    packed = weight_grad(
        normed,
        grad_qkv,
        jnp.concatenate([grad_wo, small_grads.astype(jnp.bfloat16)], axis=1),
    )
    owned = scatter_sum(packed.reshape(experts, rows_here, packed.shape[1]), "shard")
    owned, in_summed = lax.optimization_barrier((owned, in_summed))
    summed = sum_all(owned, "rep").astype(jnp.float32)
    small_sum = summed[:, 4 * model_width :]

    combined = back_rows(all_places, results.reshape(-1, model_width))
    output = (hidden + combined).astype(jnp.bfloat16)
    return (
        output,
        input_grad,
        summed[:, :model_width],
        summed[:, model_width : 2 * model_width],
        summed[:, 2 * model_width : 3 * model_width],
        summed[:, 3 * model_width : 4 * model_width],
        small_sum[:, :experts],
        small_sum[:, experts],
        small_sum[:, experts + 1],
        small_sum[:table_here, table_at : table_at + HEADS],
        in_summed.astype(jnp.float32)[None],
        out_summed.astype(jnp.float32)[None],
    )


def solution(mesh):
    in_specs = (
        P(("shard", "rep"), None),
        P("shard", None),
        P("shard", None),
        P("shard", None),
        P("shard", None),
        P("shard", None),
        P("shard"),
        P("shard"),
        P("shard", None),
        P("shard", None, None),
        P("shard", None, None),
        P(("shard", "rep"), None),
        P(("shard", "rep"), None),
        P(("shard", "rep"), None),
    )
    out_specs = (
        P(("shard", "rep"), None),
        P(("shard", "rep"), None),
        P("shard", None),
        P("shard", None),
        P("shard", None),
        P("shard", None),
        P("shard", None),
        P("shard"),
        P("shard"),
        P("shard", None),
        P("shard", None, "rep"),
        P("shard", "rep", None),
    )
    return jax.shard_map(body, mesh=mesh, in_specs=in_specs, out_specs=out_specs, check_vma=False)
```

time: 1360 us -> 515 us (0.38)
  waiting for transfers between devices: 471 us -> 98.2 us
  matrix products: 404 us -> 107 us
  local copies, waits for them, and re-layouts: 224 us -> 35.5 us
  Pallas kernels: 0 us -> 170 us
  blocking collectives: 101 us -> 0 us
  other arithmetic: 120 us -> 33.5 us
  starting transfers between devices: 19.7 us -> 48.5 us
    dot_general x35 -> x15, matrix products: 399 us -> 104 us  [the longest x1 21.1 us: body(): jnp.einsum('rf,rd->fd', active, gated, preferred_element_type=jnp.float32)]
    pallas_call x0 -> x9, Pallas kernels: none -> 170 us  [the longest x2 61.4 us: expert_forward(): pl.pallas_call(expert_forward_kernel, grid_spec=pltpu.PrefetchScalarGridS...]
    reduce_scatter x1, waiting for transfers between devices: 165 us -> 0.01 us  [body(): lax.psum_scatter(grad_out_part, 'rep', scatter_dimension=0, tiled=True)]
    reduce_scatter x4 -> x0, waiting for transfers between devices: 128 us -> none  [the longest x1 46.2 us: body(): lax.psum_scatter(partial_grads[3], 'shard', scatter_dimension=0, tiled=True)]
    reduce_scatter x1, waiting for transfers between devices: 92.6 us -> 0.01 us  [body(): lax.psum_scatter(grad_in_part, 'rep', scatter_dimension=1, tiled=True)]
    dot_general x2 -> x0, local copies, waits for them, and re-layouts: 60.8 us -> none  [block_scores(): jnp.einsum('vye,vo->oye', one_hot_matrix, relative_bias_matrix, preferred...]
    convert_element_type x6 -> x0, local copies, waits for them, and re-layouts: 58.1 us -> none  [the longest x2 46.3 us: sequence_backward(): score_gradient = (attn_probs * (grad_probs - row_dot)).astype(jnp.bfloat16)]
    ppermute x0 -> x14, waiting for transfers between devices: none -> 53.9 us  [swap(): lax.ppermute(values, axis, [(place, place ^ bit) for place in range(count)])]
  transfers between devices with their start and end apart: 16 -> 23, of which waited for: 8 -> 12; matrix products, arithmetic and copies ran while one was open for 37% -> 26% of each run, Pallas kernels for 0% -> 28%
where the time goes in v1:
time: 515 us; the launch traced here: 508 us
  Pallas kernels  170 us (33%)
  matrix products  107 us (21%)
  waiting for transfers between devices  98.2 us (19%)
  starting transfers between devices  48.5 us (9%)
  local copies, waits for them, and re-layouts  35.5 us (7%)
  other arithmetic  33.5 us (7%)
  between operations  15.2 us (3%)
    pallas_call x2, Pallas kernels, expert_forward(): pl.pallas_call(expert_forward_kernel, grid_spec=pltpu.PrefetchScalarGridS...  61.4 us
    ppermute x14, waiting for transfers between devices, swap(): lax.ppermute(values, axis, [(place, place ^ bit) for place in range(count)])  53.9 us
    pallas_call x2, Pallas kernels, expert_backward(): pl.pallas_call(expert_backward_kernel, grid=(experts // group,), in_specs...  44.7 us
    pallas_call x1, Pallas kernels, attention_backward(): pl.pallas_call(backward_kernel, grid=(pairs,), in_specs=[block, pl.BlockS...  29.8 us
    all_to_all x2, waiting for transfers between devices, body(): lax.all_to_all(pick_rows(places[k], normed_two).reshape(experts, half, mo...  23.8 us
    pallas_call x1, Pallas kernels, attention_forward(): pl.pallas_call(forward_kernel, grid=(pairs,), in_specs=[pl.BlockSpec((len...  22.5 us
    dot_general x1, matrix products, body(): jnp.einsum('rf,rd->fd', active, gated, preferred_element_type=jnp.float32)  21.1 us
    dot_general x1, matrix products, body(): jnp.einsum('rd,rf->df', rows_in, grad_pre, preferred_element_type=jnp.flo...  20.8 us
  transfers between devices with their start and end apart: 23, of which 12 were waited for; matrix products, arithmetic and copies ran while one was open for 26% of the time, Pallas kernels for 28%

profile of v1, /device:TPU:0, one launch (start us, length us, event | category | flops | bytes accessed | tf_op | source)
XLA Modules:
  0.0 508.0 jit_solution(17241626658995792310)
XLA Ops:
  22.2 9.0 %fusion.13 = bf16[3072,768]{1,0:T(8,128)(2,1)} fusion(bf16[1024,768]{1,0:T(8,128)(2,1)} %param.29, s32[1024]{0:T(1024)S(1)} %bitcast.162, s32[1024]{0:T(1024)S(1)} %bitcast.155, s32[3072]{0:T(1024)S(1)} %add.508), kind=kOutput, calls=%fused_computation.24 | convolution fusion | flops 4843634688 | bytes 6311936 | tf_op jit(solution)/shard_map/dot_general | solution.py:601
  34.8 11.0 %collective-permute-done.4 = bf16[2,96,1536]{2,1,0:T(8,128)(2,1)S(1)} collective-permute-done((bf16[2,96,1536]{2,1,0:T(8,128)(2,1)S(1)}, bf16[2,96,1536]{2,1,0:T(8,128)(2,1)S(1)}, u32[]{:S(2)}, u32[]{:S(2)}) %collective-permute-start.4) | collective-permute-done | bytes 589856 | tf_op jit(solution)/shard_map/ppermute | solution.py:441
  47.5 4.8 all-to-all-start
  76.4 22.5 %attention_forward.1 = (bf16[1024,768]{1,0:T(8,128)(2,1)S(1)}, f32[1024,128]{1,0:T(8,128)S(1)}) custom-call(bf16[1024,1536]{1,0:T(8,128)(2,1)S(1)} %convolution_convert_fusion.2.q_ref.k_ref, bf16[1024,1536]{1,0:T(8,128)(2,1)S(1)} %convolution_convert_fusion.2.q_ref.k_ref, bf16[1024,768]{1,0:T(8,128)(2,1)S(1)} %copy-done.6, ...), custom_call_target="tpu_custom_call" | custom-call | flops 1024 | bytes 1024 | tf_op jit(solution)/shard_map/attention_forward/pallas_call | solution.py:123
  102.3 4.8 all-to-all-done.g_ref
  110.4 5.5 %fusion.23 = bf16[1536,768]{1,0:T(8,128)(2,1)} fusion(bf16[1024,768]{1,0:T(8,128)(2,1)} %multiply_convert_fusion, s32[1024]{0:T(1024)S(1)} %bitcast.164, s32[1024]{0:T(1024)S(1)} %bitcast.157, s32[1536]{0:T(1024)S(1)} %add.519), kind=kOutput, calls=%fused_computation.39 | convolution fusion | flops 2421817344 | bytes 3946496 | tf_op jit(solution)/shard_map/dot_general | solution.py:601
  116.0 4.8 all-to-all-start.3
  120.9 5.5 %fusion.24 = bf16[1536,768]{1,0:T(8,128)(2,1)} fusion(bf16[1024,768]{1,0:T(8,128)(2,1)} %multiply_convert_fusion, s32[1024]{0:T(1024)S(1)} %bitcast.165, s32[1024]{0:T(1024)S(1)} %bitcast.158, s32[1536]{0:T(1024)S(1)} %add.514), kind=kOutput, calls=%fused_computation.40 | convolution fusion | flops 2421817344 | bytes 3946496 | tf_op jit(solution)/shard_map/dot_general | solution.py:601
  126.5 23.8 %all-to-all-done.3.x_ref = bf16[8,192,768]{2,1,0:T(8,128)(2,1)} async-done(((bf16[8,192,768]{2,1,0:T(8,128)(2,1)}), bf16[8,192,768]{2,1,0:T(8,128)(2,1)}, u32[]{:S(2)}, u32[]{:S(2)}) %all-to-all-start.3) | async-done | bytes 2359328 | tf_op jit(solution)/shard_map/all_to_all | solution.py:710
  150.2 4.4 all-to-all-start.1
  157.9 30.8 %expert_forward.2 = (bf16[8,384,768]{2,1,0:T(8,128)(2,1)}, bf16[3072,3072]{1,0:T(8,128)(2,1)}, bf16[3072,768]{1,0:T(8,128)(2,1)}, bf16[1536,3072]{1,0:T(8,128)(2...) custom-call(s32[1]{0:T(128)} %bitcast.15.me_ref, bf16[8,192,768]{2,1,0:T(8,128)(2,1)} %all-to-all-done.3.x_ref, ...), custom_call_target="tpu_custom_call" | custom-call | flops 14495514624 | bytes 37748736 | tf_op jit(solution)/shard_map/expert_forward/pallas_call | solution.py:360
  188.7 30.7 %expert_forward.3 = (bf16[8,384,768]{2,1,0:T(8,128)(2,1)}, bf16[3072,3072]{1,0:T(8,128)(2,1)}, bf16[3072,768]{1,0:T(8,128)(2,1)}, bf16[1536,3072]{1,0:T(8,128)(2...) custom-call(s32[1]{0:T(128)} %bitcast.15.me_ref, ...), custom_call_target="tpu_custom_call", output_to_operand_aliasing={{0}: (7, {}), {1}: (8, {}), {2}: (9, {})} | custom-call | flops 14495514624 | bytes 37748736 | tf_op jit(solution)/shard_map/expert_forward/pallas_call | solution.py:360
  219.4 21.1 %convolution_convert_fusion = bf16[3072,768]{1,0:T(8,128)(2,1)} fusion(bf16[3072,3072]{1,0:T(8,128)(2,1)} %get-tuple-element.58, bf16[3072,768]{1,0:T(8,128)(2,1)} %get-tuple-element.60.gated_ref), kind=kOutput, calls=%fused_computation.25 | convolution fusion | flops 14497873920 | bytes 28311552 | tf_op jit(solution)/shard_map/rf,rd->fd/dot_general | solution.py:738
  240.5 22.3 %expert_backward.2 = (bf16[3072,3072]{1,0:T(8,128)(2,1)}, bf16[8,192,768]{2,1,0:T(8,128)(2,1)}) custom-call(bf16[3072,768]{1,0:T(8,128)(2,1)} %get-tuple-element.60.gated_ref, bf16[1536,3072]{1,0:T(8,128)(2,1)} %get-tuple-element.61.slope_ref, bf16[1536,128]{1,0:T(8,128)(2,1)} %get-tuple-element.62.logit_ref, bf16[768,3072]{1,0:T(8,128)(2,1)} %bitcast.131, ...), custom_call_target="tpu_custom_call" | custom-call | flops 1024 | bytes 1024 | tf_op jit(solution)/shard_map/expert_backward/pallas_call | solution.py:416
  267.1 22.4 %expert_backward.3 = (bf16[3072,3072]{1,0:T(8,128)(2,1)}, bf16[8,192,768]{2,1,0:T(8,128)(2,1)}) custom-call(bf16[3072,768]{1,0:T(8,128)(2,1)} %get-tuple-element.60.gated_ref, bf16[1536,3072]{1,0:T(8,128)(2,1)} %get-tuple-element.64.slope_ref, bf16[1536,128]{1,0:T(8,128)(2,1)} %get-tuple-element.65.logit_ref, ...), custom_call_target="tpu_custom_call", output_to_operand_aliasing={{0}: (6, {})} | custom-call | flops 1024 | bytes 1024 | tf_op jit(solution)/shard_map/expert_backward/pallas_call | solution.py:416
  289.6 7.0 %all-to-all-done.4 = bf16[8,192,768]{2,1,0:T(8,128)(2,1)} async-done(((bf16[8,192,768]{2,1,0:T(8,128)(2,1)}), bf16[8,192,768]{2,1,0:T(8,128)(2,1)}, u32[]{:S(2)}, u32[]{:S(2)}) %all-to-all-start.4) | async-done | bytes 2359328 | tf_op jit(solution)/shard_map/all_to_all | solution.py:758
  296.6 4.6 all-to-all-start.5
  301.2 20.8 %convolution_convert_fusion.1 = bf16[768,3072]{1,0:T(8,128)(2,1)} fusion(bf16[3072,3072]{1,0:T(8,128)(2,1)} %get-tuple-element.70, bf16[1536,768]{1,0:T(8,128)(2,1)} %bitcast.26, bf16[1536,768]{1,0:T(8,128)(2,1)} %bitcast.25), kind=kOutput, calls=%fused_computation.26 | convolution fusion | flops 14507311104 | bytes 28311552 | tf_op jit(solution)/shard_map/rd,rf->df/dot_general | solution.py:762
  322.0 8.6 %all-to-all-done.5 = bf16[8,192,768]{2,1,0:T(8,128)(2,1)} async-done(((bf16[8,192,768]{2,1,0:T(8,128)(2,1)}), bf16[8,192,768]{2,1,0:T(8,128)(2,1)}, u32[]{:S(2)}, u32[]{:S(2)}) %all-to-all-start.5) | async-done | bytes 2359328 | tf_op jit(solution)/shard_map/all_to_all | solution.py:758
  330.7 4.6 all-to-all-start.6
  337.4 5.0 fusion.14
  342.4 5.9 %multiply_reduce_fusion = (bf16[768]{0:T(1024)(128)(2,1)S(1)}, f32[1024]{0:T(1024)S(1)}, f32[1024,768]{1,0:T(8,128)S(1)}) fusion(f32[1024,768]{1,0:T(8,128)S(1)} %get-tuple-element.205, f32[1024]{0:T(1024)S(1)} %fusion.93, f32[768]{0:T(1024)S(1)} %get-tuple-element.186, f32[1024,768]{1,0:T(8,128)S(1)} %fusion.14, bf16[1536,768]{1,0:T(8,128)(2,1)} %bitcast.27, ...), kind=kOutput, calls=%fused_computation.48 | convolution fusion | flops 2426140928 | bytes 11823616 | tf_op jit(solution)/shard_map/st,sd->td/dot_general | solution.py:605
  348.3 4.6 convert_bitcast_fusion
  357.6 4.9 convolution_convert_fusion.3.g_ref
  366.1 29.8 %attention_backward.1 = (bf16[3,1024,768]{2,1,0:T(8,128)(2,1)}, f32[6,2,1024]{2,1,0:T(2,128)S(1)}) custom-call(bf16[1024,1536]{1,0:T(8,128)(2,1)} %copy-done, bf16[1024,1536]{1,0:T(8,128)(2,1)} %copy-done, bf16[1024,768]{1,0:T(8,128)(2,1)S(1)} %copy-done.7, bf16[1024,768]{1,0:T(8,128)(2,1)S(1)} %copy-done.9, bf16[1024,768]{1,0:T(8,128)(2,1)S(1)} %copy-done.13, ...), custom_call_target="tpu_custom_call" | custom-call | flops 1024 | bytes 1024 | tf_op jit(solution)/shard_map/attention_backward/pallas_call | solution.py:234
  412.7 7.4 %weight_grad.3 = bf16[768,3328]{1,0:T(8,128)(2,1)S(1)} custom-call(bf16[1024,768]{1,0:T(8,128)(2,1)S(1)} %copy-done.5, bf16[3,1024,768]{2,1,0:T(8,128)(2,1)S(1)} %copy-done.3, bf16[768,1024]{1,0:T(8,128)(2,1)S(1)} %concatenate.50.refs_0_), custom_call_target="tpu_custom_call" | custom-call | flops 1024 | bytes 1024 | tf_op jit(solution)/shard_map/weight_grad/pallas_call | solution.py:580
  423.5 4.7 collective-permute-done.6
  434.3 13.2 %collective-permute-done.7 = bf16[2,96,1664]{2,1,0:T(8,128)(2,1)} collective-permute-done((bf16[2,96,1664]{2,1,0:T(8,128)(2,1)S(1)}, bf16[2,96,1664]{2,1,0:T(8,128)(2,1)}, u32[]{:S(2)}, u32[]{:S(2)}) %collective-permute-start.7) | collective-permute-done | bytes 639008 | tf_op jit(solution)/shard_map/ppermute | solution.py:441
  452.4 5.4 %collective-permute-done.8 = bf16[96,1664]{1,0:T(8,128)(2,1)S(1)} collective-permute-done((bf16[96,1664]{1,0:T(8,128)(2,1)S(1)}, bf16[96,1664]{1,0:T(8,128)(2,1)S(1)}, u32[]{:S(2)}, u32[]{:S(2)}) %collective-permute-start.8) | collective-permute-done | bytes 319520 | tf_op jit(solution)/shard_map/ppermute | solution.py:441
  463.4 9.6 %add_convert_fusion = bf16[1024,768]{1,0:T(8,128)(2,1)} fusion(f32[1024,768]{1,0:T(8,128)S(1)} %copy-done.29, bf16[3072,768]{1,0:T(8,128)(2,1)} %bitcast.29, s32[1024]{0:T(1024)S(1)} %bitcast.168, s32[1024]{0:T(1024)S(1)} %bitcast.161, s32[3072]{0:T(1024)S(1)} %copy-done.43), kind=kOutput, calls=%fused_computation.50 | convolution fusion | flops 4842848256 | bytes 9457664 | tf_op jit(solution)/shard_map/st,sd->td/dot_general | solution.py:605
  477.7 10.4 %collective-permute-done.12 = bf16[48,3328]{1,0:T(8,128)(2,1)S(1)} collective-permute-done((bf16[48,3328]{1,0:T(8,128)(2,1)S(1)}, bf16[48,3328]{1,0:T(8,128)(2,1)S(1)}, u32[]{:S(2)}, u32[]{:S(2)}) %collective-permute-start.12) | collective-permute-done | bytes 319520 | tf_op jit(solution)/shard_map/ppermute | solution.py:441
  491.5 6.3 %collective-permute-done.13 = bf16[48,3328]{1,0:T(8,128)(2,1)S(1)} collective-permute-done((bf16[48,3328]{1,0:T(8,128)(2,1)S(1)}, bf16[48,3328]{1,0:T(8,128)(2,1)S(1)}, u32[]{:S(2)}, u32[]{:S(2)}) %collective-permute-start.13) | collective-permute-done | bytes 319520 | tf_op jit(solution)/shard_map/ppermute | solution.py:441
  (240 shorter events, 116.5 us)
Async XLA Ops:
  7.2 14.8 %copy-start.40 = (s32[1024,2]{0,1:T(2,128)S(1)}, s32[1024,2]{0,1:T(2,128)}, u32[]{:S(2)}) copy-start(s32[1024,2]{0,1:T(2,128)} %param.28) | copy-start | bytes 24580
  8.2 23.0 %collective-permute-start.3 = (bf16[1,96,1536]{2,1,0:T(8,128)(2,1)S(1)}, bf16[1,96,1536]{2,1,0:T(8,128)(2,1)S(1)}, u32[]{:S(2)}, u32[]{:S(2)}) collective-permute-start(bf16[1,96,1536]{2,1,0:T(8,128)(2,1)S(1)} %maximum_bitcast_fusion), channel_id=1, source_target_pairs={{0,16},{4,20},{8,24},{12,28},{16,0},{20,4},{24,8},{28,12},{1,17},{... | collective-permute-start | bytes 884744 | tf_op jit(solution)/shard_map/ppermute | solution.py:441
  15.4 16.5 %collective-permute-start = (bf16[1,96,1664]{2,1,0:T(8,128)(2,1)S(1)}, bf16[1,96,1664]{2,1,0:T(8,128)(2,1)S(1)}, u32[]{:S(2)}, u32[]{:S(2)}) collective-permute-start(bf16[1,96,1664]{2,1,0:T(8,128)(2,1)S(1)} %bitcast.138), channel_id=1, source_target_pairs={{0,8},{4,12},{8,0},{12,4},{16,24},{20,28},{24,16},{28,20},{1,9},{5... | collective-permute-start | bytes 958472 | tf_op jit(solution)/shard_map/ppermute | solution.py:441
  22.1 320.3 %copy-start.44 = (s32[1024,1]{0,1:T(1,128)}, s32[1024,1]{0,1:T(1,128)S(1)}, u32[]{:S(2)}) copy-start(s32[1024,1]{0,1:T(1,128)S(1)} %get-tuple-element.203) | copy-start | bytes 12292
  31.3 14.6 %collective-permute-start.4 = (bf16[2,96,1536]{2,1,0:T(8,128)(2,1)S(1)}, bf16[2,96,1536]{2,1,0:T(8,128)(2,1)S(1)}, u32[]{:S(2)}, u32[]{:S(2)}) collective-permute-start(bf16[2,96,1536]{2,1,0:T(8,128)(2,1)S(1)} %pad_maximum_fusion.4), channel_id=1, source_target_pairs={{0,8},{4,12},{8,0},{12,4},{16,24},{20,28},{24,16},{28,20},{1,9},{5... | collective-permute-start | bytes 1769480 | tf_op jit(solution)/shard_map/ppermute | solution.py:441
  32.0 15.3 %collective-permute-start.1 = (bf16[2,96,1664]{2,1,0:T(8,128)(2,1)S(1)}, bf16[2,96,1664]{2,1,0:T(8,128)(2,1)S(1)}, u32[]{:S(2)}, u32[]{:S(2)}) collective-permute-start(bf16[2,96,1664]{2,1,0:T(8,128)(2,1)S(1)} %pad_maximum_fusion.2), channel_id=1, source_target_pairs={{0,16},{4,20},{8,24},{12,28},{16,0},{20,4},{24,8},{28,12},{1,17},{... | collective-permute-start | bytes 1916936 | tf_op jit(solution)/shard_map/ppermute | solution.py:441
  47.5 59.6 %all-to-all-start = ((bf16[8,384,768]{2,1,0:T(8,128)(2,1)}), bf16[8,384,768]{2,1,0:T(8,128)(2,1)}, u32[]{:S(2)}, u32[]{:S(2)}) async-start(bf16[8,384,768]{2,1,0:T(8,128)(2,1)} %bitcast.137), calls=%async_computation | async-start | bytes 9437184 | tf_op jit(solution)/shard_map/all_to_all | solution.py:694
  52.4 6.8 %collective-permute-start.2 = (bf16[4,96,1664]{2,1,0:T(8,128)(2,1)S(1)}, bf16[4,96,1664]{2,1,0:T(8,128)(2,1)}, u32[]{:S(2)}, u32[]{:S(2)}) collective-permute-start(bf16[4,96,1664]{2,1,0:T(8,128)(2,1)S(1)} %pad_maximum_fusion.refs_0_), channel_id=1, source_target_pairs={{0,4},{4,0},{8,12},{12,8},{16,20},{20,16},{24,28},{28,24},{1,5},{5... | collective-permute-start | bytes 3833864 | tf_op jit(solution)/shard_map/ppermute | solution.py:441
  55.4 3.8 collective-permute-start.5
  72.9 26.0 %copy-start = (bf16[1024,1536]{1,0:T(8,128)(2,1)}, bf16[1024,1536]{1,0:T(8,128)(2,1)S(1)}, u32[]{:S(2)}) copy-start(bf16[1024,1536]{1,0:T(8,128)(2,1)S(1)} %convolution_convert_fusion.2.q_ref.k_ref) | copy-start | bytes 9437188
  76.4 22.6 %copy-start.16 = (bf16[4,2,96,1536]{3,2,1,0:T(8,128)(2,1)S(1)}, bf16[4,2,96,1536]{3,2,1,0:T(8,128)(2,1)}, u32[]{:S(2)}) copy-start(bf16[4,2,96,1536]{3,2,1,0:T(8,128)(2,1)} %copy-done.14) | copy-start | bytes 7077892
  76.4 22.6 %copy-start.23 = (bf16[1024,768]{1,0:T(8,128)(2,1)S(1)}, bf16[1024,768]{1,0:T(8,128)(2,1)}, u32[]{:S(2)}) copy-start(bf16[1024,768]{1,0:T(8,128)(2,1)} %param.16) | copy-start | bytes 4718596
  100.5 241.9 %copy-start.28 = (f32[1024,768]{1,0:T(8,128)}, f32[1024,768]{1,0:T(8,128)S(1)}, u32[]{:S(2)}) copy-start(f32[1024,768]{1,0:T(8,128)S(1)} %get-tuple-element.205) | copy-start | bytes 9437188
  107.1 8.9 %all-to-all-start.2 = ((bf16[8,2,192]{2,1,0:T(2,128)(2,1)}), bf16[8,2,192]{2,1,0:T(2,128)(2,1)S(1)}, u32[]{:S(2)}, u32[]{:S(2)}) async-start(bf16[8,2,192]{2,1,0:T(2,128)(2,1)} %reshape.488), calls=%async_computation.2 | async-start | bytes 16384 | tf_op jit(solution)/shard_map/all_to_all | solution.py:686
  116.0 34.3 %all-to-all-start.3 = ((bf16[8,192,768]{2,1,0:T(8,128)(2,1)}), bf16[8,192,768]{2,1,0:T(8,128)(2,1)}, u32[]{:S(2)}, u32[]{:S(2)}) async-start(bf16[8,192,768]{2,1,0:T(8,128)(2,1)} %bitcast.142), calls=%async_computation.3 | async-start | bytes 4718592 | tf_op jit(solution)/shard_map/all_to_all | solution.py:710
  150.2 38.5 %all-to-all-start.1 = ((bf16[8,192,768]{2,1,0:T(8,128)(2,1)}), bf16[8,192,768]{2,1,0:T(8,128)(2,1)}, u32[]{:S(2)}, u32[]{:S(2)}) async-start(bf16[8,192,768]{2,1,0:T(8,128)(2,1)} %bitcast.141), calls=%async_computation.1 | async-start | bytes 4718592 | tf_op jit(solution)/shard_map/all_to_all | solution.py:710
  154.6 207.9 %reduce-scatter.3.cloned.1.call-start = ((), (), s32[]{:S(2)}) async-start(), calls=%async_computation.9 | async-start | bytes 5898240 | tf_op jit(solution)/shard_map/reduce_scatter | solution.py:741
  262.8 33.8 %all-to-all-start.4 = ((bf16[8,192,768]{2,1,0:T(8,128)(2,1)}), bf16[8,192,768]{2,1,0:T(8,128)(2,1)}, u32[]{:S(2)}, u32[]{:S(2)}) async-start(bf16[8,192,768]{2,1,0:T(8,128)(2,1)} %get-tuple-element.63), calls=%async_computation.5 | async-start | bytes 4718592 | tf_op jit(solution)/shard_map/all_to_all | solution.py:758
  296.6 34.1 %all-to-all-start.5 = ((bf16[8,192,768]{2,1,0:T(8,128)(2,1)}), bf16[8,192,768]{2,1,0:T(8,128)(2,1)}, u32[]{:S(2)}, u32[]{:S(2)}) async-start(bf16[8,192,768]{2,1,0:T(8,128)(2,1)} %get-tuple-element.69), calls=%async_computation.6 | async-start | bytes 4718592 | tf_op jit(solution)/shard_map/all_to_all | solution.py:758
  330.7 65.2 %all-to-all-start.6 = ((bf16[8,384,768]{2,1,0:T(8,128)(2,1)}), bf16[8,384,768]{2,1,0:T(8,128)(2,1)}, u32[]{:S(2)}, u32[]{:S(2)}) async-start(bf16[8,384,768]{2,1,0:T(8,128)(2,1)} %get-tuple-element.77), calls=%async_computation.7 | async-start | bytes 9437184 | tf_op jit(solution)/shard_map/all_to_all | solution.py:769
  335.3 125.1 %reduce-scatter.5.cloned.1.call-start = ((), (), s32[]{:S(2)}) async-start(), calls=%async_computation.10 | async-start | bytes 5898240 | tf_op jit(solution)/shard_map/reduce_scatter | solution.py:765
  423.2 5.0 collective-permute-start.6
  430.8 16.8 %collective-permute-start.7 = (bf16[2,96,1664]{2,1,0:T(8,128)(2,1)S(1)}, bf16[2,96,1664]{2,1,0:T(8,128)(2,1)}, u32[]{:S(2)}, u32[]{:S(2)}) collective-permute-start(bf16[2,96,1664]{2,1,0:T(8,128)(2,1)S(1)} %dynamic-slice_bitcast_fusion.2), channel_id=1, source_target_pairs={{0,8},{4,12},{8,0},{12,4},{16,24},{20,28},{24,16},{28,20},{1,9},{5... | collective-permute-start | bytes 1916936 | tf_op jit(solution)/shard_map/ppermute | solution.py:441
  432.8 17.9 %collective-permute-start.9 = (bf16[2,96,1664]{2,1,0:T(8,128)(2,1)S(1)}, bf16[2,96,1664]{2,1,0:T(8,128)(2,1)S(1)}, u32[]{:S(2)}, u32[]{:S(2)}) collective-permute-start(bf16[2,96,1664]{2,1,0:T(8,128)(2,1)S(1)} %dynamic-slice_bitcast_fusion.1), channel_id=1, source_target_pairs={{0,16},{4,20},{8,24},{12,28},{16,0},{20,4},{24,8},{28,12},{1,17},{... | collective-permute-start | bytes 1916936 | tf_op jit(solution)/shard_map/ppermute | solution.py:441
  448.9 9.0 %collective-permute-start.8 = (bf16[96,1664]{1,0:T(8,128)(2,1)S(1)}, bf16[96,1664]{1,0:T(8,128)(2,1)S(1)}, u32[]{:S(2)}, u32[]{:S(2)}) collective-permute-start(bf16[96,1664]{1,0:T(8,128)(2,1)S(1)} %dynamic-slice_bitcast_fusion.4), channel_id=1, source_target_pairs={{0,16},{4,20},{8,24},{12,28},{16,0},{20,4},{24,8},{28,12},{1,17},{... | collective-permute-start | bytes 958472 | tf_op jit(solution)/shard_map/ppermute | solution.py:441
  450.8 12.5 %copy-start.29 = (f32[1024,768]{1,0:T(8,128)S(1)}, f32[1024,768]{1,0:T(8,128)}, u32[]{:S(2)}) copy-start(f32[1024,768]{1,0:T(8,128)} %copy-done.28) | copy-start | bytes 9437188
  450.8 12.5 %copy-start.43 = (s32[3072]{0:T(1024)S(1)}, s32[3072]{0:T(1024)}, u32[]{:S(2)}) copy-start(s32[3072]{0:T(1024)} %copy-done.42) | copy-start | bytes 36868
  450.9 8.6 %collective-permute-start.10 = (bf16[96,1664]{1,0:T(8,128)(2,1)S(1)}, bf16[96,1664]{1,0:T(8,128)(2,1)S(1)}, u32[]{:S(2)}, u32[]{:S(2)}) collective-permute-start(bf16[96,1664]{1,0:T(8,128)(2,1)S(1)} %dynamic-slice_bitcast_fusion.3), channel_id=1, source_target_pairs={{0,8},{4,12},{8,0},{12,4},{16,24},{20,28},{24,16},{28,20},{1,9},{5... | collective-permute-start | bytes 958472 | tf_op jit(solution)/shard_map/ppermute | solution.py:441
  461.5 11.5 %collective-permute-start.11 = (bf16[48,3328]{1,0:T(8,128)(2,1)S(1)}, bf16[48,3328]{1,0:T(8,128)(2,1)S(1)}, u32[]{:S(2)}, u32[]{:S(2)}) collective-permute-start(bf16[48,3328]{1,0:T(8,128)(2,1)S(1)} %broadcast_select_fusion.2), channel_id=1, source_target_pairs={{0,1},{1,0},{2,3},{3,2},{4,5},{5,4},{6,7},{7,6},{8,9},{9,8},{10,11... | collective-permute-start | bytes 958472 | tf_op jit(solution)/shard_map/ppermute | solution.py:441
  473.2 15.0 %collective-permute-start.12 = (bf16[48,3328]{1,0:T(8,128)(2,1)S(1)}, bf16[48,3328]{1,0:T(8,128)(2,1)S(1)}, u32[]{:S(2)}, u32[]{:S(2)}) collective-permute-start(bf16[48,3328]{1,0:T(8,128)(2,1)S(1)} %add_convert_fusion.2), channel_id=1, source_target_pairs={{0,2},{1,3},{2,0},{3,1},{4,6},{5,7},{6,4},{7,5},{8,10},{9,11},{10,... | collective-permute-start | bytes 958472 | tf_op jit(solution)/shard_map/ppermute | solution.py:441
  475.7 12.6 %copy-start.32 = (bf16[768,768]{1,0:T(8,128)(2,1)S(1)}, bf16[768,768]{1,0:T(8,128)(2,1)}, u32[]{:S(2)}) copy-start(bf16[768,768]{1,0:T(8,128)(2,1)} %reduce-scatter.3.cloned.1.call-done) | copy-start | bytes 3538948
  488.2 9.5 %collective-permute-start.13 = (bf16[48,3328]{1,0:T(8,128)(2,1)S(1)}, bf16[48,3328]{1,0:T(8,128)(2,1)S(1)}, u32[]{:S(2)}, u32[]{:S(2)}) collective-permute-start(bf16[48,3328]{1,0:T(8,128)(2,1)S(1)} %add_convert_fusion.1), channel_id=1, source_target_pairs={{0,1},{1,0},{2,3},{3,2},{4,5},{5,4},{6,7},{7,6},{8,9},{9,8},{10,11... | collective-permute-start | bytes 958472 | tf_op jit(solution)/shard_map/ppermute | solution.py:441
  (37 other events, 176.8 us)
Sparse Core Ops, SparseCore 0:
  240.6 86.8 reduce-scatter.2
  357.7 86.8 reduce-scatter.4

commit v2 on v1

--- a/solution.py
+++ b/solution.py
@@ -82,6 +82,7 @@
     pair = pl.program_id(0)
     length, width = q_ref.shape
     half = width // 2
+    window = LONGEST + QB
     lane = lax.broadcasted_iota(jnp.int32, (QB, width), 1)
     lane_k = lax.broadcasted_iota(jnp.int32, (length, width), 1)
 
@@ -93,26 +94,32 @@
     keys = [
         jnp.where((lane_k < half) == (h == 0), k_ref[...], kl_ref[...]) for h in range(2)
     ]
-    for start in range(0, length, QB):
+    units = [(start, h) for start in range(0, length, QB) for h in range(2)]
+
+    def scores(start, h):
         low = max(0, start - LONGEST)
+        q = (q_ref[start : start + QB, :].astype(jnp.float32) * (half**-0.5)).astype(jnp.bfloat16)
+        q_own = jnp.where((lane < half) == (h == 0), q, ql_ref[start : start + QB, :])
         wide = start + QB - low
-        q = (q_ref[start : start + QB, :].astype(jnp.float32) * (half**-0.5)).astype(jnp.bfloat16)
-        outs = []
-        lse = lse_ref[start : start + QB, :]
-        for h in range(2):
-            mine = (lane < half) == (h == 0)
-            q_own = jnp.where(mine, q, ql_ref[start : start + QB, :])
-            s = nt(q_own, keys[h][low : start + QB, :]) + biases[h][:, LONGEST + QB - wide :]
-            peak = jnp.max(s, axis=1, keepdims=True)
-            p = jnp.exp(s - peak)
-            total = jnp.sum(p, axis=1, keepdims=True)
-            o = nn(p.astype(jnp.bfloat16), v_ref[low : start + QB, :])
-            outs.append(o * (1.0 / total))
-            lse = jnp.where(lane == 2 * pair + h, peak + jnp.log(total), lse)
-        lse_ref[start : start + QB, :] = lse
-        out_ref[start : start + QB, :] = jnp.where(lane < half, outs[0], outs[1]).astype(
-            jnp.bfloat16
-        )
+        return nt(q_own, keys[h][low : start + QB, :]) + biases[h][:, window - wide :]
+
+    ahead = scores(*units[0])
+    kept = None
+    for place, (start, h) in enumerate(units):
+        s = ahead
+        if place + 1 < len(units):
+            ahead = scores(*units[place + 1])
+        stop = start + QB
+        low = max(0, start - LONGEST)
+        peak = jnp.max(s, axis=1, keepdims=True)
+        p = jnp.exp(s - peak)
+        total = jnp.sum(p, axis=1, keepdims=True)
+        o = nn(p.astype(jnp.bfloat16), v_ref[low:stop, :]) * (1.0 / total)
+        lse_ref[start:stop, :] += jnp.where(lane == 2 * pair + h, peak + jnp.log(total), 0.0)
+        if h == 0:
+            kept = o
+        else:
+            out_ref[start:stop, :] = jnp.where(lane < half, kept, o).astype(jnp.bfloat16)
 
 
 def attention_forward(qk, v, query_lanes, key_lanes, rows):
@@ -182,33 +189,46 @@
     keys = [jnp.where(owned_k[h], k_ref[...], kl_ref[...]) for h in range(2)]
     bare_keys = [jnp.where(owned_k[h], k_ref[...], zero) for h in range(2)]
     values = [jnp.where(owned_k[h], v_ref[...], kl_ref[...]) for h in range(2)]
-    for start in range(0, length, QB):
+    units = [(start, h) for start in range(0, length, QB) for h in range(2)]
+
+    def products(start, h):
         low = max(0, start - LONGEST)
-        wide = start + QB - low
         stop = start + QB
+        wide = stop - low
         q = (q_ref[start:stop, :].astype(jnp.float32) * (half**-0.5)).astype(jnp.bfloat16)
         g = g_ref[start:stop, :]
         dot_all = g.astype(jnp.float32) * o_ref[start:stop, :].astype(jnp.float32)
         lse_all = lse_ref[start:stop, :]
         q_lanes = ql_ref[start:stop, :].astype(jnp.float32)
-        turned = None
-        for h in range(2):
-            mine = (lane < half) == (h == 0)
-            lse = jnp.sum(jnp.where(lane == 2 * pair + h, lse_all, 0.0), axis=1, keepdims=True)
-            dot = jnp.sum(jnp.where(mine, dot_all, 0.0), axis=1, keepdims=True)
-            q_own = jnp.where(mine, q, with_column(lane, half, q_lanes, -lse))
-            g_own = jnp.where(mine, g, with_column(lane, half, jnp.zeros_like(q_lanes), -dot))
-            s = nt(keys[h][low:stop, :], q_own) + biases[h][window - wide :, :]
-            p = jnp.exp(s)
-            dp = nt(values[h][low:stop, :], g_own)
-            ds = p * dp
-            diag_acc[h, window - wide :, :] += ds
-            ds_low = ds.astype(jnp.bfloat16)
-            dv_acc[low:stop, :] += nn(p.astype(jnp.bfloat16), jnp.where(mine, g, zero))
-            dk_acc[low:stop, :] += nn(ds_low, jnp.where(mine, q, zero))
-            part = tn(bare_keys[h][low:stop, :], ds_low)
-            turned = part if turned is None else turned + part
-        grad_ref[0, start:stop, :] = (turned * (half**-0.5)).T.astype(jnp.bfloat16)
+        mine = (lane < half) == (h == 0)
+        lse = jnp.sum(jnp.where(lane == 2 * pair + h, lse_all, 0.0), axis=1, keepdims=True)
+        dot = jnp.sum(jnp.where(mine, dot_all, 0.0), axis=1, keepdims=True)
+        q_own = jnp.where(mine, q, with_column(lane, half, q_lanes, -lse))
+        g_own = jnp.where(mine, g, with_column(lane, half, jnp.zeros_like(q_lanes), -dot))
+        s = nt(keys[h][low:stop, :], q_own) + biases[h][window - wide :, :]
+        dp = nt(values[h][low:stop, :], g_own)
+        return s, dp, jnp.where(mine, q, zero), jnp.where(mine, g, zero)
+
+    ahead = products(*units[0])
+    turned = None
+    for place, (start, h) in enumerate(units):
+        low = max(0, start - LONGEST)
+        stop = start + QB
+        wide = stop - low
+        s, dp, q_bare, g_bare = ahead
+        if place + 1 < len(units):
+            ahead = products(*units[place + 1])
+        p = jnp.exp(s)
+        ds = p * dp
+        diag_acc[h, window - wide :, :] += ds
+        ds_low = ds.astype(jnp.bfloat16)
+        dv_acc[low:stop, :] += nn(p.astype(jnp.bfloat16), g_bare)
+        dk_acc[low:stop, :] += nn(ds_low, q_bare)
+        part = tn(bare_keys[h][low:stop, :], ds_low)
+        if h == 0:
+            turned = part
+        else:
+            grad_ref[0, start:stop, :] = ((turned + part) * (half**-0.5)).T.astype(jnp.bfloat16)
     grad_ref[1] = dk_acc[...].astype(jnp.bfloat16)
     grad_ref[2] = dv_acc[...].astype(jnp.bfloat16)
     span = window + QB
@@ -299,17 +319,23 @@
     gate = 1.0 / (1.0 + jnp.exp(other_logit - own_logit))
     other_gate = 1.0 / (1.0 + jnp.exp(own_logit - other_logit))
     gated_ref[...] = (gate * grad).astype(jnp.bfloat16)
+    result = None
+    ahead = nn(x, in_ref[:, :FF_TILE])
     for low in range(0, hidden, FF_TILE):
-        cut = slice(low, low + FF_TILE)
-        v = nn(x, in_ref[:, cut])
+        high = low + FF_TILE
+        v = ahead
+        if high < hidden:
+            ahead = nn(x, in_ref[:, high : high + FF_TILE])
         square = v * v
         t = jnp.tanh(v * (GELU_A + GELU_A * GELU_B * square))
         h = 0.5 + 0.5 * t
         a = v * h
         slope = h + (a * (1.0 - h)) * (2.0 * GELU_A + 6.0 * GELU_A * GELU_B * square)
-        active_ref[:, cut] = a.astype(jnp.bfloat16)
-        slope_ref[:, cut] = slope.astype(jnp.bfloat16)
-    result = nn(active_ref[...], out_ref[...])
+        slope_ref[:, low:high] = (gate * slope).astype(jnp.bfloat16)
+        a = a.astype(jnp.bfloat16)
+        active_ref[:, low:high] = a
+        part = nn(a, out_ref[low:high, :])
+        result = part if result is None else result + part
     y_ref[...] = (gate * result).astype(jnp.bfloat16).reshape(y_ref.shape)
     gate_grad = jnp.sum(grad * result, axis=1, keepdims=True)
     weight = gate * other_gate * gate_grad
@@ -329,17 +355,16 @@
         router_grad_ref[...] += part
 
 
-def expert_backward_kernel(
-    gated_ref, slope_ref, logit_ref, in_ref, out_ref, router_ref, *refs
-):
+def expert_backward_kernel(slot_ref, slope_ref, logit_ref, in_ref, router_ref, *refs):
     pre_ref, back_ref = refs[-2:]
-    hidden = in_ref.shape[1]
-    gated = gated_ref[...]
+    rows, hidden = slope_ref.shape
+    back = nt(logit_ref[...], router_ref[...])
     for low in range(0, hidden, FF_TILE):
-        cut = slice(low, low + FF_TILE)
-        d = nt(gated, out_ref[cut, :])
-        pre_ref[:, cut] = (d * slope_ref[:, cut].astype(jnp.float32)).astype(jnp.bfloat16)
-    back = nt(pre_ref[...], in_ref[...]) + nt(logit_ref[...], router_ref[...])
+        high = low + FF_TILE
+        d = slot_ref[:, :, low:high].reshape(rows, FF_TILE).astype(jnp.float32)
+        pre = (d * slope_ref[:, low:high].astype(jnp.float32)).astype(jnp.bfloat16)
+        pre_ref[:, low:high] = pre
+        back = back + nt(pre, in_ref[:, low:high])
     back_ref[...] = back.astype(jnp.bfloat16).reshape(back_ref.shape)
 
 
@@ -402,10 +427,10 @@
 
 
 def expert_backward(
-    experts, gated, slope, logit_low, chunk, weight_in, weight_out, router_two, kept
+    experts, slot_grad, slope, logit_low, chunk, weight_in, router_two, kept
 ):
     total, hidden = slope.shape
-    model = gated.shape[1]
+    model = weight_in.shape[0]
     half = total // experts
     group = max(1, min(experts, ROW_BLOCK // half))
     rows = group * half
@@ -417,11 +442,10 @@
         expert_backward_kernel,
         grid=(experts // group,),
         in_specs=[
-            joint(model),
+            pl.BlockSpec((group, half, hidden), lambda i: (i, chunk, 0)),
             flat(hidden),
             flat(LANES),
             fixed(model, hidden),
-            fixed(hidden, model),
             fixed(model, LANES),
         ]
         + [pl.BlockSpec(memory_space=pl.ANY)] * len(kept),
@@ -431,9 +455,9 @@
             dimension_semantics=("arbitrary",), vmem_limit_bytes=56 * 1024 * 1024
         ),
         cost_estimate=pl.CostEstimate(flops=1024, bytes_accessed=1024, transcendentals=0),
-        input_output_aliases={6 + place: place for place in range(len(kept))},
+        input_output_aliases={5 + place: place for place in range(len(kept))},
         name="expert_backward",
-    )(gated, slope, logit_low, weight_in, weight_out, router_two, *kept)
+    )(slot_grad, slope, logit_low, weight_in, router_two, *kept)
 
 
 def swap(values, axis, bit):
@@ -444,17 +468,6 @@
 def bits_of(axis):
     count = lax.axis_size(axis)
     return [1 << place for place in range(count.bit_length() - 1)]
-
-
-def spread_rows(part, axis, bits):
-    held, offsets = part[None], [0]
-    for bit in bits:
-        held = jnp.concatenate([held, swap(held, axis, bit)], axis=0)
-        offsets = offsets + [offset ^ bit for offset in offsets]
-    place = [0] * len(offsets)
-    for index, offset in enumerate(offsets):
-        place[offset // 2] = index
-    return held, swap(held, axis, 1), place
 
 
 def order_kernel(order_ref, *refs):
@@ -470,7 +483,21 @@
 
 
 def gather_rows(parts, axis, orders):
-    spread = [spread_rows(part, axis, bits) for part, bits in zip(parts, orders)]
+    held = [part[None] for part in parts]
+    offsets = [[0] for _ in parts]
+    for stage in range(len(orders[0])):
+        for part, order in enumerate(orders):
+            bit = order[stage]
+            held[part] = jnp.concatenate([held[part], swap(held[part], axis, bit)], axis=0)
+            offsets[part] = offsets[part] + [offset ^ bit for offset in offsets[part]]
+        if stage == 0:
+            early = list(held)
+    spread = []
+    for part, near in enumerate(held):
+        place = [0] * len(offsets[part])
+        for index, offset in enumerate(offsets[part]):
+            place[offset // 2] = index
+        spread.append((near, swap(near, axis, 1), place))
     me = lax.axis_index(axis).astype(jnp.int32)
     chips = spread[0][0].shape[0]
     order = [(me % 2)[None]]
@@ -492,7 +519,11 @@
     return [
         array.reshape(2 * chips * part.shape[0], part.shape[1])
         for array, part in zip(full, parts)
-    ], [near for near, _, _ in spread]
+    ], early, held
+
+
+def after(first, *later):
+    return lax.optimization_barrier((first, *later))[1:]
 
 
 def scatter_sum(blocks, axis):
@@ -512,17 +543,20 @@
     left = bits[::-1]
     values = blocks.reshape((2,) * len(bits) + (rows, width))
     values, left = step(values, left, 1)
+    stages = [values]
     cut = width // 2
     parts = []
     for half, order in ((values[..., :cut], bits[1:]), (values[..., cut:], bits[:0:-1])):
         remaining = left
         for bit in order:
             half, remaining = step(half, remaining, bit)
+            if bit == order[0]:
+                stages.append(half)
         parts.append(half)
-    return jnp.concatenate(parts, axis=-1)
-
-
-def sum_all(values, axis):
+    return jnp.concatenate(parts, axis=-1), stages
+
+
+def sum_all(values, axis, beside):
     rows = values.shape[0]
     bits = bits_of(axis)
     mine = lax.axis_index(axis) % 2
@@ -530,6 +564,7 @@
     keep = jnp.where(mine == 0, low, high)
     came = swap(jnp.where(mine == 0, high, low), axis, 1)
     half = (keep.astype(jnp.float32) + came.astype(jnp.float32)).astype(jnp.bfloat16)
+    (half,) = after(beside, half)
     for bit in bits[1:]:
         came = swap(half, axis, bit)
         half = (half.astype(jnp.float32) + came.astype(jnp.float32)).astype(jnp.bfloat16)
@@ -641,7 +676,7 @@
         axis=1,
     )
     bits = bits_of("shard")
-    (first_full, second_full), (first_held, second_held) = gather_rows(
+    (first_full, second_full), early, held = gather_rows(
         (
             jnp.concatenate([w_query, w_key, small], axis=1),
             jnp.concatenate([w_value, w_output], axis=1),
@@ -682,15 +717,15 @@
     all_places = places_of(0, capacity)
 
     id_sum = jnp.sum(expert_ids, axis=1).astype(jnp.float32)
+    out_grad_later, id_sum = after(early[0], out_grad, id_sum)
+    out_grad_later, id_sum = after(early[1], out_grad_later, id_sum)
     slot_sums = jnp.dot(all_places.astype(jnp.float32), id_sum).reshape(experts, capacity)
     slot_sums = lax.all_to_all(slot_sums, "shard", split_axis=0, concat_axis=0, tiled=True)
     slot_sums = jnp.broadcast_to(
         slot_sums[:, :, None], (experts, capacity, LANES)
     ).astype(jnp.bfloat16)
-    grad_send = pick_rows(all_places, out_grad).reshape(experts, capacity, model_width)
-    grad_send, first_held, second_held = lax.optimization_barrier(
-        (grad_send, first_held, second_held)
-    )
+    grad_send = pick_rows(all_places, out_grad_later).reshape(experts, capacity, model_width)
+    grad_send, slot_sums, *held = lax.optimization_barrier((grad_send, slot_sums, *held))
     grad_received = lax.all_to_all(grad_send, "shard", split_axis=0, concat_axis=0, tiled=True)
 
     inputs_f = inputs.astype(jnp.float32)
@@ -706,18 +741,27 @@
     normed_two, grad_received = lax.optimization_barrier((normed_two, grad_received))
     weight_in = w_in[0]
     weight_out = w_out[0]
+    sends = [pick_rows(places[0], normed_two)]
+    (grad_rows,) = after(sends[0], grad_received)
+    slot_grad = (
+        nt(grad_rows.reshape(-1, model_width), weight_out)
+        .astype(jnp.bfloat16)
+        .reshape(experts, capacity, -1)
+    )
+    (normed_two_later,) = after(slot_grad, normed_two)
+    sends = sends + [pick_rows(places[k], normed_two_later) for k in range(1, CHUNKS)]
     sent = [
         lax.all_to_all(
-            pick_rows(places[k], normed_two).reshape(experts, half, model_width),
+            send.reshape(experts, half, model_width),
             "shard",
             split_axis=0,
             concat_axis=0,
             tiled=True,
         )
-        for k in range(CHUNKS)
+        for send in sends
     ]
-    kept = ()
-    slopes, logit_lows = [], []
+    kept, kept_back = (), ()
+    returned = []
     router_part = jnp.zeros((model_width, LANES), jnp.float32)
     for k in range(CHUNKS):
         *kept, slope, logit_low, part = expert_forward(
@@ -731,32 +775,24 @@
             router_two,
             kept,
         )
-        slopes.append(slope)
-        logit_lows.append(logit_low)
         router_part = router_part + part
-    results, active, gated = kept
-    grad_out_part = jnp.einsum(
-        "rf,rd->fd", active, gated, preferred_element_type=jnp.float32
-    ).astype(jnp.bfloat16)
-    out_summed = lax.psum_scatter(grad_out_part, "rep", scatter_dimension=0, tiled=True)
-    gated, grad_out_part = lax.optimization_barrier((gated, grad_out_part))
-    kept = ()
-    returned = []
-    for k in range(CHUNKS):
-        *kept, back = expert_backward(
-            experts,
-            gated,
-            slopes[k],
-            logit_lows[k],
-            k,
-            weight_in,
-            weight_out,
-            router_two,
-            kept,
+        if k == CHUNKS - 1:
+            results, active, gated = kept
+            (gated,) = after(returned[0], gated)
+            grad_out_part = jnp.einsum(
+                "rf,rd->fd", active, gated, preferred_element_type=jnp.float32
+            ).astype(jnp.bfloat16)
+            out_summed = lax.psum_scatter(grad_out_part, "rep", scatter_dimension=0, tiled=True)
+            (slope,) = after(grad_out_part, slope)
+        *kept_back, back = expert_backward(
+            experts, slot_grad, slope, logit_low, k, weight_in, router_two, kept_back
         )
         returned.append(
             lax.all_to_all(back, "shard", split_axis=0, concat_axis=0, tiled=True)
         )
+        if k + 1 < CHUNKS:
+            (sent[k + 1],) = after(kept_back[0], sent[k + 1])
+    kept = kept_back
     returned[0], grad_pre = lax.optimization_barrier((returned[0], kept[0]))
     rows_in = jnp.concatenate([part.reshape(-1, model_width) for part in sent], axis=0)
     grad_in_part = jnp.einsum(
@@ -776,16 +812,19 @@
     grad_hidden_norm, grad_gain_two = norm_two_pull(grad_normed_two)
     grad_hidden = grad_out + grad_hidden_norm
     grad_branch = grad_hidden.astype(jnp.bfloat16)
-    grad_wo = weight_grad(attended, grad_branch[None])
     grad_attended = jnp.einsum(
         "te,de->td", grad_branch, output_full, preferred_element_type=jnp.float32
     ).astype(jnp.bfloat16)
 
-    out_summed, grad_attended = lax.optimization_barrier((out_summed, grad_attended))
     grad_qkv, diagonals = attention_backward(
         qk, value, attended, grad_attended, query_lanes, key_lanes, rows, lse
     )
-    grad_qkv, results = lax.optimization_barrier((grad_qkv, results))
+    (grad_qkv,) = after(results, grad_qkv)
+    grad_qkv, out_summed = lax.optimization_barrier((grad_qkv, out_summed))
+    packed = weight_grad(normed, grad_qkv)
+    owned, stages = scatter_sum(packed.reshape(experts, rows_here, packed.shape[1]), "shard")
+    grad_qkv, diagonals, grad_branch = after(stages[0], grad_qkv, diagonals, grad_branch)
+    (results,) = after(stages[1], results)
     grad_table = table_gradient(diagonals)
     grad_normed = jnp.zeros((tokens_here, model_width), jnp.float32)
     for place, weight in enumerate(
@@ -815,18 +854,19 @@
         ],
         axis=1,
     )
-    packed = weight_grad(
-        normed,
-        grad_qkv,
-        jnp.concatenate([grad_wo, small_grads.astype(jnp.bfloat16)], axis=1),
-    )
-    owned = scatter_sum(packed.reshape(experts, rows_here, packed.shape[1]), "shard")
-    owned, in_summed = lax.optimization_barrier((owned, in_summed))
-    summed = sum_all(owned, "rep").astype(jnp.float32)
-    small_sum = summed[:, 4 * model_width :]
-
+    second_packed = weight_grad(
+        attended, grad_branch[None], small_grads.astype(jnp.bfloat16)
+    )
+    second_owned, _ = scatter_sum(
+        second_packed.reshape(experts, rows_here, second_packed.shape[1]), "shard"
+    )
     combined = back_rows(all_places, results.reshape(-1, model_width))
     output = (hidden + combined).astype(jnp.bfloat16)
+    owned, in_summed = lax.optimization_barrier((owned, in_summed))
+    summed = sum_all(jnp.concatenate([owned, second_owned], axis=1), "rep", output)
+    summed = summed.astype(jnp.float32)
+    small_sum = summed[:, 4 * model_width :]
+
     return (
         output,
         input_grad,

time: 515 us -> 493 us (0.957)
  waiting for transfers between devices: 98.2 us -> 71.8 us
  Pallas kernels: 170 us -> 150 us
  matrix products: 107 us -> 124 us
    dot_general x0 -> x1, matrix products: none -> 21.1 us  [nt(): lax.dot_general(a, b, (((1,), (1,)), ((), ())), preferred_element_type=jn...]
    all_to_all x2, waiting for transfers between devices: 23.8 us -> 4.18 us  [body(): lax.all_to_all(send.reshape(experts, half, model_width), 'shard', split_a...]
    pallas_call x2, Pallas kernels: 44.7 us -> 31.7 us  [expert_backward(): pl.pallas_call(expert_backward_kernel, grid=(experts // group,), in_specs...]
    ppermute x14 -> x19, waiting for transfers between devices: 53.9 us -> 41.3 us  [swap(): lax.ppermute(values, axis, [(place, place ^ bit) for place in range(count)])]
    all_to_all x1, waiting for transfers between devices: 0.01 us -> 7.8 us  [body(): lax.all_to_all(results, 'shard', split_axis=0, concat_axis=0, tiled=True)]
    all_to_all x2, waiting for transfers between devices: 15.7 us -> 9.1 us  [body(): lax.all_to_all(back, 'shard', split_axis=0, concat_axis=0, tiled=True)]
    ppermute x14 -> x19, starting transfers between devices: 17.5 us -> 18.8 us  [swap(): lax.ppermute(values, axis, [(place, place ^ bit) for place in range(count)])]
    unnamed x97 -> x139, local copies, waits for them, and re-layouts: 17.7 us -> 17.5 us
  transfers between devices with their start and end apart: 23 -> 28, of which waited for: 12 -> 16; matrix products, arithmetic and copies ran while one was open for 26% -> 30% of each run, Pallas kernels for 28% -> 31%
where the time goes in v2:
time: 493 us; the launch traced here: 485 us
  Pallas kernels  150 us (30%)
  matrix products  124 us (25%)
  waiting for transfers between devices  71.8 us (15%)
  starting transfers between devices  50.8 us (10%)
  local copies, waits for them, and re-layouts  38.7 us (8%)
  other arithmetic  34.5 us (7%)
  between operations  15.4 us (3%)
    pallas_call x2, Pallas kernels, expert_forward(): pl.pallas_call(expert_forward_kernel, grid_spec=pltpu.PrefetchScalarGridS...  57.3 us
    ppermute x19, waiting for transfers between devices, swap(): lax.ppermute(values, axis, [(place, place ^ bit) for place in range(count)])  41.3 us
    pallas_call x2, Pallas kernels, expert_backward(): pl.pallas_call(expert_backward_kernel, grid=(experts // group,), in_specs...  31.7 us
    pallas_call x1, Pallas kernels, attention_backward(): pl.pallas_call(backward_kernel, grid=(pairs,), in_specs=[block, pl.BlockS...  28.9 us
    dot_general x1, matrix products, nt(): lax.dot_general(a, b, (((1,), (1,)), ((), ())), preferred_element_type=jn...  21.1 us
    dot_general x1, matrix products, body(): jnp.einsum('rf,rd->fd', active, gated, preferred_element_type=jnp.float32)  20.9 us
    dot_general x1, matrix products, body(): jnp.einsum('rd,rf->df', rows_in, grad_pre, preferred_element_type=jnp.flo...  20.8 us
    dot_general x3, matrix products, back_rows(): jnp.einsum('st,sd->td', places, slots, preferred_element_type=jnp.float32)  20.8 us
  transfers between devices with their start and end apart: 28, of which 16 were waited for; matrix products, arithmetic and copies ran while one was open for 30% of the time, Pallas kernels for 31%

profile of v2, /device:TPU:0, one launch (start us, length us, event | category | flops | bytes accessed | tf_op | source)
XLA Modules:
  0.0 485.4 jit_solution(15006890632022629504)
XLA Ops:
  35.9 7.6 %fusion.12 = bf16[3072,768]{1,0:T(8,128)(2,1)} fusion(bf16[1024,768]{1,0:T(8,128)(2,1)S(1)} %copy-done.32, s32[1024]{0:T(1024)S(1)} %bitcast.193, s32[1024]{0:T(1024)S(1)} %bitcast.186, s32[3072]{0:T(1024)S(1)} %add.542), kind=kOutput, calls=%fused_computation.23 | convolution fusion | flops 4843634688 | bytes 6311936 | tf_op jit(solution)/shard_map/dot_general | solution.py:636
  48.0 5.0 %all-to-all-start.1 = ((bf16[8,384,768]{2,1,0:T(8,128)(2,1)}), bf16[8,384,768]{2,1,0:T(8,128)(2,1)}, u32[]{:S(2)}, u32[]{:S(2)}) async-start(bf16[8,384,768]{2,1,0:T(8,128)(2,1)} %bitcast.167), calls=%async_computation.1 | async-start | bytes 9437184 | tf_op jit(solution)/shard_map/all_to_all | solution.py:729
  69.7 4.5 convolution_convert_fusion.3.q_ref.k_ref
  77.7 19.5 %attention_forward.1 = (bf16[1024,768]{1,0:T(8,128)(2,1)S(1)}, f32[1024,128]{1,0:T(8,128)S(1)}) custom-call(bf16[1024,1536]{1,0:T(8,128)(2,1)S(1)} %convolution_convert_fusion.3.q_ref.k_ref, bf16[1024,1536]{1,0:T(8,128)(2,1)S(1)} %convolution_convert_fusion.3.q_ref.k_ref, bf16[1024,768]{1,0:T(8,128)(2,1)S(1)} %copy-done.6, ...), custom_call_target="tpu_custom_call" | custom-call | flops 1024 | bytes 1024 | tf_op jit(solution)/shard_map/attention_forward/pallas_call | solution.py:130
  100.5 7.2 %all-to-all-done.1.g_ref = bf16[8,384,768]{2,1,0:T(8,128)(2,1)} async-done(((bf16[8,384,768]{2,1,0:T(8,128)(2,1)}), bf16[8,384,768]{2,1,0:T(8,128)(2,1)}, u32[]{:S(2)}, u32[]{:S(2)}) %all-to-all-start.1) | async-done | bytes 4718624 | tf_op jit(solution)/shard_map/all_to_all | solution.py:729
  107.7 5.6 %fusion.24 = bf16[1536,768]{1,0:T(8,128)(2,1)} fusion(bf16[1024,768]{1,0:T(8,128)(2,1)} %multiply_convert_fusion, s32[1024]{0:T(1024)S(1)} %bitcast.194, s32[1024]{0:T(1024)S(1)} %bitcast.187, s32[1536]{0:T(1024)S(1)} %add.547), kind=kOutput, calls=%fused_computation.41 | convolution fusion | flops 2421817344 | bytes 3946496 | tf_op jit(solution)/shard_map/dot_general | solution.py:636
  113.3 4.9 %all-to-all-start.2 = ((bf16[8,192,768]{2,1,0:T(8,128)(2,1)}), bf16[8,192,768]{2,1,0:T(8,128)(2,1)}, u32[]{:S(2)}, u32[]{:S(2)}) async-start(bf16[8,192,768]{2,1,0:T(8,128)(2,1)} %bitcast.172), calls=%async_computation.2 | async-start | bytes 4718592 | tf_op jit(solution)/shard_map/all_to_all | solution.py:754
  118.3 21.1 %convolution_convert_fusion = bf16[3072,3072]{1,0:T(8,128)(2,1)} fusion(bf16[3072,768]{1,0:T(8,128)(2,1)} %bitcast.20, bf16[1,3072,768]{2,1,0:T(8,128)(2,1)} %param.26), kind=kOutput, calls=%fused_computation.2 | convolution fusion | flops 14504951808 | bytes 28311552 | tf_op jit(solution)/shard_map/dot_general | solution.py:70
  139.3 4.2 fusion.23
  143.5 4.2 all-to-all-done.2.x_ref
  147.7 4.6 all-to-all-start.4
  154.1 28.6 %expert_forward.2 = (bf16[8,384,768]{2,1,0:T(8,128)(2,1)}, bf16[3072,3072]{1,0:T(8,128)(2,1)}, bf16[3072,768]{1,0:T(8,128)(2,1)}, bf16[1536,3072]{1,0:T(8,128)(2...) custom-call(s32[1]{0:T(128)} %bitcast.23.me_ref, bf16[8,192,768]{2,1,0:T(8,128)(2,1)} %all-to-all-done.2.x_ref, ...), custom_call_target="tpu_custom_call" | custom-call | flops 14495514624 | bytes 37748736 | tf_op jit(solution)/shard_map/expert_forward/pallas_call | solution.py:385
  182.7 15.3 %expert_backward.2 = (bf16[3072,3072]{1,0:T(8,128)(2,1)}, bf16[8,192,768]{2,1,0:T(8,128)(2,1)}) custom-call(bf16[8,384,3072]{2,1,0:T(8,128)(2,1)} %bitcast.161, bf16[1536,3072]{1,0:T(8,128)(2,1)} %get-tuple-element.74.slope_ref, bf16[1536,128]{1,0:T(8,128)(2,1)} %get-tuple-element.75.logit_ref, bf16[768,3072]{1,0:T(8,128)(2,1)} %bitcast.164, ...), custom_call_target="tpu_custom_call" | custom-call | flops 1024 | bytes 1024 | tf_op jit(solution)/shard_map/expert_backward/pallas_call | solution.py:441
  198.0 4.4 all-to-all-start.3
  202.6 28.7 %expert_forward.3 = (bf16[8,384,768]{2,1,0:T(8,128)(2,1)}, bf16[3072,3072]{1,0:T(8,128)(2,1)}, bf16[3072,768]{1,0:T(8,128)(2,1)}, bf16[1536,3072]{1,0:T(8,128)(2...) custom-call(s32[1]{0:T(128)} %bitcast.23.me_ref, ...), custom_call_target="tpu_custom_call", output_to_operand_aliasing={{0}: (7, {}), {1}: (8, {}), {2}: (9, {})} | custom-call | flops 14495514624 | bytes 37748736 | tf_op jit(solution)/shard_map/expert_forward/pallas_call | solution.py:385
  231.8 20.9 %convolution_convert_fusion.1 = bf16[3072,768]{1,0:T(8,128)(2,1)} fusion(bf16[3072,3072]{1,0:T(8,128)(2,1)} %get-tuple-element.83, bf16[3072,768]{1,0:T(8,128)(2,1)} %get-tuple-element.85), kind=kOutput, calls=%fused_computation.24 | convolution fusion | flops 14497873920 | bytes 28311552 | tf_op jit(solution)/shard_map/rf,rd->fd/dot_general | solution.py:782
  252.8 16.4 %expert_backward.3 = (bf16[3072,3072]{1,0:T(8,128)(2,1)}, bf16[8,192,768]{2,1,0:T(8,128)(2,1)}) custom-call(bf16[8,384,3072]{2,1,0:T(8,128)(2,1)} %bitcast.162, bf16[1536,3072]{1,0:T(8,128)(2,1)} %get-tuple-element.87.slope_ref, bf16[1536,128]{1,0:T(8,128)(2,1)} %get-tuple-element.88.logit_ref, ...), custom_call_target="tpu_custom_call", output_to_operand_aliasing={{0}: (5, {})} | custom-call | flops 1024 | bytes 1024 | tf_op jit(solution)/shard_map/expert_backward/pallas_call | solution.py:441
  269.2 4.4 all-to-all-start.5
  273.6 20.8 %convolution_convert_fusion.2 = bf16[768,3072]{1,0:T(8,128)(2,1)} fusion(bf16[3072,3072]{1,0:T(8,128)(2,1)} %get-tuple-element.92, bf16[1536,768]{1,0:T(8,128)(2,1)} %bitcast.28, bf16[1536,768]{1,0:T(8,128)(2,1)} %bitcast.27), kind=kOutput, calls=%fused_computation.25 | convolution fusion | flops 14507311104 | bytes 28311552 | tf_op jit(solution)/shard_map/rd,rf->df/dot_general | solution.py:798
  294.4 8.6 %all-to-all-done.5 = bf16[8,192,768]{2,1,0:T(8,128)(2,1)} async-done(((bf16[8,192,768]{2,1,0:T(8,128)(2,1)}), bf16[8,192,768]{2,1,0:T(8,128)(2,1)}, u32[]{:S(2)}, u32[]{:S(2)}) %all-to-all-start.5) | async-done | bytes 2359328 | tf_op jit(solution)/shard_map/all_to_all | solution.py:791
  303.1 4.6 all-to-all-start.6
  308.4 5.0 %fusion.13 = f32[1024,768]{1,0:T(8,128)S(1)} fusion(bf16[1536,768]{1,0:T(8,128)(2,1)} %bitcast.29, s32[1024]{0:T(1024)S(1)} %bitcast.196, s32[1024]{0:T(1024)S(1)} %bitcast.189, s32[1536]{0:T(1024)S(1)} %add.547), kind=kOutput, calls=%fused_computation.26 | convolution fusion | flops 2420637696 | bytes 5519360 | tf_op jit(solution)/shard_map/st,sd->td/dot_general | solution.py:640
  313.5 6.2 %multiply_reduce_fusion = (bf16[768]{0:T(1024)(128)(2,1)}, f32[1024]{0:T(1024)S(1)}, f32[1024,768]{1,0:T(8,128)S(1)}) fusion(f32[1024,768]{1,0:T(8,128)S(1)} %get-tuple-element.231, f32[1024]{0:T(1024)S(1)} %fusion.97, f32[768]{0:T(1024)S(1)} %get-tuple-element.212, f32[1024,768]{1,0:T(8,128)S(1)} %fusion.13, bf16[1536,768]{1,0:T(8,128)(2,1)} %bitcast.30, ...), kind=kOutput, calls=%fused_computation.49 | convolution fusion | flops 2426140928 | bytes 11823616 | tf_op jit(solution)/shard_map/st,sd->td/dot_general | solution.py:640
  325.1 28.9 %attention_backward.1 = (bf16[3,1024,768]{2,1,0:T(8,128)(2,1)}, f32[6,2,1024]{2,1,0:T(2,128)S(1)}) custom-call(bf16[1024,1536]{1,0:T(8,128)(2,1)} %copy-done, bf16[1024,1536]{1,0:T(8,128)(2,1)} %copy-done, bf16[1024,768]{1,0:T(8,128)(2,1)S(1)} %copy-done.7, bf16[1024,768]{1,0:T(8,128)(2,1)S(1)} %copy-done.9, ...), custom_call_target="tpu_custom_call" | custom-call | flops 1024 | bytes 1024 | tf_op jit(solution)/shard_map/attention_backward/pallas_call | solution.py:254
  354.6 7.8 %all-to-all-done.6 = bf16[8,384,768]{2,1,0:T(8,128)(2,1)} async-done(((bf16[8,384,768]{2,1,0:T(8,128)(2,1)}), bf16[8,384,768]{2,1,0:T(8,128)(2,1)}, u32[]{:S(2)}, u32[]{:S(2)}) %all-to-all-start.6) | async-done | bytes 4718624 | tf_op jit(solution)/shard_map/all_to_all | solution.py:805
  366.2 6.4 %weight_grad.2 = bf16[768,2304]{1,0:T(8,128)(2,1)S(1)} custom-call(bf16[1024,768]{1,0:T(8,128)(2,1)S(1)} %copy-done.5, bf16[3,1024,768]{2,1,0:T(8,128)(2,1)S(1)} %copy-done.1), custom_call_target="tpu_custom_call" | custom-call | flops 1024 | bytes 1024 | tf_op jit(solution)/shard_map/weight_grad/pallas_call | solution.py:615
  389.8 4.2 fusion.26
  403.3 10.7 %collective-permute-done.9 = bf16[2,96,1152]{2,1,0:T(8,128)(2,1)S(1)} collective-permute-done((bf16[2,96,1152]{2,1,0:T(8,128)(2,1)S(1)}, bf16[2,96,1152]{2,1,0:T(8,128)(2,1)S(1)}, u32[]{:S(2)}, u32[]{:S(2)}) %collective-permute-start.9) | collective-permute-done | bytes 442400 | tf_op jit(solution)/shard_map/ppermute | solution.py:465
  416.3 4.9 %collective-permute-done.10 = bf16[96,1152]{1,0:T(8,128)(2,1)S(1)} collective-permute-done((bf16[96,1152]{1,0:T(8,128)(2,1)S(1)}, bf16[96,1152]{1,0:T(8,128)(2,1)S(1)}, u32[]{:S(2)}, u32[]{:S(2)}) %collective-permute-start.10) | collective-permute-done | bytes 221216 | tf_op jit(solution)/shard_map/ppermute | solution.py:465
  442.9 9.6 %add_convert_fusion = bf16[1024,768]{1,0:T(8,128)(2,1)} fusion(f32[1024,768]{1,0:T(8,128)S(1)} %copy-done.24, bf16[3072,768]{1,0:T(8,128)(2,1)} %bitcast.36, s32[1024]{0:T(1024)S(1)} %bitcast.198, s32[1024]{0:T(1024)S(1)} %bitcast.191, s32[3072]{0:T(1024)S(1)} %copy-done.58), kind=kOutput, calls=%fused_computation.51 | convolution fusion | flops 4842848256 | bytes 9457664 | tf_op jit(solution)/shard_map/st,sd->td/dot_general | solution.py:640
  456.0 10.5 %collective-permute-done.17 = bf16[48,3328]{1,0:T(8,128)(2,1)S(1)} collective-permute-done((bf16[48,3328]{1,0:T(8,128)(2,1)S(1)}, bf16[48,3328]{1,0:T(8,128)(2,1)S(1)}, u32[]{:S(2)}, u32[]{:S(2)}) %collective-permute-start.17) | collective-permute-done | bytes 319520 | tf_op jit(solution)/shard_map/ppermute | solution.py:465
  471.1 4.0 collective-permute-done.18
  (306 shorter events, 130.8 us)
Async XLA Ops:
  11.5 13.8 %collective-permute-start = (bf16[1,96,1664]{2,1,0:T(8,128)(2,1)S(1)}, bf16[1,96,1664]{2,1,0:T(8,128)(2,1)S(1)}, u32[]{:S(2)}, u32[]{:S(2)}) collective-permute-start(bf16[1,96,1664]{2,1,0:T(8,128)(2,1)S(1)} %bitcast.168), channel_id=1, source_target_pairs={{0,8},{4,12},{8,0},{12,4},{16,24},{20,28},{24,16},{28,20},{1,9},{5... | collective-permute-start | bytes 958472 | tf_op jit(solution)/shard_map/ppermute | solution.py:465
  15.5 8.5 %collective-permute-start.3 = (bf16[1,96,1536]{2,1,0:T(8,128)(2,1)S(1)}, bf16[1,96,1536]{2,1,0:T(8,128)(2,1)S(1)}, u32[]{:S(2)}, u32[]{:S(2)}) collective-permute-start(bf16[1,96,1536]{2,1,0:T(8,128)(2,1)S(1)} %maximum_bitcast_fusion), channel_id=1, source_target_pairs={{0,16},{4,20},{8,24},{12,28},{16,0},{20,4},{24,8},{28,12},{1,17},{... | collective-permute-start | bytes 884744 | tf_op jit(solution)/shard_map/ppermute | solution.py:465
  17.1 48.1 %copy-start.59 = (pred[1024]{0:T(1024)(128)(4,1)}, pred[1024]{0:T(1024)(128)(4,1)S(1)}, u32[]{:S(2)}) copy-start(pred[1024]{0:T(1024)(128)(4,1)S(1)} %fusion.80) | copy-start | bytes 3076
  22.4 291.0 %copy-start.61 = (s32[1024,1]{0,1:T(1,128)}, s32[1024,1]{0,1:T(1,128)S(1)}, u32[]{:S(2)}) copy-start(s32[1024,1]{0,1:T(1,128)S(1)} %get-tuple-element.226) | copy-start | bytes 12292
  22.4 291.0 %copy-start.63 = (s32[1024,1]{0,1:T(1,128)}, s32[1024,1]{0,1:T(1,128)S(1)}, u32[]{:S(2)}) copy-start(s32[1024,1]{0,1:T(1,128)S(1)} %get-tuple-element.227) | copy-start | bytes 12292
  24.9 18.7 %collective-permute-start.4 = (bf16[2,96,1536]{2,1,0:T(8,128)(2,1)}, bf16[2,96,1536]{2,1,0:T(8,128)(2,1)}, u32[]{:S(2)}, u32[]{:S(2)}) collective-permute-start(bf16[2,96,1536]{2,1,0:T(8,128)(2,1)} %pad_maximum_fusion.4), channel_id=1, source_target_pairs={{0,8},{4,12},{8,0},{12,4},{16,24},{20,28},{24,16},{28,20},{1,9},{5... | collective-permute-start | bytes 1769480 | tf_op jit(solution)/shard_map/ppermute | solution.py:465
  26.1 18.7 %collective-permute-start.1 = (bf16[2,96,1664]{2,1,0:T(8,128)(2,1)}, bf16[2,96,1664]{2,1,0:T(8,128)(2,1)}, u32[]{:S(2)}, u32[]{:S(2)}) collective-permute-start(bf16[2,96,1664]{2,1,0:T(8,128)(2,1)} %pad_maximum_fusion.2), channel_id=1, source_target_pairs={{0,16},{4,20},{8,24},{12,28},{16,0},{20,4},{24,8},{28,12},{1,17},{... | collective-permute-start | bytes 1916936 | tf_op jit(solution)/shard_map/ppermute | solution.py:465
  32.5 11.0 %all-to-all-start = ((bf16[8,2,192]{2,1,0:T(2,128)(2,1)}), bf16[8,2,192]{2,1,0:T(2,128)(2,1)S(1)}, u32[]{:S(2)}, u32[]{:S(2)}) async-start(bf16[8,2,192]{2,1,0:T(2,128)(2,1)} %reshape.511), calls=%async_computation | async-start | bytes 16384 | tf_op jit(solution)/shard_map/all_to_all | solution.py:723
  46.1 11.3 %collective-permute-start.2 = (bf16[4,96,1664]{2,1,0:T(8,128)(2,1)S(1)}, bf16[4,96,1664]{2,1,0:T(8,128)(2,1)}, u32[]{:S(2)}, u32[]{:S(2)}) collective-permute-start(bf16[4,96,1664]{2,1,0:T(8,128)(2,1)S(1)} %pad_maximum_fusion.refs_0_), channel_id=1, source_target_pairs={{0,4},{4,0},{8,12},{12,8},{16,20},{20,16},{24,28},{28,24},{1,5},{5... | collective-permute-start | bytes 3833864 | tf_op jit(solution)/shard_map/ppermute | solution.py:465
  48.0 59.8 %all-to-all-start.1 = ((bf16[8,384,768]{2,1,0:T(8,128)(2,1)}), bf16[8,384,768]{2,1,0:T(8,128)(2,1)}, u32[]{:S(2)}, u32[]{:S(2)}) async-start(bf16[8,384,768]{2,1,0:T(8,128)(2,1)} %bitcast.167), calls=%async_computation.1 | async-start | bytes 9437184 | tf_op jit(solution)/shard_map/all_to_all | solution.py:729
  54.3 3.0 collective-permute-start.5
  98.7 220.9 %copy-start.23 = (f32[1024,768]{1,0:T(8,128)}, f32[1024,768]{1,0:T(8,128)S(1)}, u32[]{:S(2)}) copy-start(f32[1024,768]{1,0:T(8,128)S(1)} %get-tuple-element.231) | copy-start | bytes 9437188
  113.3 34.4 %all-to-all-start.2 = ((bf16[8,192,768]{2,1,0:T(8,128)(2,1)}), bf16[8,192,768]{2,1,0:T(8,128)(2,1)}, u32[]{:S(2)}, u32[]{:S(2)}) async-start(bf16[8,192,768]{2,1,0:T(8,128)(2,1)} %bitcast.172), calls=%async_computation.2 | async-start | bytes 4718592 | tf_op jit(solution)/shard_map/all_to_all | solution.py:754
  147.7 50.3 %all-to-all-start.4 = ((bf16[8,192,768]{2,1,0:T(8,128)(2,1)}), bf16[8,192,768]{2,1,0:T(8,128)(2,1)}, u32[]{:S(2)}, u32[]{:S(2)}) async-start(bf16[8,192,768]{2,1,0:T(8,128)(2,1)} %bitcast.171), calls=%async_computation.4 | async-start | bytes 4718592 | tf_op jit(solution)/shard_map/all_to_all | solution.py:754
  198.0 33.9 %all-to-all-start.3 = ((bf16[8,192,768]{2,1,0:T(8,128)(2,1)}), bf16[8,192,768]{2,1,0:T(8,128)(2,1)}, u32[]{:S(2)}, u32[]{:S(2)}) async-start(bf16[8,192,768]{2,1,0:T(8,128)(2,1)} %get-tuple-element.76), calls=%async_computation.3 | async-start | bytes 4718592 | tf_op jit(solution)/shard_map/all_to_all | solution.py:791
  202.4 160.1 %reduce-scatter.3.cloned.1.call-start = ((), (), s32[]{:S(2)}) async-start(), calls=%async_computation.9 | async-start | bytes 5898240 | tf_op jit(solution)/shard_map/reduce_scatter | solution.py:785
  269.2 33.8 %all-to-all-start.5 = ((bf16[8,192,768]{2,1,0:T(8,128)(2,1)}), bf16[8,192,768]{2,1,0:T(8,128)(2,1)}, u32[]{:S(2)}, u32[]{:S(2)}) async-start(bf16[8,192,768]{2,1,0:T(8,128)(2,1)} %get-tuple-element.91), calls=%async_computation.5 | async-start | bytes 4718592 | tf_op jit(solution)/shard_map/all_to_all | solution.py:791
  303.1 59.4 %all-to-all-start.6 = ((bf16[8,384,768]{2,1,0:T(8,128)(2,1)}), bf16[8,384,768]{2,1,0:T(8,128)(2,1)}, u32[]{:S(2)}, u32[]{:S(2)}) async-start(bf16[8,384,768]{2,1,0:T(8,128)(2,1)} %get-tuple-element.94), calls=%async_computation.6 | async-start | bytes 9437184 | tf_op jit(solution)/shard_map/all_to_all | solution.py:805
  307.7 119.8 %reduce-scatter.5.cloned.1.call-start = ((), (), s32[]{:S(2)}) async-start(), calls=%async_computation.10 | async-start | bytes 5898240 | tf_op jit(solution)/shard_map/reduce_scatter | solution.py:801
  373.9 4.2 collective-permute-start.6
  382.8 19.4 %collective-permute-start.7 = (bf16[2,96,1152]{2,1,0:T(8,128)(2,1)}, bf16[2,96,1152]{2,1,0:T(8,128)(2,1)}, u32[]{:S(2)}, u32[]{:S(2)}) collective-permute-start(bf16[2,96,1152]{2,1,0:T(8,128)(2,1)} %dynamic-slice_bitcast_fusion.3), channel_id=1, source_target_pairs={{0,8},{4,12},{8,0},{12,4},{16,24},{20,28},{24,16},{28,20},{1,9},{5... | collective-permute-start | bytes 1327112 | tf_op jit(solution)/shard_map/ppermute | solution.py:465
  401.3 21.2 %collective-permute-start.11 = (bf16[2,2,96,1024]{3,2,1,0:T(8,128)(2,1)S(1)}, bf16[2,2,96,1024]{3,2,1,0:T(8,128)(2,1)S(1)}, u32[]{:S(2)}, u32[]{:S(2)}) collective-permute-start(bf16[2,2,96,1024]{3,2,1,0:T(8,128)(2,1)S(1)} %dynamic-slice_bitcast_fusion.1), channel_id=1, source_target_pairs={{0,4},{4,0},{8,12},{12,8},{16,20},{20,16},{24,28},{28,24},{1,5},{5... | collective-permute-start | bytes 2359304 | tf_op jit(solution)/shard_map/ppermute | solution.py:465
  401.5 12.5 %collective-permute-start.9 = (bf16[2,96,1152]{2,1,0:T(8,128)(2,1)S(1)}, bf16[2,96,1152]{2,1,0:T(8,128)(2,1)S(1)}, u32[]{:S(2)}, u32[]{:S(2)}) collective-permute-start(bf16[2,96,1152]{2,1,0:T(8,128)(2,1)S(1)} %dynamic-slice_bitcast_fusion.2), channel_id=1, source_target_pairs={{0,16},{4,20},{8,24},{12,28},{16,0},{20,4},{24,8},{28,12},{1,17},{... | collective-permute-start | bytes 1327112 | tf_op jit(solution)/shard_map/ppermute | solution.py:465
  414.2 7.0 %collective-permute-start.10 = (bf16[96,1152]{1,0:T(8,128)(2,1)S(1)}, bf16[96,1152]{1,0:T(8,128)(2,1)S(1)}, u32[]{:S(2)}, u32[]{:S(2)}) collective-permute-start(bf16[96,1152]{1,0:T(8,128)(2,1)S(1)} %dynamic-slice_bitcast_fusion.4), channel_id=1, source_target_pairs={{0,8},{4,12},{8,0},{12,4},{16,24},{20,28},{24,16},{28,20},{1,9},{5... | collective-permute-start | bytes 663560 | tf_op jit(solution)/shard_map/ppermute | solution.py:465
  415.7 6.7 %collective-permute-start.8 = (bf16[96,1152]{1,0:T(8,128)(2,1)S(1)}, bf16[96,1152]{1,0:T(8,128)(2,1)S(1)}, u32[]{:S(2)}, u32[]{:S(2)}) collective-permute-start(bf16[96,1152]{1,0:T(8,128)(2,1)S(1)} %dynamic-slice_bitcast_fusion.5), channel_id=1, source_target_pairs={{0,16},{4,20},{8,24},{12,28},{16,0},{20,4},{24,8},{28,12},{1,17},{... | collective-permute-start | bytes 663560 | tf_op jit(solution)/shard_map/ppermute | solution.py:465
  424.4 6.0 %collective-permute-start.14 = (bf16[2,96,512]{2,1,0:T(8,128)(2,1)}, bf16[2,96,512]{2,1,0:T(8,128)(2,1)}, u32[]{:S(2)}, u32[]{:S(2)}) collective-permute-start(bf16[2,96,512]{2,1,0:T(8,128)(2,1)} %dynamic-slice_bitcast_fusion.6), channel_id=1, source_target_pairs={{0,16},{4,20},{8,24},{12,28},{16,0},{20,4},{24,8},{28,12},{1,17},{... | collective-permute-start | bytes 589832 | tf_op jit(solution)/shard_map/ppermute | solution.py:465
  427.6 7.8 %collective-permute-start.12 = (bf16[2,96,512]{2,1,0:T(8,128)(2,1)S(1)}, bf16[2,96,512]{2,1,0:T(8,128)(2,1)S(1)}, u32[]{:S(2)}, u32[]{:S(2)}) collective-permute-start(bf16[2,96,512]{2,1,0:T(8,128)(2,1)S(1)} %dynamic-slice_bitcast_fusion.7), channel_id=1, source_target_pairs={{0,8},{4,12},{8,0},{12,4},{16,24},{20,28},{24,16},{28,20},{1,9},{5... | collective-permute-start | bytes 589832 | tf_op jit(solution)/shard_map/ppermute | solution.py:465
  431.4 5.6 %collective-permute-start.15 = (bf16[96,512]{1,0:T(8,128)(2,1)S(1)}, bf16[96,512]{1,0:T(8,128)(2,1)S(1)}, u32[]{:S(2)}, u32[]{:S(2)}) collective-permute-start(bf16[96,512]{1,0:T(8,128)(2,1)S(1)} %dynamic-slice_bitcast_fusion.8), channel_id=1, source_target_pairs={{0,8},{4,12},{8,0},{12,4},{16,24},{20,28},{24,16},{28,20},{1,9},{5... | collective-permute-start | bytes 294920 | tf_op jit(solution)/shard_map/ppermute | solution.py:465
  435.5 4.7 collective-permute-start.13
  441.3 11.2 %collective-permute-start.16 = (bf16[48,3328]{1,0:T(8,128)(2,1)S(1)}, bf16[48,3328]{1,0:T(8,128)(2,1)S(1)}, u32[]{:S(2)}, u32[]{:S(2)}) collective-permute-start(bf16[48,3328]{1,0:T(8,128)(2,1)S(1)} %broadcast_select_fusion.2), channel_id=1, source_target_pairs={{0,1},{1,0},{2,3},{3,2},{4,5},{5,4},{6,7},{7,6},{8,9},{9,8},{10,11... | collective-permute-start | bytes 958472 | tf_op jit(solution)/shard_map/ppermute | solution.py:465
  452.7 13.8 %collective-permute-start.17 = (bf16[48,3328]{1,0:T(8,128)(2,1)S(1)}, bf16[48,3328]{1,0:T(8,128)(2,1)S(1)}, u32[]{:S(2)}, u32[]{:S(2)}) collective-permute-start(bf16[48,3328]{1,0:T(8,128)(2,1)S(1)} %add_convert_fusion.2), channel_id=1, source_target_pairs={{0,2},{1,3},{2,0},{3,1},{4,6},{5,7},{6,4},{7,5},{8,10},{9,11},{10,... | collective-permute-start | bytes 958472 | tf_op jit(solution)/shard_map/ppermute | solution.py:465
  466.5 8.6 %collective-permute-start.18 = (bf16[48,3328]{1,0:T(8,128)(2,1)S(1)}, bf16[48,3328]{1,0:T(8,128)(2,1)S(1)}, u32[]{:S(2)}, u32[]{:S(2)}) collective-permute-start(bf16[48,3328]{1,0:T(8,128)(2,1)S(1)} %add_convert_fusion.1), channel_id=1, source_target_pairs={{0,1},{1,0},{2,3},{3,2},{4,5},{5,4},{6,7},{7,6},{8,9},{9,8},{10,11... | collective-permute-start | bytes 958472 | tf_op jit(solution)/shard_map/ppermute | solution.py:465
  (63 other events, 508.1 us)
Sparse Core Ops, SparseCore 0:
  252.9 86.4 reduce-scatter.2
  341.7 85.7 reduce-scatter.4

commit v3 on v2

--- a/solution.py
+++ b/solution.py
@@ -11,7 +11,7 @@
 BUCKETS = 32
 MAX_DISTANCE = 128
 LONGEST = 512
-QB = 256
+QB = 128
 BIG = 1e9
 LANES = 128
 FF_TILE = 512
@@ -564,14 +564,15 @@
     keep = jnp.where(mine == 0, low, high)
     came = swap(jnp.where(mine == 0, high, low), axis, 1)
     half = (keep.astype(jnp.float32) + came.astype(jnp.float32)).astype(jnp.bfloat16)
-    (half,) = after(beside, half)
     for bit in bits[1:]:
         came = swap(half, axis, bit)
         half = (half.astype(jnp.float32) + came.astype(jnp.float32)).astype(jnp.bfloat16)
+    (half,) = after(beside, half)
     came = swap(half, axis, 1)
-    return jnp.concatenate(
+    total = jnp.concatenate(
         [jnp.where(mine == 0, half, came), jnp.where(mine == 0, came, half)], axis=0
     )
+    return total
 
 
 def weight_grad_kernel(steps, left_ref, right_ref, *refs):
@@ -625,6 +626,60 @@
         cost_estimate=pl.CostEstimate(flops=1024, bytes_accessed=1024, transcendentals=0),
         name="weight_grad",
     )(*operands)
+
+
+def norm_back_kernel(
+    grad_ref, first_ref, second_ref, x_ref, gain_ref, hidden_ref, out_ref, gain_grad_ref
+):
+    model = x_ref.shape[1]
+    grad = nt(grad_ref[0], first_ref[:, :model])
+    grad = grad + nt(grad_ref[1], first_ref[:, model : 2 * model])
+    grad = grad + nt(grad_ref[2], second_ref[:, :model])
+    x = x_ref[...].astype(jnp.float32)
+    scale = lax.rsqrt(jnp.mean(x * x, axis=1, keepdims=True) + eps_norm)
+    scaled = grad * gain_ref[...]
+    inner = jnp.mean(x * scaled, axis=1, keepdims=True)
+    back = scale * scaled - x * (scale * scale * scale * inner)
+    out_ref[...] = (hidden_ref[...] + back).astype(jnp.bfloat16)
+    part = jnp.sum(grad * x * scale, axis=0, keepdims=True)
+
+    @pl.when(pl.program_id(0) == 0)
+    def _():
+        gain_grad_ref[...] = part
+
+    @pl.when(pl.program_id(0) > 0)
+    def _():
+        gain_grad_ref[...] += part
+
+
+def norm_back(grads, first_full, second_full, inputs, gain, grad_hidden):
+    _, tokens, model = grads.shape
+    rows = min(TILE, tokens)
+    block = pl.BlockSpec((rows, model), lambda i: (i, 0))
+    fixed = lambda array: pl.BlockSpec(array.shape, lambda i: (0, 0))
+    gain = gain[None]
+    return pl.pallas_call(
+        norm_back_kernel,
+        grid=(tokens // rows,),
+        in_specs=[
+            pl.BlockSpec((3, rows, model), lambda i: (0, i, 0)),
+            fixed(first_full),
+            fixed(second_full),
+            block,
+            fixed(gain),
+            block,
+        ],
+        out_specs=[block, pl.BlockSpec((1, model), lambda i: (0, 0))],
+        out_shape=[
+            jax.ShapeDtypeStruct((tokens, model), jnp.bfloat16),
+            jax.ShapeDtypeStruct((1, model), jnp.float32),
+        ],
+        compiler_params=pltpu.CompilerParams(
+            dimension_semantics=("arbitrary",), vmem_limit_bytes=32 * 1024 * 1024
+        ),
+        cost_estimate=pl.CostEstimate(flops=1024, bytes_accessed=1024, transcendentals=0),
+        name="norm_back",
+    )(grads, first_full, second_full, inputs, gain, grad_hidden)
 
 
 def rms_scale(values, gain_vec):
@@ -799,9 +854,8 @@
         "rd,rf->df", rows_in, grad_pre, preferred_element_type=jnp.float32
     ).astype(jnp.bfloat16)
     in_summed = lax.psum_scatter(grad_in_part, "rep", scatter_dimension=1, tiled=True)
-    *returned, grad_in_part, results = lax.optimization_barrier(
-        (*returned, grad_in_part, results)
-    )
+    last, grad_in_part, results = lax.optimization_barrier((returned[-1], grad_in_part, results))
+    returned[-1] = last
     results = lax.all_to_all(results, "shard", split_axis=0, concat_axis=0, tiled=True)
 
     grad_out = out_grad.astype(jnp.float32)
@@ -819,23 +873,17 @@
     grad_qkv, diagonals = attention_backward(
         qk, value, attended, grad_attended, query_lanes, key_lanes, rows, lse
     )
-    (grad_qkv,) = after(results, grad_qkv)
     grad_qkv, out_summed = lax.optimization_barrier((grad_qkv, out_summed))
     packed = weight_grad(normed, grad_qkv)
+    (packed,) = after(results, packed)
     owned, stages = scatter_sum(packed.reshape(experts, rows_here, packed.shape[1]), "shard")
     grad_qkv, diagonals, grad_branch = after(stages[0], grad_qkv, diagonals, grad_branch)
     (results,) = after(stages[1], results)
     grad_table = table_gradient(diagonals)
-    grad_normed = jnp.zeros((tokens_here, model_width), jnp.float32)
-    for place, weight in enumerate(
-        (qk_full[:, :model_width], qk_full[:, model_width:], value_full)
-    ):
-        grad_normed = grad_normed + jnp.einsum(
-            "te,de->td", grad_qkv[place], weight, preferred_element_type=jnp.float32
-        )
-    unused_one, norm_one_pull = jax.vjp(rms_scale, inputs_f, gain_one)
-    grad_inputs_norm, grad_gain_one = norm_one_pull(grad_normed)
-    input_grad = (grad_hidden + grad_inputs_norm).astype(jnp.bfloat16)
+    input_grad, grad_gain_one = norm_back(
+        grad_qkv, first_full, second_full, inputs, gain_one, grad_hidden
+    )
+    grad_gain_one = grad_gain_one[0]
 
     grad_router = router_part[:, :experts] + router_part[
         :, LANES // 2 : LANES // 2 + experts
@@ -854,15 +902,16 @@
         ],
         axis=1,
     )
-    second_packed = weight_grad(
-        attended, grad_branch[None], small_grads.astype(jnp.bfloat16)
-    )
+    small_grads = small_grads.astype(jnp.bfloat16)
+    small_grads, grad_branch = after(stages[1], small_grads, grad_branch)
+    small_grads, grad_branch = after(stages[2], small_grads, grad_branch)
+    second_packed = weight_grad(attended, grad_branch[None], small_grads)
     second_owned, _ = scatter_sum(
         second_packed.reshape(experts, rows_here, second_packed.shape[1]), "shard"
     )
     combined = back_rows(all_places, results.reshape(-1, model_width))
     output = (hidden + combined).astype(jnp.bfloat16)
-    owned, in_summed = lax.optimization_barrier((owned, in_summed))
+    owned, second_owned, in_summed = lax.optimization_barrier((owned, second_owned, in_summed))
     summed = sum_all(jnp.concatenate([owned, second_owned], axis=1), "rep", output)
     summed = summed.astype(jnp.float32)
     small_sum = summed[:, 4 * model_width :]

time: 493 us -> 482 us (0.978)
  matrix products: 124 us -> 114 us
    dot_general x3 -> x0, matrix products: 10.4 us -> none  [body(): jnp.einsum('te,de->td', grad_qkv[place], weight, preferred_element_type=j...]
    all_to_all x1, waiting for transfers between devices: 7.8 us -> 0.12 us  [body(): lax.all_to_all(results, 'shard', split_axis=0, concat_axis=0, tiled=True)]
    pallas_call x0 -> x1, Pallas kernels: none -> 6.34 us  [norm_back(): pl.pallas_call(norm_back_kernel, grid=(tokens // rows,), in_specs=[pl.Blo...]
    unnamed x139 -> x112, local copies, waits for them, and re-layouts: 17.5 us -> 19.3 us
  transfers between devices with their start and end apart: 28 -> 28, of which waited for: 16 -> 18; matrix products, arithmetic and copies ran while one was open for 30% -> 29% of each run, Pallas kernels for 31% -> 32%
where the time goes in v3:
time: 482 us; the launch traced here: 475 us
  Pallas kernels  151 us (31%)
  matrix products  114 us (24%)
  waiting for transfers between devices  69 us (14%)
  starting transfers between devices  52.9 us (11%)
  local copies, waits for them, and re-layouts  40.7 us (8%)
  other arithmetic  32.5 us (7%)
  between operations  15.5 us (3%)
    pallas_call x2, Pallas kernels, expert_forward(): pl.pallas_call(expert_forward_kernel, grid_spec=pltpu.PrefetchScalarGridS...  57.3 us
    ppermute x19, waiting for transfers between devices, swap(): lax.ppermute(values, axis, [(place, place ^ bit) for place in range(count)])  40.8 us
    pallas_call x2, Pallas kernels, expert_backward(): pl.pallas_call(expert_backward_kernel, grid=(experts // group,), in_specs...  31.7 us
    pallas_call x1, Pallas kernels, attention_backward(): pl.pallas_call(backward_kernel, grid=(pairs,), in_specs=[block, pl.BlockS...  26.5 us
    dot_general x1, matrix products, nt(): lax.dot_general(a, b, (((1,), (1,)), ((), ())), preferred_element_type=jn...  21 us
    dot_general x3, matrix products, back_rows(): jnp.einsum('st,sd->td', places, slots, preferred_element_type=jnp.float32)  21 us
    dot_general x1, matrix products, body(): jnp.einsum('rf,rd->fd', active, gated, preferred_element_type=jnp.float32)  20.9 us
    dot_general x1, matrix products, body(): jnp.einsum('rd,rf->df', rows_in, grad_pre, preferred_element_type=jnp.flo...  20.8 us
  transfers between devices with their start and end apart: 28, of which 18 were waited for; matrix products, arithmetic and copies ran while one was open for 29% of the time, Pallas kernels for 32%

profile of v3, /device:TPU:0, one launch (start us, length us, event | category | flops | bytes accessed | tf_op | source)
XLA Modules:
  0.0 474.9 jit_solution(3850528460783045158)
XLA Ops:
  34.3 9.0 %fusion.12 = bf16[3072,768]{1,0:T(8,128)(2,1)} fusion(bf16[1024,768]{1,0:T(8,128)(2,1)} %param.29, s32[1024]{0:T(1024)S(1)} %bitcast.189, s32[1024]{0:T(1024)S(1)} %bitcast.182, s32[3072]{0:T(1024)S(1)} %add.530), kind=kOutput, calls=%fused_computation.18 | convolution fusion | flops 4843634688 | bytes 6311936 | tf_op jit(solution)/shard_map/dot_general | solution.py:691
  48.8 4.9 %all-to-all-start.1 = ((bf16[8,384,768]{2,1,0:T(8,128)(2,1)}), bf16[8,384,768]{2,1,0:T(8,128)(2,1)}, u32[]{:S(2)}, u32[]{:S(2)}) async-start(bf16[8,384,768]{2,1,0:T(8,128)(2,1)} %bitcast.163), calls=%async_computation.1 | async-start | bytes 9437184 | tf_op jit(solution)/shard_map/all_to_all | solution.py:784
  76.0 17.6 %attention_forward.1 = (bf16[1024,768]{1,0:T(8,128)(2,1)S(1)}, f32[1024,128]{1,0:T(8,128)S(1)}) custom-call(bf16[1024,1536]{1,0:T(8,128)(2,1)S(1)} %convolution_convert_fusion.3.q_ref.k_ref, bf16[1024,1536]{1,0:T(8,128)(2,1)S(1)} %convolution_convert_fusion.3.q_ref.k_ref, bf16[1024,768]{1,0:T(8,128)(2,1)S(1)} %copy-done.13, ...), custom_call_target="tpu_custom_call" | custom-call | flops 1024 | bytes 1024 | tf_op jit(solution)/shard_map/attention_forward/pallas_call | solution.py:130
  96.9 11.6 %all-to-all-done.1.g_ref = bf16[8,384,768]{2,1,0:T(8,128)(2,1)} async-done(((bf16[8,384,768]{2,1,0:T(8,128)(2,1)}), bf16[8,384,768]{2,1,0:T(8,128)(2,1)}, u32[]{:S(2)}, u32[]{:S(2)}) %all-to-all-start.1) | async-done | bytes 4718624 | tf_op jit(solution)/shard_map/all_to_all | solution.py:784
  108.5 5.5 %fusion.22 = bf16[1536,768]{1,0:T(8,128)(2,1)} fusion(bf16[1024,768]{1,0:T(8,128)(2,1)} %multiply_convert_fusion, s32[1024]{0:T(1024)S(1)} %bitcast.190, s32[1024]{0:T(1024)S(1)} %bitcast.183, s32[1536]{0:T(1024)S(1)} %add.535), kind=kOutput, calls=%fused_computation.36 | convolution fusion | flops 2421817344 | bytes 3946496 | tf_op jit(solution)/shard_map/dot_general | solution.py:691
  114.1 4.6 all-to-all-start.2
  118.6 21.0 %convolution_convert_fusion = bf16[3072,3072]{1,0:T(8,128)(2,1)} fusion(bf16[3072,768]{1,0:T(8,128)(2,1)} %bitcast.20, bf16[1,3072,768]{2,1,0:T(8,128)(2,1)} %param.26), kind=kOutput, calls=%fused_computation.2 | convolution fusion | flops 14504951808 | bytes 28311552 | tf_op jit(solution)/shard_map/dot_general | solution.py:70
  139.7 4.2 fusion.21
  143.9 4.2 all-to-all-done.2.x_ref
  148.1 4.6 all-to-all-start.3
  154.5 28.6 %expert_forward.2 = (bf16[8,384,768]{2,1,0:T(8,128)(2,1)}, bf16[3072,3072]{1,0:T(8,128)(2,1)}, bf16[3072,768]{1,0:T(8,128)(2,1)}, bf16[1536,3072]{1,0:T(8,128)(2...) custom-call(s32[1]{0:T(128)} %bitcast.23.me_ref, bf16[8,192,768]{2,1,0:T(8,128)(2,1)} %all-to-all-done.2.x_ref, ...), custom_call_target="tpu_custom_call" | custom-call | flops 14495514624 | bytes 37748736 | tf_op jit(solution)/shard_map/expert_forward/pallas_call | solution.py:385
  183.1 15.3 %expert_backward.2 = (bf16[3072,3072]{1,0:T(8,128)(2,1)}, bf16[8,192,768]{2,1,0:T(8,128)(2,1)}) custom-call(bf16[8,384,3072]{2,1,0:T(8,128)(2,1)} %bitcast.157, bf16[1536,3072]{1,0:T(8,128)(2,1)} %get-tuple-element.80.slope_ref, bf16[1536,128]{1,0:T(8,128)(2,1)} %get-tuple-element.81.logit_ref, bf16[768,3072]{1,0:T(8,128)(2,1)} %bitcast.160, ...), custom_call_target="tpu_custom_call" | custom-call | flops 1024 | bytes 1024 | tf_op jit(solution)/shard_map/expert_backward/pallas_call | solution.py:441
  198.4 4.4 all-to-all-start.4
  203.3 28.7 %expert_forward.3 = (bf16[8,384,768]{2,1,0:T(8,128)(2,1)}, bf16[3072,3072]{1,0:T(8,128)(2,1)}, bf16[3072,768]{1,0:T(8,128)(2,1)}, bf16[1536,3072]{1,0:T(8,128)(2...) custom-call(s32[1]{0:T(128)} %bitcast.23.me_ref, ...), custom_call_target="tpu_custom_call", output_to_operand_aliasing={{0}: (7, {}), {1}: (8, {}), {2}: (9, {})} | custom-call | flops 14495514624 | bytes 37748736 | tf_op jit(solution)/shard_map/expert_forward/pallas_call | solution.py:385
  232.3 20.9 %convolution_convert_fusion.1 = bf16[3072,768]{1,0:T(8,128)(2,1)} fusion(bf16[3072,3072]{1,0:T(8,128)(2,1)} %get-tuple-element.88, bf16[3072,768]{1,0:T(8,128)(2,1)} %get-tuple-element.91), kind=kOutput, calls=%fused_computation.19 | convolution fusion | flops 14497873920 | bytes 28311552 | tf_op jit(solution)/shard_map/rf,rd->fd/dot_general | solution.py:837
  253.2 16.4 %expert_backward.3 = (bf16[3072,3072]{1,0:T(8,128)(2,1)}, bf16[8,192,768]{2,1,0:T(8,128)(2,1)}) custom-call(bf16[8,384,3072]{2,1,0:T(8,128)(2,1)} %bitcast.158, bf16[1536,3072]{1,0:T(8,128)(2,1)} %get-tuple-element.93.slope_ref, bf16[1536,128]{1,0:T(8,128)(2,1)} %get-tuple-element.94.logit_ref, ...), custom_call_target="tpu_custom_call", output_to_operand_aliasing={{0}: (5, {})} | custom-call | flops 1024 | bytes 1024 | tf_op jit(solution)/shard_map/expert_backward/pallas_call | solution.py:441
  269.6 4.4 all-to-all-start.5
  274.0 20.8 %convolution_convert_fusion.2 = bf16[768,3072]{1,0:T(8,128)(2,1)} fusion(bf16[3072,3072]{1,0:T(8,128)(2,1)} %get-tuple-element.97, bf16[1536,768]{1,0:T(8,128)(2,1)} %bitcast.28, bf16[1536,768]{1,0:T(8,128)(2,1)} %bitcast.27), kind=kOutput, calls=%fused_computation.20 | convolution fusion | flops 14507311104 | bytes 28311552 | tf_op jit(solution)/shard_map/rd,rf->df/dot_general | solution.py:853
  294.8 8.6 %all-to-all-done.5 = bf16[8,192,768]{2,1,0:T(8,128)(2,1)} async-done(((bf16[8,192,768]{2,1,0:T(8,128)(2,1)}), bf16[8,192,768]{2,1,0:T(8,128)(2,1)}, u32[]{:S(2)}, u32[]{:S(2)}) %all-to-all-start.5) | async-done | bytes 2359328 | tf_op jit(solution)/shard_map/all_to_all | solution.py:846
  303.4 4.6 all-to-all-start.6
  308.8 5.0 %fusion.13 = f32[1024,768]{1,0:T(8,128)S(1)} fusion(bf16[1536,768]{1,0:T(8,128)(2,1)} %bitcast.29, s32[1024]{0:T(1024)S(1)} %bitcast.192, s32[1024]{0:T(1024)S(1)} %bitcast.185, s32[1536]{0:T(1024)S(1)} %add.535), kind=kOutput, calls=%fused_computation.21 | convolution fusion | flops 2420637696 | bytes 5519360 | tf_op jit(solution)/shard_map/st,sd->td/dot_general | solution.py:695
  313.8 6.5 %multiply_reduce_fusion = (bf16[768]{0:T(1024)(128)(2,1)}, f32[1024]{0:T(1024)S(1)}, f32[1024,768]{1,0:T(8,128)S(1)}) fusion(f32[1024,768]{1,0:T(8,128)S(1)} %get-tuple-element.243, f32[1024]{0:T(1024)S(1)} %fusion.80, f32[768]{0:T(1024)S(1)} %get-tuple-element.222, f32[1024,768]{1,0:T(8,128)S(1)} %fusion.13, bf16[1536,768]{1,0:T(8,128)(2,1)} %bitcast.30, ...), kind=kOutput, calls=%fused_computation.41 | convolution fusion | flops 2426140928 | bytes 11823616 | tf_op jit(solution)/shard_map/st,sd->td/dot_general | solution.py:695
  325.5 26.5 %attention_backward.1 = (bf16[3,1024,768]{2,1,0:T(8,128)(2,1)}, f32[6,2,768]{2,1,0:T(2,128)S(1)}) custom-call(bf16[1024,1536]{1,0:T(8,128)(2,1)} %copy-done, bf16[1024,1536]{1,0:T(8,128)(2,1)} %copy-done, bf16[1024,768]{1,0:T(8,128)(2,1)S(1)} %copy-done.14, bf16[1024,768]{1,0:T(8,128)(2,1)S(1)} %copy-done.11, ...), custom_call_target="tpu_custom_call" | custom-call | flops 1024 | bytes 1024 | tf_op jit(solution)/shard_map/attention_backward/pallas_call | solution.py:254
  356.3 6.4 %weight_grad.2 = bf16[768,2304]{1,0:T(8,128)(2,1)S(1)} custom-call(bf16[1024,768]{1,0:T(8,128)(2,1)S(1)} %copy-done.9, bf16[3,1024,768]{2,1,0:T(8,128)(2,1)S(1)} %copy-done.1), custom_call_target="tpu_custom_call" | custom-call | flops 1024 | bytes 1024 | tf_op jit(solution)/shard_map/weight_grad/pallas_call | solution.py:616
  376.3 6.3 %norm_back.1 = (bf16[1024,768]{1,0:T(8,128)(2,1)}, f32[1,768]{1,0:T(1,128)S(1)}) custom-call(bf16[3,1024,768]{2,1,0:T(8,128)(2,1)S(1)} %bitcast.142, bf16[768,1664]{1,0:T(8,128)(2,1)S(1)} %bitcast.152, bf16[768,1536]{1,0:T(8,128)(2,1)S(1)} %bitcast.156, bf16[1024,768]{1,0:T(8,128)(2,1)S(1)} %copy-done.4, f32[1,768]{1,0:T(1,128)S(1)} %reshape.473.gain_ref, ...), custom_call_target="tpu_custom_call" | custom-call | flops 1024 | bytes 1024 | tf_op jit(solution)/shard_map/norm_back/pallas_call | solution.py:661
  391.5 7.3 %collective-permute-done.9 = bf16[2,96,1152]{2,1,0:T(8,128)(2,1)} collective-permute-done((bf16[2,96,1152]{2,1,0:T(8,128)(2,1)}, bf16[2,96,1152]{2,1,0:T(8,128)(2,1)}, u32[]{:S(2)}, u32[]{:S(2)}) %collective-permute-start.9) | collective-permute-done | bytes 442400 | tf_op jit(solution)/shard_map/ppermute | solution.py:465
  405.4 5.7 %collective-permute-done.8 = bf16[96,1152]{1,0:T(8,128)(2,1)S(1)} collective-permute-done((bf16[96,1152]{1,0:T(8,128)(2,1)S(1)}, bf16[96,1152]{1,0:T(8,128)(2,1)S(1)}, u32[]{:S(2)}, u32[]{:S(2)}) %collective-permute-start.8) | collective-permute-done | bytes 221216 | tf_op jit(solution)/shard_map/ppermute | solution.py:465
  414.9 4.4 collective-permute-done.12
  430.9 7.8 %collective-permute-done.16 = bf16[48,3328]{1,0:T(8,128)(2,1)S(1)} collective-permute-done((bf16[48,3328]{1,0:T(8,128)(2,1)S(1)}, bf16[48,3328]{1,0:T(8,128)(2,1)S(1)}, u32[]{:S(2)}, u32[]{:S(2)}) %collective-permute-start.16) | collective-permute-done | bytes 319520 | tf_op jit(solution)/shard_map/ppermute | solution.py:465
  441.8 9.6 %add_convert_fusion = bf16[1024,768]{1,0:T(8,128)(2,1)} fusion(f32[1024,768]{1,0:T(8,128)S(1)} %copy-done.32, bf16[3072,768]{1,0:T(8,128)(2,1)} %bitcast.36, s32[1024]{0:T(1024)S(1)} %bitcast.194, s32[1024]{0:T(1024)S(1)} %bitcast.187, s32[3072]{0:T(1024)S(1)} %copy-done.46), kind=kOutput, calls=%fused_computation.42 | convolution fusion | flops 4842848256 | bytes 9457664 | tf_op jit(solution)/shard_map/st,sd->td/dot_general | solution.py:695
  451.4 4.0 collective-permute-done.17
  458.8 5.6 %collective-permute-done.18 = bf16[48,3328]{1,0:T(8,128)(2,1)S(1)} collective-permute-done((bf16[48,3328]{1,0:T(8,128)(2,1)S(1)}, bf16[48,3328]{1,0:T(8,128)(2,1)S(1)}, u32[]{:S(2)}, u32[]{:S(2)}) %collective-permute-start.18) | collective-permute-done | bytes 319520 | tf_op jit(solution)/shard_map/ppermute | solution.py:465
  (278 shorter events, 124.3 us)
Async XLA Ops:
  8.3 14.5 %collective-permute-start.3 = (bf16[1,96,1536]{2,1,0:T(8,128)(2,1)S(1)}, bf16[1,96,1536]{2,1,0:T(8,128)(2,1)S(1)}, u32[]{:S(2)}, u32[]{:S(2)}) collective-permute-start(bf16[1,96,1536]{2,1,0:T(8,128)(2,1)S(1)} %maximum_bitcast_fusion), channel_id=1, source_target_pairs={{0,16},{4,20},{8,24},{12,28},{16,0},{20,4},{24,8},{28,12},{1,17},{... | collective-permute-start | bytes 884744 | tf_op jit(solution)/shard_map/ppermute | solution.py:465
  15.5 9.1 %collective-permute-start = (bf16[1,96,1664]{2,1,0:T(8,128)(2,1)S(1)}, bf16[1,96,1664]{2,1,0:T(8,128)(2,1)S(1)}, u32[]{:S(2)}, u32[]{:S(2)}) collective-permute-start(bf16[1,96,1664]{2,1,0:T(8,128)(2,1)S(1)} %bitcast.164), channel_id=1, source_target_pairs={{0,8},{4,12},{8,0},{12,4},{16,24},{20,28},{24,16},{28,20},{1,9},{5... | collective-permute-start | bytes 958472 | tf_op jit(solution)/shard_map/ppermute | solution.py:465
  17.1 38.7 %copy-start.41 = (s32[768]{0:T(1024)}, s32[768]{0:T(1024)S(1)}, u32[]{:S(2)}) copy-start(s32[768]{0:T(1024)S(1)} %compare_select_fusion.1) | copy-start | bytes 9220
  17.1 49.4 %copy-start.47 = (pred[768]{0:T(1024)(128)(4,1)}, pred[768]{0:T(1024)(128)(4,1)S(1)}, u32[]{:S(2)}) copy-start(pred[768]{0:T(1024)(128)(4,1)S(1)} %fusion.64) | copy-start | bytes 2308
  22.4 291.4 %copy-start.49 = (s32[1024,1]{0,1:T(1,128)}, s32[1024,1]{0,1:T(1,128)S(1)}, u32[]{:S(2)}) copy-start(s32[1024,1]{0,1:T(1,128)S(1)} %get-tuple-element.239) | copy-start | bytes 12292
  23.7 19.8 %collective-permute-start.4 = (bf16[2,96,1536]{2,1,0:T(8,128)(2,1)}, bf16[2,96,1536]{2,1,0:T(8,128)(2,1)}, u32[]{:S(2)}, u32[]{:S(2)}) collective-permute-start(bf16[2,96,1536]{2,1,0:T(8,128)(2,1)} %pad_maximum_fusion.3), channel_id=1, source_target_pairs={{0,8},{4,12},{8,0},{12,4},{16,24},{20,28},{24,16},{28,20},{1,9},{5... | collective-permute-start | bytes 1769480 | tf_op jit(solution)/shard_map/ppermute | solution.py:465
  25.5 20.2 %collective-permute-start.1 = (bf16[2,96,1664]{2,1,0:T(8,128)(2,1)}, bf16[2,96,1664]{2,1,0:T(8,128)(2,1)}, u32[]{:S(2)}, u32[]{:S(2)}) collective-permute-start(bf16[2,96,1664]{2,1,0:T(8,128)(2,1)} %pad_maximum_fusion.2), channel_id=1, source_target_pairs={{0,16},{4,20},{8,24},{12,28},{16,0},{20,4},{24,8},{28,12},{1,17},{... | collective-permute-start | bytes 1916936 | tf_op jit(solution)/shard_map/ppermute | solution.py:465
  30.4 13.0 %all-to-all-start = ((bf16[8,2,192]{2,1,0:T(2,128)(2,1)}), bf16[8,2,192]{2,1,0:T(2,128)(2,1)S(1)}, u32[]{:S(2)}, u32[]{:S(2)}) async-start(bf16[8,2,192]{2,1,0:T(2,128)(2,1)} %reshape.509), calls=%async_computation | async-start | bytes 16384 | tf_op jit(solution)/shard_map/all_to_all | solution.py:778
  46.9 11.4 %collective-permute-start.2 = (bf16[4,96,1664]{2,1,0:T(8,128)(2,1)S(1)}, bf16[4,96,1664]{2,1,0:T(8,128)(2,1)}, u32[]{:S(2)}, u32[]{:S(2)}) collective-permute-start(bf16[4,96,1664]{2,1,0:T(8,128)(2,1)S(1)} %pad_maximum_fusion.refs_0_), channel_id=1, source_target_pairs={{0,4},{4,0},{8,12},{12,8},{16,20},{20,16},{24,28},{28,24},{1,5},{5... | collective-permute-start | bytes 3833864 | tf_op jit(solution)/shard_map/ppermute | solution.py:465
  48.8 59.7 %all-to-all-start.1 = ((bf16[8,384,768]{2,1,0:T(8,128)(2,1)}), bf16[8,384,768]{2,1,0:T(8,128)(2,1)}, u32[]{:S(2)}, u32[]{:S(2)}) async-start(bf16[8,384,768]{2,1,0:T(8,128)(2,1)} %bitcast.163), calls=%async_computation.1 | async-start | bytes 9437184 | tf_op jit(solution)/shard_map/all_to_all | solution.py:784
  55.1 3.3 collective-permute-start.5
  95.1 225.2 %copy-start.31 = (f32[1024,768]{1,0:T(8,128)}, f32[1024,768]{1,0:T(8,128)S(1)}, u32[]{:S(2)}) copy-start(f32[1024,768]{1,0:T(8,128)S(1)} %get-tuple-element.243) | copy-start | bytes 9437188
  114.1 34.1 %all-to-all-start.2 = ((bf16[8,192,768]{2,1,0:T(8,128)(2,1)}), bf16[8,192,768]{2,1,0:T(8,128)(2,1)}, u32[]{:S(2)}, u32[]{:S(2)}) async-start(bf16[8,192,768]{2,1,0:T(8,128)(2,1)} %bitcast.168), calls=%async_computation.2 | async-start | bytes 4718592 | tf_op jit(solution)/shard_map/all_to_all | solution.py:809
  148.1 50.3 %all-to-all-start.3 = ((bf16[8,192,768]{2,1,0:T(8,128)(2,1)}), bf16[8,192,768]{2,1,0:T(8,128)(2,1)}, u32[]{:S(2)}, u32[]{:S(2)}) async-start(bf16[8,192,768]{2,1,0:T(8,128)(2,1)} %bitcast.167), calls=%async_computation.3 | async-start | bytes 4718592 | tf_op jit(solution)/shard_map/all_to_all | solution.py:809
  198.4 33.8 %all-to-all-start.4 = ((bf16[8,192,768]{2,1,0:T(8,128)(2,1)}), bf16[8,192,768]{2,1,0:T(8,128)(2,1)}, u32[]{:S(2)}, u32[]{:S(2)}) async-start(bf16[8,192,768]{2,1,0:T(8,128)(2,1)} %get-tuple-element.89), calls=%async_computation.4 | async-start | bytes 4718592 | tf_op jit(solution)/shard_map/all_to_all | solution.py:846
  202.8 149.8 %reduce-scatter.3.cloned.1.call-start = ((), (), s32[]{:S(2)}) async-start(), calls=%async_computation.9 | async-start | bytes 5898240 | tf_op jit(solution)/shard_map/reduce_scatter | solution.py:840
  269.6 33.8 %all-to-all-start.5 = ((bf16[8,192,768]{2,1,0:T(8,128)(2,1)}), bf16[8,192,768]{2,1,0:T(8,128)(2,1)}, u32[]{:S(2)}, u32[]{:S(2)}) async-start(bf16[8,192,768]{2,1,0:T(8,128)(2,1)} %get-tuple-element.95), calls=%async_computation.5 | async-start | bytes 4718592 | tf_op jit(solution)/shard_map/all_to_all | solution.py:846
  303.4 59.4 %all-to-all-start.6 = ((bf16[8,384,768]{2,1,0:T(8,128)(2,1)}), bf16[8,384,768]{2,1,0:T(8,128)(2,1)}, u32[]{:S(2)}, u32[]{:S(2)}) async-start(bf16[8,384,768]{2,1,0:T(8,128)(2,1)} %get-tuple-element.99), calls=%async_computation.6 | async-start | bytes 9437184 | tf_op jit(solution)/shard_map/all_to_all | solution.py:859
  308.1 120.1 %reduce-scatter.5.cloned.1.call-start = ((), (), s32[]{:S(2)}) async-start(), calls=%async_computation.10 | async-start | bytes 5898240 | tf_op jit(solution)/shard_map/reduce_scatter | solution.py:856
  364.2 4.8 %collective-permute-start.6 = (bf16[2,2,96,2304]{3,2,1,0:T(8,128)(2,1)}, bf16[2,2,96,2304]{3,2,1,0:T(8,128)(2,1)}, u32[]{:S(2)}, u32[]{:S(2)}) collective-permute-start(bf16[2,2,96,2304]{3,2,1,0:T(8,128)(2,1)} %dynamic-slice_bitcast_fusion), channel_id=1, source_target_pairs={{0,4},{4,0},{8,12},{12,8},{16,20},{20,16},{24,28},{28,24},{1,5},{5... | collective-permute-start | bytes 5308424 | tf_op jit(solution)/shard_map/ppermute | solution.py:465
  372.9 17.3 %collective-permute-start.7 = (bf16[2,96,1152]{2,1,0:T(8,128)(2,1)}, bf16[2,96,1152]{2,1,0:T(8,128)(2,1)}, u32[]{:S(2)}, u32[]{:S(2)}) collective-permute-start(bf16[2,96,1152]{2,1,0:T(8,128)(2,1)} %dynamic-slice_bitcast_fusion.3), channel_id=1, source_target_pairs={{0,8},{4,12},{8,0},{12,4},{16,24},{20,28},{24,16},{28,20},{1,9},{5... | collective-permute-start | bytes 1327112 | tf_op jit(solution)/shard_map/ppermute | solution.py:465
  386.3 12.5 %collective-permute-start.9 = (bf16[2,96,1152]{2,1,0:T(8,128)(2,1)}, bf16[2,96,1152]{2,1,0:T(8,128)(2,1)}, u32[]{:S(2)}, u32[]{:S(2)}) collective-permute-start(bf16[2,96,1152]{2,1,0:T(8,128)(2,1)} %dynamic-slice_bitcast_fusion.2), channel_id=1, source_target_pairs={{0,16},{4,20},{8,24},{12,28},{16,0},{20,4},{24,8},{28,12},{1,17},{... | collective-permute-start | bytes 1327112 | tf_op jit(solution)/shard_map/ppermute | solution.py:465
  403.1 9.4 %collective-permute-start.11 = (bf16[2,2,96,1024]{3,2,1,0:T(8,128)(2,1)S(1)}, bf16[2,2,96,1024]{3,2,1,0:T(8,128)(2,1)S(1)}, u32[]{:S(2)}, u32[]{:S(2)}) collective-permute-start(bf16[2,2,96,1024]{3,2,1,0:T(8,128)(2,1)S(1)} %dynamic-slice_bitcast_fusion.1), channel_id=1, source_target_pairs={{0,4},{4,0},{8,12},{12,8},{16,20},{20,16},{24,28},{28,24},{1,5},{5... | collective-permute-start | bytes 2359304 | tf_op jit(solution)/shard_map/ppermute | solution.py:465
  403.2 7.9 %collective-permute-start.8 = (bf16[96,1152]{1,0:T(8,128)(2,1)S(1)}, bf16[96,1152]{1,0:T(8,128)(2,1)S(1)}, u32[]{:S(2)}, u32[]{:S(2)}) collective-permute-start(bf16[96,1152]{1,0:T(8,128)(2,1)S(1)} %dynamic-slice_bitcast_fusion.5), channel_id=1, source_target_pairs={{0,16},{4,20},{8,24},{12,28},{16,0},{20,4},{24,8},{28,12},{1,17},{... | collective-permute-start | bytes 663560 | tf_op jit(solution)/shard_map/ppermute | solution.py:465
  404.8 7.6 %collective-permute-start.10 = (bf16[96,1152]{1,0:T(8,128)(2,1)S(1)}, bf16[96,1152]{1,0:T(8,128)(2,1)S(1)}, u32[]{:S(2)}, u32[]{:S(2)}) collective-permute-start(bf16[96,1152]{1,0:T(8,128)(2,1)S(1)} %dynamic-slice_bitcast_fusion.4), channel_id=1, source_target_pairs={{0,8},{4,12},{8,0},{12,4},{16,24},{20,28},{24,16},{28,20},{1,9},{5... | collective-permute-start | bytes 663560 | tf_op jit(solution)/shard_map/ppermute | solution.py:465
  412.9 6.4 %collective-permute-start.12 = (bf16[2,96,512]{2,1,0:T(8,128)(2,1)S(1)}, bf16[2,96,512]{2,1,0:T(8,128)(2,1)S(1)}, u32[]{:S(2)}, u32[]{:S(2)}) collective-permute-start(bf16[2,96,512]{2,1,0:T(8,128)(2,1)S(1)} %dynamic-slice_bitcast_fusion.7), channel_id=1, source_target_pairs={{0,8},{4,12},{8,0},{12,4},{16,24},{20,28},{24,16},{28,20},{1,9},{5... | collective-permute-start | bytes 589832 | tf_op jit(solution)/shard_map/ppermute | solution.py:465
  414.3 6.1 %collective-permute-start.14 = (bf16[2,96,512]{2,1,0:T(8,128)(2,1)S(1)}, bf16[2,96,512]{2,1,0:T(8,128)(2,1)S(1)}, u32[]{:S(2)}, u32[]{:S(2)}) collective-permute-start(bf16[2,96,512]{2,1,0:T(8,128)(2,1)S(1)} %dynamic-slice_bitcast_fusion.6), channel_id=1, source_target_pairs={{0,16},{4,20},{8,24},{12,28},{16,0},{20,4},{24,8},{28,12},{1,17},{... | collective-permute-start | bytes 589832 | tf_op jit(solution)/shard_map/ppermute | solution.py:465
  419.4 4.7 collective-permute-start.13
  420.5 4.8 %collective-permute-start.15 = (bf16[96,512]{1,0:T(8,128)(2,1)S(1)}, bf16[96,512]{1,0:T(8,128)(2,1)S(1)}, u32[]{:S(2)}, u32[]{:S(2)}) collective-permute-start(bf16[96,512]{1,0:T(8,128)(2,1)S(1)} %dynamic-slice_bitcast_fusion.8), channel_id=1, source_target_pairs={{0,8},{4,12},{8,0},{12,4},{16,24},{20,28},{24,16},{28,20},{1,9},{5... | collective-permute-start | bytes 294920 | tf_op jit(solution)/shard_map/ppermute | solution.py:465
  429.3 9.4 %collective-permute-start.16 = (bf16[48,3328]{1,0:T(8,128)(2,1)S(1)}, bf16[48,3328]{1,0:T(8,128)(2,1)S(1)}, u32[]{:S(2)}, u32[]{:S(2)}) collective-permute-start(bf16[48,3328]{1,0:T(8,128)(2,1)S(1)} %broadcast_select_fusion.2), channel_id=1, source_target_pairs={{0,1},{1,0},{2,3},{3,2},{4,5},{5,4},{6,7},{7,6},{8,9},{9,8},{10,11... | collective-permute-start | bytes 958472 | tf_op jit(solution)/shard_map/ppermute | solution.py:465
  438.8 16.6 %collective-permute-start.17 = (bf16[48,3328]{1,0:T(8,128)(2,1)S(1)}, bf16[48,3328]{1,0:T(8,128)(2,1)S(1)}, u32[]{:S(2)}, u32[]{:S(2)}) collective-permute-start(bf16[48,3328]{1,0:T(8,128)(2,1)S(1)} %add_convert_fusion.2), channel_id=1, source_target_pairs={{0,2},{1,3},{2,0},{3,1},{4,6},{5,7},{6,4},{7,5},{8,10},{9,11},{10,... | collective-permute-start | bytes 958472 | tf_op jit(solution)/shard_map/ppermute | solution.py:465
  455.5 8.9 %collective-permute-start.18 = (bf16[48,3328]{1,0:T(8,128)(2,1)S(1)}, bf16[48,3328]{1,0:T(8,128)(2,1)S(1)}, u32[]{:S(2)}, u32[]{:S(2)}) collective-permute-start(bf16[48,3328]{1,0:T(8,128)(2,1)S(1)} %add_convert_fusion.1), channel_id=1, source_target_pairs={{0,1},{1,0},{2,3},{3,2},{4,5},{5,4},{6,7},{7,6},{8,9},{9,8},{10,11... | collective-permute-start | bytes 958472 | tf_op jit(solution)/shard_map/ppermute | solution.py:465
  (49 other events, 368.3 us)
Sparse Core Ops, SparseCore 0:
  253.3 86.7 reduce-scatter.2
  342.4 85.7 reduce-scatter.4

commit v4 on v3

--- a/solution.py
+++ b/solution.py
@@ -330,9 +330,11 @@
         t = jnp.tanh(v * (GELU_A + GELU_A * GELU_B * square))
         h = 0.5 + 0.5 * t
         a = v * h
-        slope = h + (a * (1.0 - h)) * (2.0 * GELU_A + 6.0 * GELU_A * GELU_B * square)
-        slope_ref[:, low:high] = (gate * slope).astype(jnp.bfloat16)
         a = a.astype(jnp.bfloat16)
+        h = h.astype(jnp.bfloat16)
+        cubic = (2.0 * GELU_A + 6.0 * GELU_A * GELU_B * square).astype(jnp.bfloat16)
+        slope = h + (a * (1.0 - h)) * cubic
+        slope_ref[:, low:high] = gate.astype(jnp.bfloat16) * slope
         active_ref[:, low:high] = a
         part = nn(a, out_ref[low:high, :])
         result = part if result is None else result + part
@@ -793,7 +795,9 @@
     hidden = inputs_f + jnp.dot(attended, output_full, preferred_element_type=jnp.float32)
     normed_two = rms_scale(hidden, gain_two).astype(jnp.bfloat16)
 
-    normed_two, grad_received = lax.optimization_barrier((normed_two, grad_received))
+    normed_two, grad_received, router_two = lax.optimization_barrier(
+        (normed_two, grad_received, router_two)
+    )
     weight_in = w_in[0]
     weight_out = w_out[0]
     sends = [pick_rows(places[0], normed_two)]

time: 482 us -> 481 us (level)
    unnamed x112 -> x114, local copies, waits for them, and re-layouts: 19.3 us -> 18 us
  transfers between devices with their start and end apart: 28 -> 28, of which waited for: 18 -> 15; matrix products, arithmetic and copies ran while one was open for 29% -> 30% of each run, Pallas kernels for 32% -> 32%
where the time goes in v4:
time: 481 us; the launch traced here: 473 us
  Pallas kernels  150 us (31%)
  matrix products  114 us (24%)
  waiting for transfers between devices  69 us (14%)
  starting transfers between devices  52.5 us (11%)
  local copies, waits for them, and re-layouts  39.7 us (8%)
  other arithmetic  32.8 us (7%)
  between operations  15.5 us (3%)
    pallas_call x2, Pallas kernels, expert_forward(): pl.pallas_call(expert_forward_kernel, grid_spec=pltpu.PrefetchScalarGridS...  56.5 us
    ppermute x19, waiting for transfers between devices, swap(): lax.ppermute(values, axis, [(place, place ^ bit) for place in range(count)])  39 us
    pallas_call x2, Pallas kernels, expert_backward(): pl.pallas_call(expert_backward_kernel, grid=(experts // group,), in_specs...  31.6 us
    pallas_call x1, Pallas kernels, attention_backward(): pl.pallas_call(backward_kernel, grid=(pairs,), in_specs=[block, pl.BlockS...  26.5 us
    dot_general x1, matrix products, nt(): lax.dot_general(a, b, (((1,), (1,)), ((), ())), preferred_element_type=jn...  21.1 us
    dot_general x3, matrix products, back_rows(): jnp.einsum('st,sd->td', places, slots, preferred_element_type=jnp.float32)  21 us
    dot_general x1, matrix products, body(): jnp.einsum('rf,rd->fd', active, gated, preferred_element_type=jnp.float32)  20.9 us
    dot_general x1, matrix products, body(): jnp.einsum('rd,rf->df', rows_in, grad_pre, preferred_element_type=jnp.flo...  20.9 us
  transfers between devices with their start and end apart: 28, of which 15 were waited for; matrix products, arithmetic and copies ran while one was open for 30% of the time, Pallas kernels for 32%

profile of v4, /device:TPU:0, one launch (start us, length us, event | category | flops | bytes accessed | tf_op | source)
XLA Modules:
  0.0 473.4 jit_solution(14684061427821466594)
XLA Ops:
  31.2 4.2 all-to-all-start
  35.4 9.0 %fusion.12 = bf16[3072,768]{1,0:T(8,128)(2,1)} fusion(bf16[1024,768]{1,0:T(8,128)(2,1)} %param.29, s32[1024]{0:T(1024)S(1)} %bitcast.189, s32[1024]{0:T(1024)S(1)} %bitcast.182, s32[3072]{0:T(1024)S(1)} %add.530), kind=kOutput, calls=%fused_computation.18 | convolution fusion | flops 4843634688 | bytes 6311936 | tf_op jit(solution)/shard_map/dot_general | solution.py:693
  50.1 4.9 %all-to-all-start.1 = ((bf16[8,384,768]{2,1,0:T(8,128)(2,1)}), bf16[8,384,768]{2,1,0:T(8,128)(2,1)}, u32[]{:S(2)}, u32[]{:S(2)}) async-start(bf16[8,384,768]{2,1,0:T(8,128)(2,1)} %bitcast.163), calls=%async_computation.1 | async-start | bytes 9437184 | tf_op jit(solution)/shard_map/all_to_all | solution.py:786
  73.1 17.6 %attention_forward.1 = (bf16[1024,768]{1,0:T(8,128)(2,1)S(1)}, f32[1024,128]{1,0:T(8,128)S(1)}) custom-call(bf16[1024,1536]{1,0:T(8,128)(2,1)S(1)} %convolution_convert_fusion.3.q_ref.k_ref, bf16[1024,1536]{1,0:T(8,128)(2,1)S(1)} %convolution_convert_fusion.3.q_ref.k_ref, bf16[1024,768]{1,0:T(8,128)(2,1)S(1)} %copy-done.13, ...), custom_call_target="tpu_custom_call" | custom-call | flops 1024 | bytes 1024 | tf_op jit(solution)/shard_map/attention_forward/pallas_call | solution.py:130
  96.1 13.6 %all-to-all-done.1.g_ref = bf16[8,384,768]{2,1,0:T(8,128)(2,1)} async-done(((bf16[8,384,768]{2,1,0:T(8,128)(2,1)}), bf16[8,384,768]{2,1,0:T(8,128)(2,1)}, u32[]{:S(2)}, u32[]{:S(2)}) %all-to-all-start.1) | async-done | bytes 4718624 | tf_op jit(solution)/shard_map/all_to_all | solution.py:786
  109.8 5.6 %fusion.22 = bf16[1536,768]{1,0:T(8,128)(2,1)} fusion(bf16[1024,768]{1,0:T(8,128)(2,1)} %multiply_convert_fusion, s32[1024]{0:T(1024)S(1)} %bitcast.190, s32[1024]{0:T(1024)S(1)} %bitcast.183, s32[1536]{0:T(1024)S(1)} %add.535), kind=kOutput, calls=%fused_computation.36 | convolution fusion | flops 2421817344 | bytes 3946496 | tf_op jit(solution)/shard_map/dot_general | solution.py:693
  115.3 4.6 all-to-all-start.2
  119.9 21.1 %convolution_convert_fusion = bf16[3072,3072]{1,0:T(8,128)(2,1)} fusion(bf16[3072,768]{1,0:T(8,128)(2,1)} %bitcast.20, bf16[1,3072,768]{2,1,0:T(8,128)(2,1)} %param.26), kind=kOutput, calls=%fused_computation.2 | convolution fusion | flops 14504951808 | bytes 28311552 | tf_op jit(solution)/shard_map/dot_general | solution.py:70
  141.0 4.2 fusion.21
  145.2 4.2 all-to-all-done.2.x_ref
  149.4 4.6 all-to-all-start.3
  154.0 28.2 %expert_forward.2 = (bf16[8,384,768]{2,1,0:T(8,128)(2,1)}, bf16[3072,3072]{1,0:T(8,128)(2,1)}, bf16[3072,768]{1,0:T(8,128)(2,1)}, bf16[1536,3072]{1,0:T(8,128)(2...) custom-call(s32[1]{0:T(128)} %bitcast.23.me_ref, bf16[8,192,768]{2,1,0:T(8,128)(2,1)} %all-to-all-done.2.x_ref, ...), custom_call_target="tpu_custom_call" | custom-call | flops 14495514624 | bytes 37748736 | tf_op jit(solution)/shard_map/expert_forward/pallas_call | solution.py:387
  182.2 15.3 %expert_backward.2 = (bf16[3072,3072]{1,0:T(8,128)(2,1)}, bf16[8,192,768]{2,1,0:T(8,128)(2,1)}) custom-call(bf16[8,384,3072]{2,1,0:T(8,128)(2,1)} %bitcast.157, bf16[1536,3072]{1,0:T(8,128)(2,1)} %get-tuple-element.82.slope_ref, bf16[1536,128]{1,0:T(8,128)(2,1)} %get-tuple-element.83.logit_ref, bf16[768,3072]{1,0:T(8,128)(2,1)} %bitcast.160, ...), custom_call_target="tpu_custom_call" | custom-call | flops 1024 | bytes 1024 | tf_op jit(solution)/shard_map/expert_backward/pallas_call | solution.py:443
  197.5 4.4 all-to-all-start.4
  202.4 28.3 %expert_forward.3 = (bf16[8,384,768]{2,1,0:T(8,128)(2,1)}, bf16[3072,3072]{1,0:T(8,128)(2,1)}, bf16[3072,768]{1,0:T(8,128)(2,1)}, bf16[1536,3072]{1,0:T(8,128)(2...) custom-call(s32[1]{0:T(128)} %bitcast.23.me_ref, ...), custom_call_target="tpu_custom_call", output_to_operand_aliasing={{0}: (7, {}), {1}: (8, {}), {2}: (9, {})} | custom-call | flops 14495514624 | bytes 37748736 | tf_op jit(solution)/shard_map/expert_forward/pallas_call | solution.py:387
  231.4 20.9 %convolution_convert_fusion.1 = bf16[3072,768]{1,0:T(8,128)(2,1)} fusion(bf16[3072,3072]{1,0:T(8,128)(2,1)} %get-tuple-element.90, bf16[3072,768]{1,0:T(8,128)(2,1)} %get-tuple-element.93), kind=kOutput, calls=%fused_computation.19 | convolution fusion | flops 14497873920 | bytes 28311552 | tf_op jit(solution)/shard_map/rf,rd->fd/dot_general | solution.py:841
  252.3 16.3 %expert_backward.3 = (bf16[3072,3072]{1,0:T(8,128)(2,1)}, bf16[8,192,768]{2,1,0:T(8,128)(2,1)}) custom-call(bf16[8,384,3072]{2,1,0:T(8,128)(2,1)} %bitcast.158, bf16[1536,3072]{1,0:T(8,128)(2,1)} %get-tuple-element.95.slope_ref, bf16[1536,128]{1,0:T(8,128)(2,1)} %get-tuple-element.96.logit_ref, ...), custom_call_target="tpu_custom_call", output_to_operand_aliasing={{0}: (5, {})} | custom-call | flops 1024 | bytes 1024 | tf_op jit(solution)/shard_map/expert_backward/pallas_call | solution.py:443
  268.6 4.4 all-to-all-start.5
  273.0 20.9 %convolution_convert_fusion.2 = bf16[768,3072]{1,0:T(8,128)(2,1)} fusion(bf16[3072,3072]{1,0:T(8,128)(2,1)} %get-tuple-element.99, bf16[1536,768]{1,0:T(8,128)(2,1)} %bitcast.28, bf16[1536,768]{1,0:T(8,128)(2,1)} %bitcast.27), kind=kOutput, calls=%fused_computation.20 | convolution fusion | flops 14507311104 | bytes 28311552 | tf_op jit(solution)/shard_map/rd,rf->df/dot_general | solution.py:857
  293.9 8.6 %all-to-all-done.5 = bf16[8,192,768]{2,1,0:T(8,128)(2,1)} async-done(((bf16[8,192,768]{2,1,0:T(8,128)(2,1)}), bf16[8,192,768]{2,1,0:T(8,128)(2,1)}, u32[]{:S(2)}, u32[]{:S(2)}) %all-to-all-start.5) | async-done | bytes 2359328 | tf_op jit(solution)/shard_map/all_to_all | solution.py:850
  302.5 4.6 all-to-all-start.6
  307.9 5.0 %fusion.13 = f32[1024,768]{1,0:T(8,128)S(1)} fusion(bf16[1536,768]{1,0:T(8,128)(2,1)} %bitcast.29, s32[1024]{0:T(1024)S(1)} %bitcast.192, s32[1024]{0:T(1024)S(1)} %bitcast.185, s32[1536]{0:T(1024)S(1)} %add.535), kind=kOutput, calls=%fused_computation.21 | convolution fusion | flops 2420637696 | bytes 5519360 | tf_op jit(solution)/shard_map/st,sd->td/dot_general | solution.py:697
  312.9 6.4 %multiply_reduce_fusion = (bf16[768]{0:T(1024)(128)(2,1)}, f32[1024]{0:T(1024)S(1)}, f32[1024,768]{1,0:T(8,128)S(1)}) fusion(f32[1024,768]{1,0:T(8,128)S(1)} %get-tuple-element.245, f32[1024]{0:T(1024)S(1)} %fusion.80, f32[768]{0:T(1024)S(1)} %get-tuple-element.224, f32[1024,768]{1,0:T(8,128)S(1)} %fusion.13, bf16[1536,768]{1,0:T(8,128)(2,1)} %bitcast.30, ...), kind=kOutput, calls=%fused_computation.41 | convolution fusion | flops 2426140928 | bytes 11823616 | tf_op jit(solution)/shard_map/st,sd->td/dot_general | solution.py:697
  324.5 26.5 %attention_backward.1 = (bf16[3,1024,768]{2,1,0:T(8,128)(2,1)}, f32[6,2,768]{2,1,0:T(2,128)S(1)}) custom-call(bf16[1024,1536]{1,0:T(8,128)(2,1)} %copy-done, bf16[1024,1536]{1,0:T(8,128)(2,1)} %copy-done, bf16[1024,768]{1,0:T(8,128)(2,1)S(1)} %copy-done.14, bf16[1024,768]{1,0:T(8,128)(2,1)S(1)} %copy-done.11, ...), custom_call_target="tpu_custom_call" | custom-call | flops 1024 | bytes 1024 | tf_op jit(solution)/shard_map/attention_backward/pallas_call | solution.py:254
  355.4 6.4 %weight_grad.2 = bf16[768,2304]{1,0:T(8,128)(2,1)S(1)} custom-call(bf16[1024,768]{1,0:T(8,128)(2,1)S(1)} %copy-done.9, bf16[3,1024,768]{2,1,0:T(8,128)(2,1)S(1)} %copy-done.1), custom_call_target="tpu_custom_call" | custom-call | flops 1024 | bytes 1024 | tf_op jit(solution)/shard_map/weight_grad/pallas_call | solution.py:618
  375.4 6.3 %norm_back.1 = (bf16[1024,768]{1,0:T(8,128)(2,1)}, f32[1,768]{1,0:T(1,128)S(1)}) custom-call(bf16[3,1024,768]{2,1,0:T(8,128)(2,1)S(1)} %bitcast.142, bf16[768,1664]{1,0:T(8,128)(2,1)S(1)} %bitcast.152, bf16[768,1536]{1,0:T(8,128)(2,1)S(1)} %bitcast.156, bf16[1024,768]{1,0:T(8,128)(2,1)S(1)} %copy-done.4, f32[1,768]{1,0:T(1,128)S(1)} %reshape.473.gain_ref, ...), custom_call_target="tpu_custom_call" | custom-call | flops 1024 | bytes 1024 | tf_op jit(solution)/shard_map/norm_back/pallas_call | solution.py:663
  390.6 7.3 %collective-permute-done.9 = bf16[2,96,1152]{2,1,0:T(8,128)(2,1)} collective-permute-done((bf16[2,96,1152]{2,1,0:T(8,128)(2,1)}, bf16[2,96,1152]{2,1,0:T(8,128)(2,1)}, u32[]{:S(2)}, u32[]{:S(2)}) %collective-permute-start.9) | collective-permute-done | bytes 442400 | tf_op jit(solution)/shard_map/ppermute | solution.py:467
  404.6 5.6 %collective-permute-done.8 = bf16[96,1152]{1,0:T(8,128)(2,1)S(1)} collective-permute-done((bf16[96,1152]{1,0:T(8,128)(2,1)S(1)}, bf16[96,1152]{1,0:T(8,128)(2,1)S(1)}, u32[]{:S(2)}, u32[]{:S(2)}) %collective-permute-start.8) | collective-permute-done | bytes 221216 | tf_op jit(solution)/shard_map/ppermute | solution.py:467
  414.1 4.4 collective-permute-done.12
  429.5 7.9 %collective-permute-done.16 = bf16[48,3328]{1,0:T(8,128)(2,1)S(1)} collective-permute-done((bf16[48,3328]{1,0:T(8,128)(2,1)S(1)}, bf16[48,3328]{1,0:T(8,128)(2,1)S(1)}, u32[]{:S(2)}, u32[]{:S(2)}) %collective-permute-start.16) | collective-permute-done | bytes 319520 | tf_op jit(solution)/shard_map/ppermute | solution.py:467
  440.5 9.6 %add_convert_fusion = bf16[1024,768]{1,0:T(8,128)(2,1)} fusion(f32[1024,768]{1,0:T(8,128)S(1)} %copy-done.31, bf16[3072,768]{1,0:T(8,128)(2,1)} %bitcast.36, s32[1024]{0:T(1024)S(1)} %bitcast.194, s32[1024]{0:T(1024)S(1)} %bitcast.187, s32[3072]{0:T(1024)S(1)} %copy-done.47), kind=kOutput, calls=%fused_computation.42 | convolution fusion | flops 4842848256 | bytes 9457664 | tf_op jit(solution)/shard_map/st,sd->td/dot_general | solution.py:697
  457.4 5.5 %collective-permute-done.18 = bf16[48,3328]{1,0:T(8,128)(2,1)S(1)} collective-permute-done((bf16[48,3328]{1,0:T(8,128)(2,1)S(1)}, bf16[48,3328]{1,0:T(8,128)(2,1)S(1)}, u32[]{:S(2)}, u32[]{:S(2)}) %collective-permute-start.18) | collective-permute-done | bytes 319520 | tf_op jit(solution)/shard_map/ppermute | solution.py:467
  (280 shorter events, 121.5 us)
Async XLA Ops:
  8.3 15.8 %collective-permute-start.3 = (bf16[1,96,1536]{2,1,0:T(8,128)(2,1)S(1)}, bf16[1,96,1536]{2,1,0:T(8,128)(2,1)S(1)}, u32[]{:S(2)}, u32[]{:S(2)}) collective-permute-start(bf16[1,96,1536]{2,1,0:T(8,128)(2,1)S(1)} %maximum_bitcast_fusion), channel_id=1, source_target_pairs={{0,16},{4,20},{8,24},{12,28},{16,0},{20,4},{24,8},{28,12},{1,17},{... | collective-permute-start | bytes 884744 | tf_op jit(solution)/shard_map/ppermute | solution.py:467
  15.5 10.1 %collective-permute-start = (bf16[1,96,1664]{2,1,0:T(8,128)(2,1)S(1)}, bf16[1,96,1664]{2,1,0:T(8,128)(2,1)S(1)}, u32[]{:S(2)}, u32[]{:S(2)}) collective-permute-start(bf16[1,96,1664]{2,1,0:T(8,128)(2,1)S(1)} %bitcast.164), channel_id=1, source_target_pairs={{0,8},{4,12},{8,0},{12,4},{16,24},{20,28},{24,16},{28,20},{1,9},{5... | collective-permute-start | bytes 958472 | tf_op jit(solution)/shard_map/ppermute | solution.py:467
  17.1 38.2 %copy-start.42 = (s32[768]{0:T(1024)}, s32[768]{0:T(1024)S(1)}, u32[]{:S(2)}) copy-start(s32[768]{0:T(1024)S(1)} %compare_select_fusion.1) | copy-start | bytes 9220
  17.1 46.5 %copy-start.48 = (pred[768]{0:T(1024)(128)(4,1)}, pred[768]{0:T(1024)(128)(4,1)S(1)}, u32[]{:S(2)}) copy-start(pred[768]{0:T(1024)(128)(4,1)S(1)} %fusion.64) | copy-start | bytes 2308
  23.7 289.2 %copy-start.50 = (s32[1024,1]{0,1:T(1,128)}, s32[1024,1]{0,1:T(1,128)S(1)}, u32[]{:S(2)}) copy-start(s32[1024,1]{0,1:T(1,128)S(1)} %get-tuple-element.241) | copy-start | bytes 12292
  25.1 21.4 %collective-permute-start.4 = (bf16[2,96,1536]{2,1,0:T(8,128)(2,1)}, bf16[2,96,1536]{2,1,0:T(8,128)(2,1)}, u32[]{:S(2)}, u32[]{:S(2)}) collective-permute-start(bf16[2,96,1536]{2,1,0:T(8,128)(2,1)} %pad_maximum_fusion.3), channel_id=1, source_target_pairs={{0,8},{4,12},{8,0},{12,4},{16,24},{20,28},{24,16},{28,20},{1,9},{5... | collective-permute-start | bytes 1769480 | tf_op jit(solution)/shard_map/ppermute | solution.py:467
  26.5 18.0 %collective-permute-start.1 = (bf16[2,96,1664]{2,1,0:T(8,128)(2,1)}, bf16[2,96,1664]{2,1,0:T(8,128)(2,1)}, u32[]{:S(2)}, u32[]{:S(2)}) collective-permute-start(bf16[2,96,1664]{2,1,0:T(8,128)(2,1)} %pad_maximum_fusion.2), channel_id=1, source_target_pairs={{0,16},{4,20},{8,24},{12,28},{16,0},{20,4},{24,8},{28,12},{1,17},{... | collective-permute-start | bytes 1916936 | tf_op jit(solution)/shard_map/ppermute | solution.py:467
  31.2 13.2 %all-to-all-start = ((bf16[8,2,192]{2,1,0:T(2,128)(2,1)}), bf16[8,2,192]{2,1,0:T(2,128)(2,1)S(1)}, u32[]{:S(2)}, u32[]{:S(2)}) async-start(bf16[8,2,192]{2,1,0:T(2,128)(2,1)} %reshape.509), calls=%async_computation | async-start | bytes 16384 | tf_op jit(solution)/shard_map/all_to_all | solution.py:780
  45.9 10.5 %collective-permute-start.2 = (bf16[4,96,1664]{2,1,0:T(8,128)(2,1)S(1)}, bf16[4,96,1664]{2,1,0:T(8,128)(2,1)}, u32[]{:S(2)}, u32[]{:S(2)}) collective-permute-start(bf16[4,96,1664]{2,1,0:T(8,128)(2,1)S(1)} %pad_maximum_fusion.refs_0_), channel_id=1, source_target_pairs={{0,4},{4,0},{8,12},{12,8},{16,20},{20,16},{24,28},{28,24},{1,5},{5... | collective-permute-start | bytes 3833864 | tf_op jit(solution)/shard_map/ppermute | solution.py:467
  48.7 7.7 %collective-permute-start.5 = (bf16[4,96,1536]{2,1,0:T(8,128)(2,1)}, bf16[4,96,1536]{2,1,0:T(8,128)(2,1)}, u32[]{:S(2)}, u32[]{:S(2)}) collective-permute-start(bf16[4,96,1536]{2,1,0:T(8,128)(2,1)} %pad_maximum_fusion.1.refs_2_), channel_id=1, source_target_pairs={{0,4},{4,0},{8,12},{12,8},{16,20},{20,16},{24,28},{28,24},{1,5},{5... | collective-permute-start | bytes 3538952 | tf_op jit(solution)/shard_map/ppermute | solution.py:467
  50.1 59.7 %all-to-all-start.1 = ((bf16[8,384,768]{2,1,0:T(8,128)(2,1)}), bf16[8,384,768]{2,1,0:T(8,128)(2,1)}, u32[]{:S(2)}, u32[]{:S(2)}) async-start(bf16[8,384,768]{2,1,0:T(8,128)(2,1)} %bitcast.163), calls=%async_computation.1 | async-start | bytes 9437184 | tf_op jit(solution)/shard_map/all_to_all | solution.py:786
  94.3 225.0 %copy-start.30 = (f32[1024,768]{1,0:T(8,128)}, f32[1024,768]{1,0:T(8,128)S(1)}, u32[]{:S(2)}) copy-start(f32[1024,768]{1,0:T(8,128)S(1)} %get-tuple-element.245) | copy-start | bytes 9437188
  115.3 34.1 %all-to-all-start.2 = ((bf16[8,192,768]{2,1,0:T(8,128)(2,1)}), bf16[8,192,768]{2,1,0:T(8,128)(2,1)}, u32[]{:S(2)}, u32[]{:S(2)}) async-start(bf16[8,192,768]{2,1,0:T(8,128)(2,1)} %bitcast.168), calls=%async_computation.2 | async-start | bytes 4718592 | tf_op jit(solution)/shard_map/all_to_all | solution.py:813
  149.4 48.1 %all-to-all-start.3 = ((bf16[8,192,768]{2,1,0:T(8,128)(2,1)}), bf16[8,192,768]{2,1,0:T(8,128)(2,1)}, u32[]{:S(2)}, u32[]{:S(2)}) async-start(bf16[8,192,768]{2,1,0:T(8,128)(2,1)} %bitcast.167), calls=%async_computation.3 | async-start | bytes 4718592 | tf_op jit(solution)/shard_map/all_to_all | solution.py:813
  197.5 33.9 %all-to-all-start.4 = ((bf16[8,192,768]{2,1,0:T(8,128)(2,1)}), bf16[8,192,768]{2,1,0:T(8,128)(2,1)}, u32[]{:S(2)}, u32[]{:S(2)}) async-start(bf16[8,192,768]{2,1,0:T(8,128)(2,1)} %get-tuple-element.91), calls=%async_computation.4 | async-start | bytes 4718592 | tf_op jit(solution)/shard_map/all_to_all | solution.py:850
  201.9 149.8 %reduce-scatter.3.cloned.1.call-start = ((), (), s32[]{:S(2)}) async-start(), calls=%async_computation.9 | async-start | bytes 5898240 | tf_op jit(solution)/shard_map/reduce_scatter | solution.py:844
  268.6 33.8 %all-to-all-start.5 = ((bf16[8,192,768]{2,1,0:T(8,128)(2,1)}), bf16[8,192,768]{2,1,0:T(8,128)(2,1)}, u32[]{:S(2)}, u32[]{:S(2)}) async-start(bf16[8,192,768]{2,1,0:T(8,128)(2,1)} %get-tuple-element.97), calls=%async_computation.5 | async-start | bytes 4718592 | tf_op jit(solution)/shard_map/all_to_all | solution.py:850
  302.5 59.4 %all-to-all-start.6 = ((bf16[8,384,768]{2,1,0:T(8,128)(2,1)}), bf16[8,384,768]{2,1,0:T(8,128)(2,1)}, u32[]{:S(2)}, u32[]{:S(2)}) async-start(bf16[8,384,768]{2,1,0:T(8,128)(2,1)} %get-tuple-element.101), calls=%async_computation.6 | async-start | bytes 9437184 | tf_op jit(solution)/shard_map/all_to_all | solution.py:863
  307.1 119.7 %reduce-scatter.5.cloned.1.call-start = ((), (), s32[]{:S(2)}) async-start(), calls=%async_computation.10 | async-start | bytes 5898240 | tf_op jit(solution)/shard_map/reduce_scatter | solution.py:860
  363.2 4.9 %collective-permute-start.6 = (bf16[2,2,96,2304]{3,2,1,0:T(8,128)(2,1)}, bf16[2,2,96,2304]{3,2,1,0:T(8,128)(2,1)}, u32[]{:S(2)}, u32[]{:S(2)}) collective-permute-start(bf16[2,2,96,2304]{3,2,1,0:T(8,128)(2,1)} %dynamic-slice_bitcast_fusion), channel_id=1, source_target_pairs={{0,4},{4,0},{8,12},{12,8},{16,20},{20,16},{24,28},{28,24},{1,5},{5... | collective-permute-start | bytes 5308424 | tf_op jit(solution)/shard_map/ppermute | solution.py:467
  372.0 17.3 %collective-permute-start.7 = (bf16[2,96,1152]{2,1,0:T(8,128)(2,1)}, bf16[2,96,1152]{2,1,0:T(8,128)(2,1)}, u32[]{:S(2)}, u32[]{:S(2)}) collective-permute-start(bf16[2,96,1152]{2,1,0:T(8,128)(2,1)} %dynamic-slice_bitcast_fusion.3), channel_id=1, source_target_pairs={{0,8},{4,12},{8,0},{12,4},{16,24},{20,28},{24,16},{28,20},{1,9},{5... | collective-permute-start | bytes 1327112 | tf_op jit(solution)/shard_map/ppermute | solution.py:467
  385.4 12.5 %collective-permute-start.9 = (bf16[2,96,1152]{2,1,0:T(8,128)(2,1)}, bf16[2,96,1152]{2,1,0:T(8,128)(2,1)}, u32[]{:S(2)}, u32[]{:S(2)}) collective-permute-start(bf16[2,96,1152]{2,1,0:T(8,128)(2,1)} %dynamic-slice_bitcast_fusion.2), channel_id=1, source_target_pairs={{0,16},{4,20},{8,24},{12,28},{16,0},{20,4},{24,8},{28,12},{1,17},{... | collective-permute-start | bytes 1327112 | tf_op jit(solution)/shard_map/ppermute | solution.py:467
  402.3 9.4 %collective-permute-start.11 = (bf16[2,2,96,1024]{3,2,1,0:T(8,128)(2,1)S(1)}, bf16[2,2,96,1024]{3,2,1,0:T(8,128)(2,1)S(1)}, u32[]{:S(2)}, u32[]{:S(2)}) collective-permute-start(bf16[2,2,96,1024]{3,2,1,0:T(8,128)(2,1)S(1)} %dynamic-slice_bitcast_fusion.1), channel_id=1, source_target_pairs={{0,4},{4,0},{8,12},{12,8},{16,20},{20,16},{24,28},{28,24},{1,5},{5... | collective-permute-start | bytes 2359304 | tf_op jit(solution)/shard_map/ppermute | solution.py:467
  402.4 7.9 %collective-permute-start.8 = (bf16[96,1152]{1,0:T(8,128)(2,1)S(1)}, bf16[96,1152]{1,0:T(8,128)(2,1)S(1)}, u32[]{:S(2)}, u32[]{:S(2)}) collective-permute-start(bf16[96,1152]{1,0:T(8,128)(2,1)S(1)} %dynamic-slice_bitcast_fusion.5), channel_id=1, source_target_pairs={{0,16},{4,20},{8,24},{12,28},{16,0},{20,4},{24,8},{28,12},{1,17},{... | collective-permute-start | bytes 663560 | tf_op jit(solution)/shard_map/ppermute | solution.py:467
  404.0 7.6 %collective-permute-start.10 = (bf16[96,1152]{1,0:T(8,128)(2,1)S(1)}, bf16[96,1152]{1,0:T(8,128)(2,1)S(1)}, u32[]{:S(2)}, u32[]{:S(2)}) collective-permute-start(bf16[96,1152]{1,0:T(8,128)(2,1)S(1)} %dynamic-slice_bitcast_fusion.4), channel_id=1, source_target_pairs={{0,8},{4,12},{8,0},{12,4},{16,24},{20,28},{24,16},{28,20},{1,9},{5... | collective-permute-start | bytes 663560 | tf_op jit(solution)/shard_map/ppermute | solution.py:467
  412.1 6.4 %collective-permute-start.12 = (bf16[2,96,512]{2,1,0:T(8,128)(2,1)S(1)}, bf16[2,96,512]{2,1,0:T(8,128)(2,1)S(1)}, u32[]{:S(2)}, u32[]{:S(2)}) collective-permute-start(bf16[2,96,512]{2,1,0:T(8,128)(2,1)S(1)} %dynamic-slice_bitcast_fusion.7), channel_id=1, source_target_pairs={{0,8},{4,12},{8,0},{12,4},{16,24},{20,28},{24,16},{28,20},{1,9},{5... | collective-permute-start | bytes 589832 | tf_op jit(solution)/shard_map/ppermute | solution.py:467
  413.6 6.1 %collective-permute-start.14 = (bf16[2,96,512]{2,1,0:T(8,128)(2,1)S(1)}, bf16[2,96,512]{2,1,0:T(8,128)(2,1)S(1)}, u32[]{:S(2)}, u32[]{:S(2)}) collective-permute-start(bf16[2,96,512]{2,1,0:T(8,128)(2,1)S(1)} %dynamic-slice_bitcast_fusion.6), channel_id=1, source_target_pairs={{0,16},{4,20},{8,24},{12,28},{16,0},{20,4},{24,8},{28,12},{1,17},{... | collective-permute-start | bytes 589832 | tf_op jit(solution)/shard_map/ppermute | solution.py:467
  418.6 4.7 collective-permute-start.13
  419.7 4.7 collective-permute-start.15
  428.0 9.4 %collective-permute-start.16 = (bf16[48,3328]{1,0:T(8,128)(2,1)S(1)}, bf16[48,3328]{1,0:T(8,128)(2,1)S(1)}, u32[]{:S(2)}, u32[]{:S(2)}) collective-permute-start(bf16[48,3328]{1,0:T(8,128)(2,1)S(1)} %broadcast_select_fusion.2), channel_id=1, source_target_pairs={{0,1},{1,0},{2,3},{3,2},{4,5},{5,4},{6,7},{7,6},{8,9},{9,8},{10,11... | collective-permute-start | bytes 958472 | tf_op jit(solution)/shard_map/ppermute | solution.py:467
  437.5 16.6 %collective-permute-start.17 = (bf16[48,3328]{1,0:T(8,128)(2,1)S(1)}, bf16[48,3328]{1,0:T(8,128)(2,1)S(1)}, u32[]{:S(2)}, u32[]{:S(2)}) collective-permute-start(bf16[48,3328]{1,0:T(8,128)(2,1)S(1)} %add_convert_fusion.2), channel_id=1, source_target_pairs={{0,2},{1,3},{2,0},{3,1},{4,6},{5,7},{6,4},{7,5},{8,10},{9,11},{10,... | collective-permute-start | bytes 958472 | tf_op jit(solution)/shard_map/ppermute | solution.py:467
  454.1 8.8 %collective-permute-start.18 = (bf16[48,3328]{1,0:T(8,128)(2,1)S(1)}, bf16[48,3328]{1,0:T(8,128)(2,1)S(1)}, u32[]{:S(2)}, u32[]{:S(2)}) collective-permute-start(bf16[48,3328]{1,0:T(8,128)(2,1)S(1)} %add_convert_fusion.1), channel_id=1, source_target_pairs={{0,1},{1,0},{2,3},{3,2},{4,5},{5,4},{6,7},{7,6},{8,9},{9,8},{10,11... | collective-permute-start | bytes 958472 | tf_op jit(solution)/shard_map/ppermute | solution.py:467
  (50 other events, 389.8 us)
Sparse Core Ops, SparseCore 0:
  252.4 86.2 reduce-scatter.2
  341.0 85.7 reduce-scatter.4
